TPU v7x, 256 devices: a whole 4x4x8 slice. The times are simulated.
256 devices in a mesh: blk: 128 (over x, z_lo, y, core), row: 2 (over z_hi).
Axes of the slice: x: 4, y: 4, z: 8 (z_hi: 2, z_lo: 4; z = z_hi * 4 + z_lo), core: 2. Of those that a mesh axis runs over, the one named last changes fastest.
Arguments:
- row_feats: bfloat16 [3072, 2048], P('row'), may hold values from -9 to 9
- col_feats: bfloat16 [65536, 2048], P('blk'), may hold values from -9 to 9
- offsets: int32 [3, 4], replicated, may hold values from 0 to 255
Outputs:
- energy: float32 [2, 3072, 32768], P(None, 'row', 'blk')
- norms: float32 [3, 2, 32768], P(None, None, 'blk')
All inputs are finite; a program needn't handle non-finite values.
Results may differ from a plain program's by a relative error of at most 0.0003.
Values sent between devices are 32-bit elements; how exact they have to be, the bound alone decides.
No kernel may reach another device: no remote copies, remote signals or barrier semaphores. Data moves between devices by JAX's collectives and lax.ppermute only.
A program may use at most 64 MiB of HBM per device.

v0:
```python
import functools
import math

import jax
import jax.numpy as jnp
from jax import lax
from jax.experimental import pallas as pl
from jax.experimental.pallas import tpu as pltpu
from jax.sharding import PartitionSpec as P

F32 = jnp.float32
BF16 = jnp.bfloat16
W = 256
LAGS = 96
VMEM_LIMIT = 48 * 1024 * 1024


def group_rows(m):
    return (16 * m, 16) if m < 4 else (64 + 8 * (m - 4), 8)


def lag_targets(o):
    t, s = [0], [0]
    first, second = [0], [1]
    rows = {}
    for step in range(4):
        count = 1 << step
        for m in range(count):
            start, _ = group_rows(m)
            place = {3: 0, 2: 8, 1: 12, 0: 14}[step]
            for n in range(count):
                lag = (o[step] + s[n] - t[m]) & (W - 1)
                rows[start + place + n] = lag + W * second[n]
        if step < 3:
            t, s = t + [x + o[step] for x in s], s + [x - o[step] for x in t]
            first, second = first + second, second + first
    rows[15] = 0
    rows[16 + 14] = W
    return rows, t, first


def split(x):
    hi = x.astype(BF16)
    return hi, (x - hi.astype(F32)).astype(BF16)


TN = (((0,), (0,)), ((), ()))
NT = (((1,), (1,)), ((), ()))


def skew(x):
    row = lax.broadcasted_iota(jnp.int32, (W, W), 0)
    for bit in (1, 2, 4):
        x = jnp.where((row & bit) != 0, pltpu.roll(x, W - bit, 1), x)
    tiles = [pltpu.roll(x[8 * t : 8 * t + 8], (W - 8 * t) % W, 1) for t in range(W // 8)]
    return jnp.concatenate(tiles, axis=0)


def build_onehot(o, table_ref):
    rows, bases, first = lag_targets(o)
    table_ref[...] = jnp.full((LAGS, 128), -1, jnp.int32)
    for r, target in rows.items():
        table_ref[r : r + 1, :] = jnp.full((1, 128), target, jnp.int32)
    return bases, first


def lag_products(gram_ref, o, table_ref, out_ref):
    bases, first = build_onehot(o, table_ref)
    table = table_ref[...]
    table = jnp.concatenate([table] * 4, axis=1)
    onehot = (table == lax.broadcasted_iota(jnp.int32, (LAGS, 2 * W), 1)).astype(F32).astype(BF16)
    diags = {}
    for kind in (0, 1):
        sheets = []
        for side in (0, 1):
            block = gram_ref[kind * W : (kind + 1) * W, side * W : (side + 1) * W]
            sheets.append(skew(block))
        sheet = jnp.concatenate(sheets, axis=1)
        hi, lo = split(sheet)
        lowest = (sheet - hi.astype(F32) - lo.astype(F32)).astype(BF16)
        total = None
        for part in (lowest, lo, hi):
            term = lax.dot_general(onehot, part, NT, preferred_element_type=F32)
            total = term if total is None else total + term
        diags[kind] = total
    for m in range(8):
        start, count = group_rows(m)
        tile = diags[first[m]][start : start + count]
        base = bases[m]
        if m > 0:
            tile = pltpu.roll(tile, (-base) & (W - 1), 1)
        out_ref[start : start + count, :] = tile


def gram_step(a, b, gram_ref):
    both = jnp.concatenate([a, b], axis=1)
    hi, lo = split(both)
    g = lax.dot_general(hi, lo, TN, preferred_element_type=F32)
    g += lax.dot_general(lo, hi, TN, preferred_element_type=F32)
    g += lax.dot_general(hi, hi, TN, preferred_element_type=F32)
    gram_ref[...] += g


def angle(g, upper_sq, lower_sq):
    twice = 2.0 * g
    diff = upper_sq - lower_sq
    scale = jnp.maximum(jnp.abs(twice), jnp.abs(diff))
    live = scale > 0.0
    safe = jnp.where(live, scale, 1.0)
    x = jnp.where(live, diff / safe, 1.0)
    y = jnp.where(live, twice / safe, 0.0)
    r = jnp.sqrt(x * x + y * y)
    big = jnp.sqrt(0.5 * (1.0 + jnp.abs(x) / r))
    small = 0.5 * jnp.abs(y) / (r * big)
    wide = x < 0.0
    c = jnp.where(wide, small, big)
    s = jnp.where(wide, big, small)
    s = jnp.where(y < 0.0, -s, s)
    cross = twice * c * s
    return c, s, c * c * upper_sq + cross + s * s * lower_sq, s * s * upper_sq - cross + c * c * lower_sq


def angles(lags, o, coef_ref):
    row = lax.broadcasted_iota(jnp.int32, (8, W), 0)
    a = jnp.ones((8, W), F32)
    b = jnp.ones((8, W), F32)
    upper_sq = lags[15:16]
    lower_sq = lags[30:31]
    tiles = [lags[16 * m + 8 : 16 * m + 16] for m in range(4)]
    last = [lags[group_rows(m)[0] : group_rows(m)[0] + 8] for m in range(8)]
    for step in range(4):
        count = 1 << step
        if step == 3:
            parts, place = last, 0
        else:
            parts, place = tiles[:count], (6, 4, 0)[step]
        acc = None
        for m in range(count):
            term = a[m : m + 1] * parts[m]
            acc = term if acc is None else acc + term
        view = pltpu.roll(b, place, 0) if place else b
        acc = jnp.where((row >= place) & (row < place + count), acc * view, 0.0)
        g = jnp.sum(acc, axis=0, keepdims=True)
        c, s, upper_sq, lower_sq = angle(g, upper_sq, lower_sq)
        coef_ref[step : step + 1, :] = c
        coef_ref[4 + step : 5 + step, :] = s
        if step < 3:
            shift_a, shift_b = pltpu.roll(a, count, 0), pltpu.roll(b, count, 0)
            a, b = jnp.where(row < count, c * a, s * shift_b), jnp.where(row < count, c * b, -s * shift_a)
            turn = (o[step] - o[step + 1]) & (W - 1)
            b = pltpu.roll(b, turn, 1)
            lower_sq = pltpu.roll(jnp.broadcast_to(lower_sq, (8, W)), turn, 1)[0:1]
    coef_ref[8:9, :] = upper_sq
    coef_ref[9:10, :] = pltpu.roll(jnp.broadcast_to(lower_sq, (8, W)), o[3] & (W - 1), 1)[0:1]


def rotate(upper, lower, coef, o):
    lower = pltpu.roll(lower, (-o[0]) & (W - 1), 1)
    for step in range(4):
        c, s = coef[step : step + 1], coef[4 + step : 5 + step]
        upper, lower = c * upper + s * lower, c * lower - s * upper
        turn = (o[step] - o[step + 1]) if step < 3 else o[3]
        lower = pltpu.roll(lower, turn & (W - 1), 1)
    return upper, lower


def spec_rows(r):
    return pl.BlockSpec((r, W), lambda i: (i, 0))


def spec_whole(shape):
    return pl.BlockSpec(shape, lambda i: (0,) * len(shape))


SMEM = pl.BlockSpec(memory_space=pltpu.SMEM)


def tile_rows(rows, most=512):
    r = most
    while rows % r:
        r //= 2
    return r


def block(rows):
    return jax.ShapeDtypeStruct((rows, W), F32)


LAG_SHAPE = jax.ShapeDtypeStruct((LAGS, W), F32)
COEF_SHAPE = jax.ShapeDtypeStruct((16, W), F32)
GRAM_SCRATCH = [pltpu.VMEM((2 * W, 2 * W), F32), pltpu.VMEM((LAGS, 128), jnp.int32)]


def call(kernel, name, grid, in_specs, out_specs, out_shape, scratch=(), flops=0, moved=0):
    return pl.pallas_call(
        kernel,
        name=name,
        grid=(grid,),
        in_specs=in_specs,
        out_specs=out_specs,
        out_shape=out_shape,
        scratch_shapes=list(scratch),
        compiler_params=pltpu.CompilerParams(vmem_limit_bytes=VMEM_LIMIT),
        cost_estimate=pl.CostEstimate(flops=flops, bytes_accessed=moved, transcendentals=0),
    )


def offsets_of(o_ref, round_index):
    return [o_ref[round_index, j] for j in range(4)]


def pick(flag, a, b):
    return jnp.where(flag, a, b), jnp.where(flag, b, a)


def first_kernel(o_ref, rows_ref, cols_ref, upper_ref, lower_ref, lag_ref, gram_ref, table_ref, norm_ref):
    i = pl.program_id(0)
    count, feat = cols_ref.shape

    @pl.when(i == 0)
    def _():
        gram_ref[...] = jnp.zeros_like(gram_ref)
        ones = jnp.ones((8, feat), BF16)
        for k in range(0, count, 128):
            wide = cols_ref[k : k + 128].astype(F32)
            hi, lo = split(wide * wide)
            norm_ref[:, k : k + 128] = lax.dot_general(
                ones, lo, NT, preferred_element_type=F32
            ) + lax.dot_general(ones, hi, NT, preferred_element_type=F32)

    rows = rows_ref[...]
    wide = rows.astype(F32)
    row_norm = jnp.sum(wide * wide, axis=1, keepdims=True)
    cross = lax.dot_general(rows, cols_ref[...], NT, preferred_element_type=F32)
    kernel = jnp.exp(
        -(0.25 / math.sqrt(feat)) * (row_norm + norm_ref[0:1] - 2.0 * cross - 2.0 * feat)
    )
    upper, lower = kernel[:, :W], kernel[:, W:]
    upper_ref[...] = upper
    lower_ref[...] = lower
    gram_step(upper, lower, gram_ref)

    @pl.when(i == pl.num_programs(0) - 1)
    def _():
        lag_products(gram_ref, offsets_of(o_ref, 0), table_ref, lag_ref)


def first(offsets, row_feats, col_feats):
    rows, feat = row_feats.shape
    r = tile_rows(rows)
    return call(
        first_kernel,
        "first",
        rows // r,
        [SMEM, pl.BlockSpec((r, feat), lambda i: (i, 0)), spec_whole(col_feats.shape)],
        (spec_rows(r), spec_rows(r), spec_whole((LAGS, W))),
        (block(rows), block(rows), LAG_SHAPE),
        GRAM_SCRATCH + [pltpu.VMEM((8, 2 * W), F32)],
    )(offsets, row_feats, col_feats)


def turn_kernel(round_index, o_ref, p_ref, mine_ref, other_ref, a_ref, b_ref, first_ref, second_ref, coef_ref):
    p = p_ref[0]
    core = p & 1
    o = offsets_of(o_ref, round_index)

    @pl.when(pl.program_id(0) == 0)
    def _():
        angles(mine_ref[...] + other_ref[...], o, coef_ref)

    a, b = a_ref[...], b_ref[...]
    if round_index == 0:
        upper, lower = a, b
        keep = (core == 1) | (p == 0)
    else:
        upper, lower = pick(core == 0, a, b)
        keep = (core == 0) & (p != 0)
    upper, lower = rotate(upper, lower, coef_ref[...], o)
    first_ref[...], second_ref[...] = pick(keep, upper, lower)


def turn(round_index, offsets, p, mine, other, a, b):
    rows = a.shape[0]
    r = tile_rows(rows)
    lag = spec_whole((LAGS, W))
    return call(
        functools.partial(turn_kernel, round_index),
        "turn%d" % round_index,
        rows // r,
        [SMEM, SMEM, lag, lag, spec_rows(r), spec_rows(r)],
        (spec_rows(r), spec_rows(r), spec_whole((16, W))),
        (block(rows), block(rows), COEF_SHAPE),
    )(offsets, p, mine, other, a, b)


def pairs_kernel(o_ref, p_ref, a_ref, b_ref, lag_ref, gram_ref, table_ref):
    i = pl.program_id(0)

    @pl.when(i == 0)
    def _():
        gram_ref[...] = jnp.zeros_like(gram_ref)

    upper, lower = pick((p_ref[0] & 1) == 0, a_ref[...], b_ref[...])
    gram_step(upper, lower, gram_ref)

    @pl.when(i == pl.num_programs(0) - 1)
    def _():
        lag_products(gram_ref, offsets_of(o_ref, 1), table_ref, lag_ref)


def pairs(offsets, p, a, b):
    rows = a.shape[0]
    r = tile_rows(rows)
    return call(
        pairs_kernel,
        "pairs",
        rows // r,
        [SMEM, SMEM, spec_rows(r), spec_rows(r)],
        spec_whole((LAGS, W)),
        LAG_SHAPE,
        GRAM_SCRATCH,
    )(offsets, p, a, b)


def side_kernel(last, o_ref, p_ref, coef_ref, sx_ref, ry_ref, z_ref, q_ref, lag_ref, gram_ref, table_ref):
    i = pl.program_id(0)
    p = p_ref[0]
    core = p & 1

    @pl.when(i == 0)
    def _():
        gram_ref[...] = jnp.zeros_like(gram_ref)

    near_end = (p == 1) | (p == last - 1)
    upper, lower = pick((core == 0) != near_end, sx_ref[...], ry_ref[...])
    upper, lower = rotate(upper, lower, coef_ref[...], offsets_of(o_ref, 1))
    q = jnp.where((core == 1) | (p == last - 1), upper, lower)
    q_ref[...] = q
    upper, lower = pick(core == 0, z_ref[...], q)
    gram_step(upper, lower, gram_ref)

    @pl.when(i == pl.num_programs(0) - 1)
    def _():
        lag_products(gram_ref, offsets_of(o_ref, 2), table_ref, lag_ref)


def side(last, offsets, p, coef, sx, ry, z):
    rows = sx.shape[0]
    r = tile_rows(rows)
    return call(
        functools.partial(side_kernel, last),
        "side",
        rows // r,
        [SMEM, SMEM, spec_whole((16, W))] + [spec_rows(r)] * 3,
        (spec_rows(r), spec_whole((LAGS, W))),
        (block(rows), LAG_SHAPE),
        GRAM_SCRATCH,
    )(offsets, p, coef, sx, ry, z)


def solve_kernel(o_ref, mine_ref, other_ref, coef_ref):
    angles(mine_ref[...] + other_ref[...], offsets_of(o_ref, 2), coef_ref)


def solve(offsets, mine, other):
    lag = spec_whole((LAGS, W))
    return call(solve_kernel, "solve", 1, [SMEM, lag, lag], spec_whole((16, W)), COEF_SHAPE)(offsets, mine, other)


def last_kernel(last, o_ref, p_ref, own_ref, got_ref, z_ref, q_ref, r_ref, v_ref, out_ref):
    p = p_ref[0]
    core = p & 1
    o = offsets_of(o_ref, 2)
    upper, lower = pick(core == 0, z_ref[...], q_ref[...])
    upper, lower = rotate(upper, lower, own_ref[...], o)
    own = jnp.where((core == 1) & (p != 1), upper, lower)
    upper, lower = pick((core == 0) != ((p == 0) | (p == last)), r_ref[...], v_ref[...])
    upper, lower = rotate(upper, lower, got_ref[...], o)
    got = jnp.where((core == 0) | (p == last), upper, lower)
    own, got = own * own, got * got
    out_ref[0], out_ref[1] = pick(core == 0, got, own)


def finish(last, offsets, p, own, got, z, q, r_block, v):
    rows = z.shape[0]
    r = tile_rows(rows)
    coef = spec_whole((16, W))
    return call(
        functools.partial(last_kernel, last),
        "finish",
        rows // r,
        [SMEM, SMEM, coef, coef] + [spec_rows(r)] * 4,
        pl.BlockSpec((2, r, W), lambda i: (0, i, 0)),
        jax.ShapeDtypeStruct((2, rows, W), F32),
    )(offsets, p, own, got, z, q, r_block, v)


def body(row_feats, col_feats, offsets):
    n = lax.axis_size("blk")
    chips = n // 2
    p = lax.axis_index("blk").astype(jnp.int32).reshape(1)
    row_total = row_feats.shape[0] * lax.axis_size("row")
    across = [(0, 1), (1, 0)]
    sibling = [(i, i ^ 1) for i in range(n)]
    meet = [(2 * j + 1, 2 * j + 2) for j in range(chips - 1)] + [(2 * j, 2 * j - 1) for j in range(1, chips)]
    meet += [(0, 0), (n - 1, n - 1)]
    lend = [(2 * j, 2 * j + 3) for j in range(chips - 1)] + [(2 * j + 1, 2 * j - 2) for j in range(1, chips)]
    lend += [(1, 1), (n - 2, n - 2)]
    deal = [(2 * j, 2 * j + 2) for j in range(chips - 1)] + [(2 * j + 1, 2 * j - 1) for j in range(1, chips)]
    deal += [(1, 0), (n - 2, n - 1)]
    tell = [(2 * j, 2 * j - 2) for j in range(1, chips)] + [(2 * j + 1, 2 * j + 3) for j in range(chips - 1)]
    tell += [(0, 1), (n - 1, n - 2)]

    upper, lower, lag = first(offsets, row_feats, col_feats)
    lag_other = lax.ppermute(lag, "row", across)
    x, y, coef_a = turn(0, offsets, p, lag, lag_other, upper, lower)
    rx = lax.ppermute(x, "blk", meet)
    sy = lax.ppermute(y, "blk", sibling)
    rx, sy, x, y = lax.optimization_barrier((rx, sy, x, y))
    ry = lax.ppermute(y, "blk", lend)
    sx = lax.ppermute(x, "blk", sibling)
    lag = pairs(offsets, p, rx, sy)
    lag_other = lax.ppermute(lag, "row", across)
    z, v, coef_b = turn(1, offsets, p, lag, lag_other, rx, sy)
    r_block = lax.ppermute(z, "blk", deal)
    coef_side = lax.ppermute(coef_b, "blk", tell)
    q, lag = side(n - 1, offsets, p, coef_side, sx, ry, z)
    lag_other = lax.ppermute(lag, "row", across)
    coef_c = solve(offsets, lag, lag_other)
    coef_got = lax.ppermute(coef_c, "blk", deal)
    coef_norm = lax.ppermute(coef_c, "blk", sibling)
    energy = finish(n - 1, offsets, p, coef_c, coef_got, z, q, r_block, v)
    norms = jnp.stack([coef_a[8:10], coef_b[8:10], coef_norm[8:10]]) / row_total
    return (energy, norms)


def solution(mesh):
    return jax.shard_map(
        body,
        mesh=mesh,
        in_specs=(P("row", None), P("blk", None), P()),
        out_specs=(P(None, "row", "blk"), P(None, None, "blk")),
        check_vma=False,
    )
```

profile of v0, /device:TPU:4, one launch (start us, length us, event | category | flops | bytes accessed | tf_op | source)
XLA Modules:
  0.0 142.2 jit_solution(16918101066129329763)
XLA Ops:
  0.6 1.6 %copy-done.3 = bf16[512,2048]{1,0:T(8,128)(2,1)S(1)} copy-done((bf16[512,2048]{1,0:T(8,128)(2,1)S(1)}, bf16[512,2048]{1,0:T(8,128)(2,1)}, u32[]{:S(2)}) %copy-start.3) | copy-done | bytes 2097176
  2.9 12.2 %first.1 = (f32[1536,256]{1,0:T(8,128)S(1)}, f32[1536,256]{1,0:T(8,128)S(1)}, f32[96,256]{1,0:T(8,128)S(1)}) custom-call(s32[3,4]{1,0:T(4,128)S(1)} %copy-done.6, bf16[1536,2048]{1,0:T(8,128)(2,1)} %rows_ref.1, bf16[512,2048]{1,0:T(8,128)(2,1)S(1)} %copy-done.3), custom_call_target="tpu_custom_call" | custom-call | tf_op jit(solution)/shard_map/first/pallas_call | solution.py:251
  15.1 1.1 copy-done.4
  16.2 7.2 %collective-permute-start = (f32[96,256]{1,0:T(8,128)S(1)}, f32[96,256]{1,0:T(8,128)S(1)}, u32[]{:S(2)}, u32[]{:S(2)}) collective-permute-start(f32[96,256]{1,0:T(8,128)S(1)} %get-tuple-element.17.mine_ref), channel_id=1, source_target_pairs={{0,1},{1,0},{2,3},{3,2},{4,5},{5,4},{6,7},{7,6},{8,9},{9,8},{10,11... | collective-permute-start | bytes 294920 | tf_op jit(solution)/shard_map/ppermute | solution.py:415
  23.4 2.9 %collective-permute-done.other_ref = f32[96,256]{1,0:T(8,128)S(1)} collective-permute-done((f32[96,256]{1,0:T(8,128)S(1)}, f32[96,256]{1,0:T(8,128)S(1)}, u32[]{:S(2)}, u32[]{:S(2)}) %collective-permute-start) | collective-permute-done | bytes 98336 | tf_op jit(solution)/shard_map/ppermute | solution.py:415
  26.3 4.8 %turn0.1 = (f32[1536,256]{1,0:T(8,128)S(1)}, f32[1536,256]{1,0:T(8,128)S(1)}, f32[16,256]{1,0:T(8,128)S(1)}) custom-call(s32[3,4]{1,0:T(4,128)S(1)} %copy-done.7, s32[1]{0:T(128)} %bitcast.p_ref, f32[96,256]{1,0:T(8,128)S(1)} %get-tuple-element.17.mine_ref, f32[96,256]{1,0:T(8,128)S(1)} %collective-permute-done.other_ref, ...), custom_call_target="tpu_custom_call" | custom-call | tf_op jit(solution)/shard_map/turn0/pallas_call | solution.py:286
  31.1 5.9 %collective-permute-start.1 = (f32[1536,256]{1,0:T(8,128)S(1)}, f32[1536,256]{1,0:T(8,128)S(1)}, u32[]{:S(2)}, u32[]{:S(2)}) collective-permute-start(f32[1536,256]{1,0:T(8,128)S(1)} %get-tuple-element.25), channel_id=1, source_target_pairs={{2,4},{6,8},{10,12},{14,16},{18,20},{22,24},{26,28},{30,32},{34,36... | collective-permute-start | bytes 4718600 | tf_op jit(solution)/shard_map/ppermute | solution.py:417
  37.0 20.6 %collective-permute-done.1.a_ref = f32[1536,256]{1,0:T(8,128)S(1)} collective-permute-done((f32[1536,256]{1,0:T(8,128)S(1)}, f32[1536,256]{1,0:T(8,128)S(1)}, u32[]{:S(2)}, u32[]{:S(2)}) %collective-permute-start.1) | collective-permute-done | bytes 1572896 | tf_op jit(solution)/shard_map/ppermute | solution.py:417
  57.6 1.9 %collective-permute-start.6 = (f32[1536,256]{1,0:T(8,128)S(1)}, f32[1536,256]{1,0:T(8,128)S(1)}, u32[]{:S(2)}, u32[]{:S(2)}) collective-permute-start(f32[1536,256]{1,0:T(8,128)S(1)} %get-tuple-element.26), channel_id=1, source_target_pairs={{0,6},{4,10},{8,14},{12,18},{16,22},{20,26},{24,30},{28,34},{32,38... | collective-permute-start | bytes 4718600 | tf_op jit(solution)/shard_map/ppermute | solution.py:420
  59.5 5.7 %pairs.1.mine_ref = f32[96,256]{1,0:T(8,128)S(1)} custom-call(s32[3,4]{1,0:T(4,128)S(1)} %copy-done.7, s32[1]{0:T(128)} %bitcast.p_ref, f32[1536,256]{1,0:T(8,128)S(1)} %collective-permute-done.1.a_ref, f32[1536,256]{1,0:T(8,128)S(1)} %collective-permute-done.2.b_ref), custom_call_target="tpu_custom_call" | custom-call | tf_op jit(solution)/shard_map/pairs/pallas_call | solution.py:314
  65.3 7.3 %collective-permute-start.3 = (f32[96,256]{1,0:T(8,128)S(1)}, f32[96,256]{1,0:T(8,128)S(1)}, u32[]{:S(2)}, u32[]{:S(2)}) collective-permute-start(f32[96,256]{1,0:T(8,128)S(1)} %pairs.1.mine_ref), channel_id=1, source_target_pairs={{0,1},{1,0},{2,3},{3,2},{4,5},{5,4},{6,7},{7,6},{8,9},{9,8},{10,11... | collective-permute-start | bytes 294920 | tf_op jit(solution)/shard_map/ppermute | solution.py:423
  72.6 3.8 %collective-permute-done.3.other_ref = f32[96,256]{1,0:T(8,128)S(1)} collective-permute-done((f32[96,256]{1,0:T(8,128)S(1)}, f32[96,256]{1,0:T(8,128)S(1)}, u32[]{:S(2)}, u32[]{:S(2)}) %collective-permute-start.3) | collective-permute-done | bytes 98336 | tf_op jit(solution)/shard_map/ppermute | solution.py:423
  76.4 4.9 %turn1.1 = (f32[1536,256]{1,0:T(8,128)S(1)}, f32[1536,256]{1,0:T(8,128)S(1)}, f32[16,256]{1,0:T(8,128)S(1)}) custom-call(s32[3,4]{1,0:T(4,128)S(1)} %copy-done.7, s32[1]{0:T(128)} %bitcast.p_ref, f32[96,256]{1,0:T(8,128)S(1)} %pairs.1.mine_ref, f32[96,256]{1,0:T(8,128)S(1)} %collective-permute-done.3.other_ref, ...), custom_call_target="tpu_custom_call" | custom-call | tf_op jit(solution)/shard_map/turn1/pallas_call | solution.py:286
  81.3 1.2 copy-done.5
  82.4 19.7 %collective-permute-start.4 = (f32[16,256]{1,0:T(8,128)S(1)}, f32[16,256]{1,0:T(8,128)S(1)}, u32[]{:S(2)}, u32[]{:S(2)}) collective-permute-start(f32[16,256]{1,0:T(8,128)S(1)} %get-tuple-element.24), channel_id=1, source_target_pairs={{4,0},{8,4},{12,8},{16,12},{20,16},{24,20},{28,24},{32,28},{36,32}... | collective-permute-start | bytes 49160 | tf_op jit(solution)/shard_map/ppermute | solution.py:426
  102.2 1.5 %collective-permute-done.4.coef_ref = f32[16,256]{1,0:T(8,128)S(1)} collective-permute-done((f32[16,256]{1,0:T(8,128)S(1)}, f32[16,256]{1,0:T(8,128)S(1)}, u32[]{:S(2)}, u32[]{:S(2)}) %collective-permute-start.4) | collective-permute-done | bytes 16416 | tf_op jit(solution)/shard_map/ppermute | solution.py:426
  103.7 8.8 %side.1 = (f32[1536,256]{1,0:T(8,128)S(1)}, f32[96,256]{1,0:T(8,128)S(1)}) custom-call(s32[3,4]{1,0:T(4,128)S(1)} %copy-done.7, s32[1]{0:T(128)} %bitcast.p_ref, f32[16,256]{1,0:T(8,128)S(1)} %collective-permute-done.4.coef_ref, f32[1536,256]{1,0:T(8,128)S(1)} %collective-permute-done.5.sx_ref, f32[1536,256]{1,0:T(8,128)S(1)} %collective-permute-done.6.ry_ref, ...), custom_call_target="tpu_custom_call" | custom-call | tf_op jit(solution)/shard_map/side/pallas_call | solution.py:350
  112.5 8.6 %collective-permute-done.7.other_ref = f32[96,256]{1,0:T(8,128)S(1)} collective-permute-done((f32[96,256]{1,0:T(8,128)S(1)}, f32[96,256]{1,0:T(8,128)S(1)}, u32[]{:S(2)}, u32[]{:S(2)}) %collective-permute-start.7) | collective-permute-done | bytes 98336 | tf_op jit(solution)/shard_map/ppermute | solution.py:428
  121.1 1.1 solve.1.own_ref
  122.2 1.5 %collective-permute-start.10 = (f32[16,256]{1,0:T(8,128)S(1)}, f32[16,256]{1,0:T(8,128)S(1)}, u32[]{:S(2)}, u32[]{:S(2)}) collective-permute-start(f32[16,256]{1,0:T(8,128)S(1)} %solve.1.own_ref), channel_id=1, source_target_pairs={{0,2},{2,0},{4,6},{6,4},{8,10},{10,8},{12,14},{14,12},{16,18},{18,... | collective-permute-start | bytes 49160 | tf_op jit(solution)/shard_map/ppermute | solution.py:431
  123.8 0.8 collective-permute-done.10
  125.2 7.1 %collective-permute-done.8.got_ref = f32[16,256]{1,0:T(8,128)S(1)} collective-permute-done((f32[16,256]{1,0:T(8,128)S(1)}, f32[16,256]{1,0:T(8,128)S(1)}, u32[]{:S(2)}, u32[]{:S(2)}) %collective-permute-start.8) | collective-permute-done | bytes 16416 | tf_op jit(solution)/shard_map/ppermute | solution.py:430
  132.3 1.4 copy-done.2
  133.7 8.4 %finish.1 = f32[2,1536,256]{2,1,0:T(8,128)} custom-call(s32[3,4]{1,0:T(4,128)S(1)} %copy-done.7, s32[1]{0:T(128)} %bitcast.p_ref, f32[16,256]{1,0:T(8,128)S(1)} %solve.1.own_ref, f32[16,256]{1,0:T(8,128)S(1)} %collective-permute-done.8.got_ref, f32[1536,256]{1,0:T(8,128)S(1)} %copy-done.2, f32[1536,256]{1,0:T(8,128)S(1)} %get-tuple-element.29.q_ref, ...), custom_call_target="tpu_custom_call" | custom-call | tf_op jit(solution)/shard_map/finish/pallas_call | solution.py:388
  (25 shorter events, 1.5 us)
Async XLA Ops:
  0.6 1.6 %copy-start.3 = (bf16[512,2048]{1,0:T(8,128)(2,1)S(1)}, bf16[512,2048]{1,0:T(8,128)(2,1)}, u32[]{:S(2)}) copy-start(bf16[512,2048]{1,0:T(8,128)(2,1)} %cols_ref.1) | copy-start | bytes 6291460
  2.2 0.7 copy-start.6
  2.9 23.4 %copy-start.7 = (s32[3,4]{1,0:T(4,128)S(1)}, s32[3,4]{1,0:T(4,128)}, u32[]{:S(2)}) copy-start(s32[3,4]{1,0:T(4,128)} %o_ref.13) | copy-start | bytes 148
  15.1 1.1 copy-start.4
  16.2 10.1 %collective-permute-start = (f32[96,256]{1,0:T(8,128)S(1)}, f32[96,256]{1,0:T(8,128)S(1)}, u32[]{:S(2)}, u32[]{:S(2)}) collective-permute-start(f32[96,256]{1,0:T(8,128)S(1)} %get-tuple-element.17.mine_ref), channel_id=1, source_target_pairs={{0,1},{1,0},{2,3},{3,2},{4,5},{5,4},{6,7},{7,6},{8,9},{9,8},{10,11... | collective-permute-start | bytes 294920 | tf_op jit(solution)/shard_map/ppermute | solution.py:415
  31.1 26.5 %collective-permute-start.1 = (f32[1536,256]{1,0:T(8,128)S(1)}, f32[1536,256]{1,0:T(8,128)S(1)}, u32[]{:S(2)}, u32[]{:S(2)}) collective-permute-start(f32[1536,256]{1,0:T(8,128)S(1)} %get-tuple-element.25), channel_id=1, source_target_pairs={{2,4},{6,8},{10,12},{14,16},{18,20},{22,24},{26,28},{30,32},{34,36... | collective-permute-start | bytes 4718600 | tf_op jit(solution)/shard_map/ppermute | solution.py:417
  36.9 20.7 %collective-permute-start.2 = (f32[1536,256]{1,0:T(8,128)S(1)}, f32[1536,256]{1,0:T(8,128)S(1)}, u32[]{:S(2)}, u32[]{:S(2)}) collective-permute-start(f32[1536,256]{1,0:T(8,128)S(1)} %get-tuple-element.26), channel_id=1, source_target_pairs={{0,2},{2,0},{4,6},{6,4},{8,10},{10,8},{12,14},{14,12},{16,18},{18,... | collective-permute-start | bytes 4718600 | tf_op jit(solution)/shard_map/ppermute | solution.py:418
  57.6 7.7 %copy-start = (f32[1536,256]{1,0:T(8,128)}, f32[1536,256]{1,0:T(8,128)S(1)}, u32[]{:S(2)}) copy-start(f32[1536,256]{1,0:T(8,128)S(1)} %collective-permute-done.2.b_ref) | copy-start | bytes 4718596
  57.6 46.1 %collective-permute-start.5 = (f32[1536,256]{1,0:T(8,128)S(1)}, f32[1536,256]{1,0:T(8,128)S(1)}, u32[]{:S(2)}, u32[]{:S(2)}) collective-permute-start(f32[1536,256]{1,0:T(8,128)S(1)} %get-tuple-element.25), channel_id=1, source_target_pairs={{0,2},{2,0},{4,6},{6,4},{8,10},{10,8},{12,14},{14,12},{16,18},{18,... | collective-permute-start | bytes 4718600 | tf_op jit(solution)/shard_map/ppermute | solution.py:421
  57.6 46.1 %collective-permute-start.6 = (f32[1536,256]{1,0:T(8,128)S(1)}, f32[1536,256]{1,0:T(8,128)S(1)}, u32[]{:S(2)}, u32[]{:S(2)}) collective-permute-start(f32[1536,256]{1,0:T(8,128)S(1)} %get-tuple-element.26), channel_id=1, source_target_pairs={{0,6},{4,10},{8,14},{12,18},{16,22},{20,26},{24,30},{28,34},{32,38... | collective-permute-start | bytes 4718600 | tf_op jit(solution)/shard_map/ppermute | solution.py:420
  65.3 11.1 %collective-permute-start.3 = (f32[96,256]{1,0:T(8,128)S(1)}, f32[96,256]{1,0:T(8,128)S(1)}, u32[]{:S(2)}, u32[]{:S(2)}) collective-permute-start(f32[96,256]{1,0:T(8,128)S(1)} %pairs.1.mine_ref), channel_id=1, source_target_pairs={{0,1},{1,0},{2,3},{3,2},{4,5},{5,4},{6,7},{7,6},{8,9},{9,8},{10,11... | collective-permute-start | bytes 294920 | tf_op jit(solution)/shard_map/ppermute | solution.py:423
  81.3 1.2 copy-start.5
  82.4 21.2 %copy-start.1 = (f32[1536,256]{1,0:T(8,128)}, f32[1536,256]{1,0:T(8,128)S(1)}, u32[]{:S(2)}) copy-start(f32[1536,256]{1,0:T(8,128)S(1)} %get-tuple-element.27.z_ref) | copy-start | bytes 4718596
  82.4 42.8 %collective-permute-start.9 = (f32[1536,256]{1,0:T(8,128)S(1)}, f32[1536,256]{1,0:T(8,128)S(1)}, u32[]{:S(2)}, u32[]{:S(2)}) collective-permute-start(f32[1536,256]{1,0:T(8,128)S(1)} %get-tuple-element.27.z_ref), channel_id=1, source_target_pairs={{0,4},{4,8},{8,12},{12,16},{16,20},{20,24},{24,28},{28,32},{32,36}... | collective-permute-start | bytes 4718600 | tf_op jit(solution)/shard_map/ppermute | solution.py:425
  82.4 21.2 %collective-permute-start.4 = (f32[16,256]{1,0:T(8,128)S(1)}, f32[16,256]{1,0:T(8,128)S(1)}, u32[]{:S(2)}, u32[]{:S(2)}) collective-permute-start(f32[16,256]{1,0:T(8,128)S(1)} %get-tuple-element.24), channel_id=1, source_target_pairs={{4,0},{8,4},{12,8},{16,12},{20,16},{24,20},{28,24},{32,28},{36,32}... | collective-permute-start | bytes 49160 | tf_op jit(solution)/shard_map/ppermute | solution.py:426
  112.4 8.7 %collective-permute-start.7 = (f32[96,256]{1,0:T(8,128)S(1)}, f32[96,256]{1,0:T(8,128)S(1)}, u32[]{:S(2)}, u32[]{:S(2)}) collective-permute-start(f32[96,256]{1,0:T(8,128)S(1)} %get-tuple-element.28.mine_ref), channel_id=1, source_target_pairs={{0,1},{1,0},{2,3},{3,2},{4,5},{5,4},{6,7},{7,6},{8,9},{9,8},{10,11... | collective-permute-start | bytes 294920 | tf_op jit(solution)/shard_map/ppermute | solution.py:428
  122.2 2.4 %collective-permute-start.10 = (f32[16,256]{1,0:T(8,128)S(1)}, f32[16,256]{1,0:T(8,128)S(1)}, u32[]{:S(2)}, u32[]{:S(2)}) collective-permute-start(f32[16,256]{1,0:T(8,128)S(1)} %solve.1.own_ref), channel_id=1, source_target_pairs={{0,2},{2,0},{4,6},{6,4},{8,10},{10,8},{12,14},{14,12},{16,18},{18,... | collective-permute-start | bytes 49160 | tf_op jit(solution)/shard_map/ppermute | solution.py:431
  123.8 8.5 %collective-permute-start.8 = (f32[16,256]{1,0:T(8,128)S(1)}, f32[16,256]{1,0:T(8,128)S(1)}, u32[]{:S(2)}, u32[]{:S(2)}) collective-permute-start(f32[16,256]{1,0:T(8,128)S(1)} %solve.1.own_ref), channel_id=1, source_target_pairs={{0,4},{4,8},{8,12},{12,16},{16,20},{20,24},{24,28},{28,32},{32,36}... | collective-permute-start | bytes 49160 | tf_op jit(solution)/shard_map/ppermute | solution.py:430
  132.3 1.4 copy-start.2
where the time goes:
time: 143 us; the launch traced here: 142 us
  Pallas kernels  45.8 us (32%)
  waiting for transfers between devices  45.3 us (32%)
  starting transfers between devices  43.7 us (31%)
  local copies, waits for them, and re-layouts  5.98 us (4%)
    ppermute x1, waiting for transfers between devices, body(): rx = lax.ppermute(x, 'blk', meet)  20.6 us
    ppermute x1, starting transfers between devices, body(): coef_side = lax.ppermute(coef_b, 'blk', tell)  19.7 us
    ppermute x3, waiting for transfers between devices, body(): lag_other = lax.ppermute(lag, 'row', across)  15.3 us
    ppermute x3, starting transfers between devices, body(): lag_other = lax.ppermute(lag, 'row', across)  14.6 us
    pallas_call x1, Pallas kernels, first(): call(first_kernel, 'first', rows // r, [SMEM, pl.BlockSpec((r, feat), lam...  12.2 us
    pallas_call x2, Pallas kernels, turn(): call(functools.partial(turn_kernel, round_index), 'turn%d' % round_index,...  9.65 us
    pallas_call x1, Pallas kernels, side(): call(functools.partial(side_kernel, last), 'side', rows // r, [SMEM, SMEM...  8.75 us
    pallas_call x1, Pallas kernels, finish(): call(functools.partial(last_kernel, last), 'finish', rows // r, [SMEM, SM...  8.44 us
  transfers between devices with their start and end apart: 11, of which 7 were waited for; matrix products, arithmetic and copies ran while one was open for 0% of the time, Pallas kernels for 14%

commit v1 on v0

v1 whole, which is shorter than its diff:
```python
import functools
import math

import jax
import jax.numpy as jnp
from jax import lax
from jax.experimental import pallas as pl
from jax.experimental.pallas import tpu as pltpu
from jax.sharding import PartitionSpec as P

F32 = jnp.float32
BF16 = jnp.bfloat16
W = 256
H = 128
LAGS = 96
VMEM_LIMIT = 24 * 1024 * 1024
FIRST_LIMIT = 50 * 1024 * 1024


def group_rows(m):
    return (16 * m, 16) if m < 4 else (64 + 8 * (m - 4), 8)


def lag_targets(o):
    t, s = [0], [0]
    first, second = [0], [1]
    rows = {}
    for step in range(4):
        count = 1 << step
        for m in range(count):
            start, _ = group_rows(m)
            place = {3: 0, 2: 8, 1: 12, 0: 14}[step]
            for n in range(count):
                lag = (o[step] + s[n] - t[m]) & (W - 1)
                rows[start + place + n] = lag + W * second[n]
        if step < 3:
            t, s = t + [x + o[step] for x in s], s + [x - o[step] for x in t]
            first, second = first + second, second + first
    rows[15] = 0
    rows[16 + 14] = W
    return rows, t, first


def split(x):
    hi = x.astype(BF16)
    return hi, (x - hi.astype(F32)).astype(BF16)


TN = (((0,), (0,)), ((), ()))
NT = (((1,), (1,)), ((), ()))


def skew(x):
    row = lax.broadcasted_iota(jnp.int32, (W, W), 0)
    for bit in (1, 2, 4):
        x = jnp.where((row & bit) != 0, pltpu.roll(x, W - bit, 1), x)
    tiles = [pltpu.roll(x[8 * t : 8 * t + 8], (W - 8 * t) % W, 1) for t in range(W // 8)]
    return jnp.concatenate(tiles, axis=0)


def build_onehot(o, table_ref):
    rows, _, _ = lag_targets(o)
    table_ref[...] = jnp.full((LAGS, 128), -1, jnp.int32)
    for r, target in rows.items():
        table_ref[r : r + 1, :] = jnp.full((1, 128), target, jnp.int32)
    table = jnp.concatenate([table_ref[...]] * 4, axis=1)
    return (table == lax.broadcasted_iota(jnp.int32, (LAGS, 2 * W), 1)).astype(F32).astype(BF16)


def lag_products(gram, o, onehot, out_ref):
    _, bases, first = lag_targets(o)
    diags = {}
    for kind in (0, 1):
        sheets = [skew(gram[kind * W : (kind + 1) * W, side * W : (side + 1) * W]) for side in (0, 1)]
        hi, lo = split(jnp.concatenate(sheets, axis=1))
        diags[kind] = lax.dot_general(onehot, lo, NT, preferred_element_type=F32) + lax.dot_general(
            onehot, hi, NT, preferred_element_type=F32
        )
    for m in range(8):
        start, count = group_rows(m)
        tile = diags[first[m]][start : start + count]
        if m > 0:
            tile = pltpu.roll(tile, (-bases[m]) & (W - 1), 1)
        out_ref[start : start + count, :] = tile


def gram_of(a, b):
    hi, lo = split(jnp.concatenate([a, b], axis=1))
    return (
        lax.dot_general(hi, lo, TN, preferred_element_type=F32)
        + lax.dot_general(lo, hi, TN, preferred_element_type=F32)
        + lax.dot_general(hi, hi, TN, preferred_element_type=F32)
    )


def angle(g, upper_sq, lower_sq):
    twice = 2.0 * g
    diff = upper_sq - lower_sq
    scale = jnp.maximum(jnp.abs(twice), jnp.abs(diff))
    live = scale > 0.0
    safe = jnp.where(live, scale, 1.0)
    x = jnp.where(live, diff / safe, 1.0)
    y = jnp.where(live, twice / safe, 0.0)
    r = jnp.sqrt(x * x + y * y)
    big = jnp.sqrt(0.5 * (1.0 + jnp.abs(x) / r))
    small = 0.5 * jnp.abs(y) / (r * big)
    wide = x < 0.0
    c = jnp.where(wide, small, big)
    s = jnp.where(wide, big, small)
    s = jnp.where(y < 0.0, -s, s)
    cross = twice * c * s
    return c, s, c * c * upper_sq + cross + s * s * lower_sq, s * s * upper_sq - cross + c * c * lower_sq


def angles(lags, o, coef_ref):
    row = lax.broadcasted_iota(jnp.int32, (8, W), 0)
    a = jnp.ones((8, W), F32)
    b = jnp.ones((8, W), F32)
    upper_sq = lags[15:16]
    lower_sq = lags[30:31]
    tiles = [lags[16 * m + 8 : 16 * m + 16] for m in range(4)]
    last = [lags[group_rows(m)[0] : group_rows(m)[0] + 8] for m in range(8)]
    for step in range(4):
        count = 1 << step
        if step == 3:
            parts, place = last, 0
        else:
            parts, place = tiles[:count], (6, 4, 0)[step]
        acc = None
        for m in range(count):
            term = a[m : m + 1] * parts[m]
            acc = term if acc is None else acc + term
        view = pltpu.roll(b, place, 0) if place else b
        acc = jnp.where((row >= place) & (row < place + count), acc * view, 0.0)
        g = jnp.sum(acc, axis=0, keepdims=True)
        c, s, upper_sq, lower_sq = angle(g, upper_sq, lower_sq)
        coef_ref[step : step + 1, :] = c
        coef_ref[4 + step : 5 + step, :] = s
        if step < 3:
            shift_a, shift_b = pltpu.roll(a, count, 0), pltpu.roll(b, count, 0)
            a, b = jnp.where(row < count, c * a, s * shift_b), jnp.where(row < count, c * b, -s * shift_a)
            turn = (o[step] - o[step + 1]) & (W - 1)
            b = pltpu.roll(b, turn, 1)
            lower_sq = pltpu.roll(jnp.broadcast_to(lower_sq, (8, W)), turn, 1)[0:1]
    coef_ref[8:9, :] = upper_sq
    coef_ref[9:10, :] = pltpu.roll(jnp.broadcast_to(lower_sq, (8, W)), o[3] & (W - 1), 1)[0:1]


def halves(x):
    return [x[:, :H], x[:, H:]]


def turn_halves(x, amount):
    short = amount & (H - 1)
    lane = lax.broadcasted_iota(jnp.int32, (1, H), 1)
    cross = (lane < short) != ((amount & H) != 0)
    a, b = pltpu.roll(x[0], short, 1), pltpu.roll(x[1], short, 1)
    return [jnp.where(cross, b, a), jnp.where(cross, a, b)]


def rotate(upper, lower, coef, o):
    upper, lower = list(upper), turn_halves(lower, (-o[0]) & (W - 1))
    for step in range(4):
        for h in (0, 1):
            c = coef[step : step + 1, h * H : (h + 1) * H]
            s = coef[4 + step : 5 + step, h * H : (h + 1) * H]
            upper[h], lower[h] = c * upper[h] + s * lower[h], c * lower[h] - s * upper[h]
        turn = (o[step] - o[step + 1]) if step < 3 else o[3]
        lower = turn_halves(lower, turn & (W - 1))
    return upper, lower


SMEM = pl.BlockSpec(memory_space=pltpu.SMEM)
VMEM = pl.BlockSpec(memory_space=pltpu.VMEM)
ANY = pl.BlockSpec(memory_space=pl.ANY)
LAG_SHAPE = jax.ShapeDtypeStruct((LAGS, W), F32)
COEF_SHAPE = jax.ShapeDtypeStruct((16, W), F32)
ONEHOT_SHAPE = jax.ShapeDtypeStruct((LAGS, 2 * W), BF16)
TABLE = pltpu.VMEM((LAGS, 128), jnp.int32)


def tile_rows(rows, most=512):
    r = most
    while rows % r:
        r //= 2
    return r


def block(rows):
    return jax.ShapeDtypeStruct((rows, W), F32)


def call(kernel, name, in_specs, out_specs, out_shape, scratch=(), us=1, limit=VMEM_LIMIT):
    return pl.pallas_call(
        kernel,
        name=name,
        in_specs=in_specs,
        out_specs=out_specs,
        out_shape=out_shape,
        scratch_shapes=list(scratch),
        compiler_params=pltpu.CompilerParams(vmem_limit_bytes=limit),
        cost_estimate=pl.CostEstimate(flops=us * 10**9, bytes_accessed=us * 3 * 10**6, transcendentals=0),
    )


def offsets_of(o_ref, round_index):
    return [o_ref[round_index, j] for j in range(4)]


def pick(flag, a, b):
    return jnp.where(flag, a, b), jnp.where(flag, b, a)


def pick_halves(flag, a, b):
    pairs = [pick(flag, x, y) for x, y in zip(a, b)]
    return [x for x, _ in pairs], [y for _, y in pairs]


def read(ref, rows):
    return [ref[rows, :H], ref[rows, H:]]


def write(ref, rows, x):
    ref[rows, :H] = x[0]
    ref[rows, H:] = x[1]


def by_tiles(rows, go):
    r = tile_rows(rows)

    @pl.loop(0, rows // r)
    def _(i):
        go(pl.ds(pl.multiple_of(i * r, r), r))


def first_kernel(
    o_hbm, rows_hbm, cols_hbm, upper_ref, lower_ref, lag_ref, rows_ref, cols_ref, table_ref, norm_ref, o_ref, sem
):
    count, feat = cols_ref.shape
    total = rows_ref.shape[0]
    r = tile_rows(total)
    tiles = total // r
    half = count // 2
    fetch_cols = [
        pltpu.make_async_copy(cols_hbm.at[pl.ds(k * half, half)], cols_ref.at[pl.ds(k * half, half)], sem.at[k])
        for k in range(2)
    ]
    fetch_rows = [
        pltpu.make_async_copy(rows_hbm.at[pl.ds(t * r, r)], rows_ref.at[pl.ds(t * r, r)], sem.at[2 + t])
        for t in range(tiles)
    ]
    fetch_o = pltpu.make_async_copy(o_hbm, o_ref, sem.at[15])
    for copy in [fetch_o] + fetch_cols + fetch_rows:
        copy.start()
    fetch_o.wait()
    o = offsets_of(o_ref, 0)
    onehot = build_onehot(o, table_ref)
    for copy in fetch_cols:
        copy.wait()
    for t in range(tiles):
        fetch_rows[t].wait()
        if t == 0:
            for k in range(0, count, H):
                wide = cols_ref[k : k + H].astype(F32)
                sums = jnp.sum(wide * wide, axis=1, keepdims=True)
                norm_ref[:, k : k + H] = jnp.transpose(jnp.broadcast_to(sums, (H, H)))[0:8]
        part = slice(t * r, (t + 1) * r)
        rows = rows_ref[part]
        cross = lax.dot_general(rows, cols_ref[...], NT, preferred_element_type=F32)
        wide = rows.astype(F32)
        row_norm = jnp.sum(wide * wide, axis=1, keepdims=True)
        kernel = jnp.exp(
            -(0.25 / math.sqrt(feat)) * (row_norm + norm_ref[0:1] - 2.0 * cross - 2.0 * feat)
        )
        upper_ref[part] = kernel[:, :W]
        lower_ref[part] = kernel[:, W:]
    lag_products(gram_of(upper_ref[...], lower_ref[...]), o, onehot, lag_ref)


def first(offsets, row_feats, col_feats):
    rows, feat = row_feats.shape
    return call(
        first_kernel,
        "first",
        [ANY, ANY, ANY],
        (VMEM, VMEM, VMEM),
        (block(rows), block(rows), LAG_SHAPE),
        [
            pltpu.VMEM(row_feats.shape, BF16),
            pltpu.VMEM(col_feats.shape, BF16),
            TABLE,
            pltpu.VMEM((8, 2 * W), F32),
            pltpu.SMEM((3, 4), jnp.int32),
            pltpu.SemaphoreType.DMA((16,)),
        ],
        us=10,
        limit=FIRST_LIMIT,
    )(offsets, row_feats, col_feats)


def table_kernel(round_index, o_ref, after_ref, out_ref, table_ref):
    out_ref[...] = build_onehot(offsets_of(o_ref, round_index), table_ref)


def table(round_index, offsets, after):
    return call(
        functools.partial(table_kernel, round_index), "table%d" % round_index, [SMEM, ANY], VMEM, ONEHOT_SHAPE, [TABLE]
    )(offsets, after)


def turn_kernel(round_index, o_ref, p_ref, mine_ref, other_ref, a_ref, b_ref, first_ref, second_ref, coef_ref):
    p = p_ref[0]
    core = p & 1
    o = offsets_of(o_ref, round_index)
    angles(mine_ref[...] + other_ref[...], o, coef_ref)
    coef = coef_ref[...]

    def go(rows):
        upper, lower = read(a_ref, rows), read(b_ref, rows)
        if round_index == 0:
            keep = (core == 1) | (p == 0)
        else:
            upper, lower = pick_halves(core == 0, upper, lower)
            keep = (core == 0) & (p != 0)
        upper, lower = rotate(upper, lower, coef, o)
        upper, lower = pick_halves(keep, upper, lower)
        write(first_ref, rows, upper)
        write(second_ref, rows, lower)

    by_tiles(a_ref.shape[0], go)


def turn(round_index, offsets, p, mine, other, a, b):
    rows = a.shape[0]
    return call(
        functools.partial(turn_kernel, round_index),
        "turn%d" % round_index,
        [SMEM, SMEM] + [VMEM] * 4,
        (VMEM, VMEM, VMEM),
        (block(rows), block(rows), COEF_SHAPE),
        us=40,
    )(offsets, p, mine, other, a, b)


def pairs_kernel(o_ref, p_ref, hot_ref, a_ref, b_ref, lag_ref):
    upper, lower = pick((p_ref[0] & 1) == 0, a_ref[...], b_ref[...])
    lag_products(gram_of(upper, lower), offsets_of(o_ref, 1), hot_ref[...], lag_ref)


def pairs(offsets, p, hot, a, b):
    return call(
        pairs_kernel, "pairs", [SMEM, SMEM] + [VMEM] * 3, VMEM, LAG_SHAPE, us=5
    )(offsets, p, hot, a, b)


def side_kernel(last, o_ref, p_ref, hot_ref, coef_ref, sx_ref, ry_ref, z_ref, q_ref, lag_ref):
    p = p_ref[0]
    core = p & 1
    o = offsets_of(o_ref, 1)
    coef = coef_ref[...]
    near_end = (p == 1) | (p == last - 1)

    def go(rows):
        upper, lower = pick_halves((core == 0) != near_end, read(sx_ref, rows), read(ry_ref, rows))
        upper, lower = rotate(upper, lower, coef, o)
        wanted, _ = pick_halves((core == 1) | (p == last - 1), upper, lower)
        write(q_ref, rows, wanted)

    by_tiles(sx_ref.shape[0], go)
    upper, lower = pick(core == 0, z_ref[...], q_ref[...])
    lag_products(gram_of(upper, lower), offsets_of(o_ref, 2), hot_ref[...], lag_ref)


def side(last, offsets, p, hot, coef, sx, ry, z):
    return call(
        functools.partial(side_kernel, last),
        "side",
        [SMEM, SMEM] + [VMEM] * 5,
        (VMEM, VMEM),
        (block(sx.shape[0]), LAG_SHAPE),
        us=8,
    )(offsets, p, hot, coef, sx, ry, z)


def solve_kernel(o_ref, mine_ref, other_ref, coef_ref):
    angles(mine_ref[...] + other_ref[...], offsets_of(o_ref, 2), coef_ref)


def solve(offsets, mine, other):
    return call(solve_kernel, "solve", [SMEM, VMEM, VMEM], VMEM, COEF_SHAPE)(offsets, mine, other)


def own_kernel(o_ref, p_ref, coef_ref, z_ref, q_ref, out_ref):
    p = p_ref[0]
    core = p & 1
    o = offsets_of(o_ref, 2)
    coef = coef_ref[...]

    def go(rows):
        upper, lower = pick_halves(core == 0, read(z_ref, rows), read(q_ref, rows))
        upper, lower = rotate(upper, lower, coef, o)
        wanted, _ = pick_halves((core == 1) & (p != 1), upper, lower)
        write(out_ref, rows, [x * x for x in wanted])

    by_tiles(z_ref.shape[0], go)


def own(offsets, p, coef, z, q):
    return call(own_kernel, "own", [SMEM, SMEM] + [VMEM] * 3, VMEM, block(z.shape[0]), us=4)(
        offsets, p, coef, z, q
    )


def finish_kernel(
    last, row_total, o_ref, p_ref, coef_ref, a_ref, b_ref, c_ref, own_ref, r_ref, v_ref, out_hbm, norm_ref, e_ref, sem
):
    p = p_ref[0]
    core = p & 1
    o = offsets_of(o_ref, 2)
    keep = pltpu.make_async_copy(own_ref, out_hbm.at[1 - core], sem.at[0])
    keep.start()
    coef = coef_ref[...]
    for k, ref in enumerate((a_ref, b_ref, c_ref)):
        norm_ref[k] = ref[8:10, :] / row_total
    total = r_ref.shape[0]
    r = tile_rows(total)
    sends = []
    for t in range(total // r):
        rows = pl.ds(t * r, r)
        swap = (p == 0) | (p == last)
        upper, lower = pick_halves((core == 0) != swap, read(r_ref, rows), read(v_ref, rows))
        upper, lower = rotate(upper, lower, coef, o)
        wanted, _ = pick_halves((core == 0) | (p == last), upper, lower)
        write(e_ref, rows, [x * x for x in wanted])
        copy = pltpu.make_async_copy(e_ref.at[rows], out_hbm.at[core, rows], sem.at[1 + t])
        copy.start()
        sends.append(copy)
    for copy in [keep] + sends:
        copy.wait()


def finish(last, row_total, offsets, p, coef, coefs, own_block, r_block, v):
    rows = v.shape[0]
    return call(
        functools.partial(finish_kernel, last, row_total),
        "finish",
        [SMEM, SMEM] + [VMEM] * 7,
        (ANY, VMEM),
        (jax.ShapeDtypeStruct((2, rows, W), F32), jax.ShapeDtypeStruct((3, 2, W), F32)),
        [pltpu.VMEM((rows, W), F32), pltpu.SemaphoreType.DMA((16,))],
        us=5,
    )(offsets, p, coef, *coefs, own_block, r_block, v)


def body(row_feats, col_feats, offsets):
    n = lax.axis_size("blk")
    chips = n // 2
    p = lax.axis_index("blk").astype(jnp.int32).reshape(1)
    row_total = row_feats.shape[0] * lax.axis_size("row")
    across = [(0, 1), (1, 0)]
    sibling = [(i, i ^ 1) for i in range(n)]
    meet = [(2 * j + 1, 2 * j + 2) for j in range(chips - 1)] + [(2 * j, 2 * j - 1) for j in range(1, chips)]
    meet += [(0, 0), (n - 1, n - 1)]
    lend = [(2 * j, 2 * j + 3) for j in range(chips - 1)] + [(2 * j + 1, 2 * j - 2) for j in range(1, chips)]
    lend += [(1, 1), (n - 2, n - 2)]
    deal = [(2 * j, 2 * j + 2) for j in range(chips - 1)] + [(2 * j + 1, 2 * j - 1) for j in range(1, chips)]
    deal += [(1, 0), (n - 2, n - 1)]
    tell = [(2 * j, 2 * j - 2) for j in range(1, chips)] + [(2 * j + 1, 2 * j + 3) for j in range(chips - 1)]
    tell += [(0, 1), (n - 1, n - 2)]

    upper, lower, lag = first(offsets, row_feats, col_feats)
    lag_other = lax.ppermute(lag, "row", across)
    hot = table(1, offsets, lag)
    x, y, coef_a = turn(0, offsets, p, lag, lag_other, upper, lower)
    rx = lax.ppermute(x, "blk", meet)
    sy = lax.ppermute(y, "blk", sibling)
    sx = lax.ppermute(x, "blk", sibling)
    lag = pairs(offsets, p, hot, rx, sy)
    lag_other = lax.ppermute(lag, "row", across)
    hot = table(2, offsets, lag)
    y, hot = lax.optimization_barrier((y, hot))
    ry = lax.ppermute(y, "blk", lend)
    z, v, coef_b = turn(1, offsets, p, lag, lag_other, rx, sy)
    coef_side = lax.ppermute(coef_b, "blk", tell)
    z, coef_side = lax.optimization_barrier((z, coef_side))
    r_block = lax.ppermute(z, "blk", deal)
    q, lag = side(n - 1, offsets, p, hot, coef_side, sx, ry, z)
    lag_other = lax.ppermute(lag, "row", across)
    coef_c = solve(offsets, lag, lag_other)
    coef_got = lax.ppermute(coef_c, "blk", deal)
    coef_norm = lax.ppermute(coef_c, "blk", sibling)
    own_block = own(offsets, p, coef_c, z, q)
    return finish(n - 1, row_total, offsets, p, coef_got, (coef_a, coef_b, coef_norm), own_block, r_block, v)


def solution(mesh):
    return jax.shard_map(
        body,
        mesh=mesh,
        in_specs=(P("row", None), P("blk", None), P()),
        out_specs=(P(None, "row", "blk"), P(None, None, "blk")),
        check_vma=False,
    )
```

time: 143 us -> 121 us (0.85)
  starting transfers between devices: 43.7 us -> 33.1 us
  Pallas kernels: 45.8 us -> 40.4 us
  local copies, waits for them, and re-layouts: 5.98 us -> 0.68 us
    ppermute x1, starting transfers between devices: 19.7 us -> 6.44 us  [body(): coef_side = lax.ppermute(coef_b, 'blk', tell)]
    ppermute x1, waiting for transfers between devices: 0.01 us -> 7.72 us  [body(): ry = lax.ppermute(y, 'blk', lend)]
    unnamed x16 -> x4, local copies, waits for them, and re-layouts: 5.98 us -> 0.68 us
    ppermute x1, waiting for transfers between devices: 7.1 us -> 3.53 us  [body(): coef_got = lax.ppermute(coef_c, 'blk', deal)]
    pallas_call x5 -> x8, Pallas kernels: 36.1 us -> 33 us  [the longest x1 10.7 us: first(): call(first_kernel, 'first', [ANY, ANY, ANY], (VMEM, VMEM, VMEM), (block(r...]
    ppermute x1, starting transfers between devices: 1.53 us -> 3.85 us  [body(): coef_norm = lax.ppermute(coef_c, 'blk', sibling)]
    ppermute x3, waiting for transfers between devices: 15.3 us -> 13 us  [body(): lag_other = lax.ppermute(lag, 'row', across)]
    pallas_call x2, Pallas kernels: 9.65 us -> 7.47 us  [turn(): call(functools.partial(turn_kernel, round_index), 'turn%d' % round_index,...]
where the time goes in v1:
time: 121 us
  waiting for transfers between devices  45.5 us (38%)
  Pallas kernels  40.4 us (33%)
  starting transfers between devices  33.1 us (27%)
    ppermute x1, waiting for transfers between devices, body(): rx = lax.ppermute(x, 'blk', meet)  19.8 us
    ppermute x3, starting transfers between devices, body(): lag_other = lax.ppermute(lag, 'row', across)  14.8 us
    ppermute x3, waiting for transfers between devices, body(): lag_other = lax.ppermute(lag, 'row', across)  13 us
    pallas_call x1, Pallas kernels, first(): call(first_kernel, 'first', [ANY, ANY, ANY], (VMEM, VMEM, VMEM), (block(r...  10.7 us
    ppermute x1, waiting for transfers between devices, body(): ry = lax.ppermute(y, 'blk', lend)  7.72 us
    pallas_call x2, Pallas kernels, turn(): call(functools.partial(turn_kernel, round_index), 'turn%d' % round_index,...  7.47 us
    pallas_call x1, Pallas kernels, side(): call(functools.partial(side_kernel, last), 'side', [SMEM, SMEM] + [VMEM]...  7.28 us
    ppermute x1, starting transfers between devices, body(): coef_side = lax.ppermute(coef_b, 'blk', tell)  6.44 us
  transfers between devices with their start and end apart: 11, of which 7 were waited for; matrix products, arithmetic and copies ran while one was open for 0% of the time, Pallas kernels for 14%

profile of v1, /device:TPU:4, one launch (start us, length us, event | category | flops | bytes accessed | tf_op | source)
XLA Modules:
  0.0 120.7 jit_solution(6648884531546172944)
XLA Ops:
  0.6 0.7 copy-done
  1.3 10.7 %first.1 = (f32[1536,256]{1,0:T(8,128)S(1)}, f32[1536,256]{1,0:T(8,128)S(1)}, f32[96,256]{1,0:T(8,128)S(1)}) custom-call(s32[3,4]{1,0:T(4,128)S(1)} %copy-done, bf16[1536,2048]{1,0:T(8,128)(2,1)} %rows_hbm.1, bf16[512,2048]{1,0:T(8,128)(2,1)} %cols_hbm.1), custom_call_target="tpu_custom_call" | custom-call | flops 10000000000 | bytes 30000000 | tf_op jit(solution)/shard_map/first/pallas_call | solution.py:282
  12.0 7.3 %collective-permute-start = (f32[96,256]{1,0:T(8,128)S(1)}, f32[96,256]{1,0:T(8,128)S(1)}, u32[]{:S(2)}, u32[]{:S(2)}) collective-permute-start(f32[96,256]{1,0:T(8,128)S(1)} %get-tuple-element.17.mine_ref.after_ref), channel_id=1, source_target_pairs={{0,1},{1,0},{2,3},{3,2},{4,5},{5,4},{6,7},{7,6},{8,9},{9,8},{10,11... | collective-permute-start | bytes 294920 | tf_op jit(solution)/shard_map/ppermute | solution.py:472
  19.3 2.9 %collective-permute-done.other_ref = f32[96,256]{1,0:T(8,128)S(1)} collective-permute-done((f32[96,256]{1,0:T(8,128)S(1)}, f32[96,256]{1,0:T(8,128)S(1)}, u32[]{:S(2)}, u32[]{:S(2)}) %collective-permute-start) | collective-permute-done | bytes 98336 | tf_op jit(solution)/shard_map/ppermute | solution.py:472
  22.2 3.7 %turn0.1 = (f32[1536,256]{1,0:T(8,128)S(1)}, f32[1536,256]{1,0:T(8,128)S(1)}, f32[16,256]{1,0:T(8,128)S(1)}) custom-call(s32[3,4]{1,0:T(4,128)S(1)} %copy-done.1, s32[1]{0:T(128)} %bitcast.p_ref, f32[96,256]{1,0:T(8,128)S(1)} %get-tuple-element.17.mine_ref.after_ref, f32[96,256]{1,0:T(8,128)S(1)} %collective-permute-done.other_ref, ...), custom_call_target="tpu_custom_call" | custom-call | flops 40000000000 | bytes 120000000 | tf_op jit(solution)/shard_map/turn0/pallas_call | solution.py:335
  26.0 5.8 %collective-permute-start.1 = (f32[1536,256]{1,0:T(8,128)S(1)}, f32[1536,256]{1,0:T(8,128)S(1)}, u32[]{:S(2)}, u32[]{:S(2)}) collective-permute-start(f32[1536,256]{1,0:T(8,128)S(1)} %get-tuple-element.21), channel_id=1, source_target_pairs={{2,4},{6,8},{10,12},{14,16},{18,20},{22,24},{26,28},{30,32},{34,36... | collective-permute-start | bytes 4718600 | tf_op jit(solution)/shard_map/ppermute | solution.py:475
  32.1 0.7 table1.1.hot_ref
  32.7 19.8 %collective-permute-done.1.a_ref = f32[1536,256]{1,0:T(8,128)S(1)} collective-permute-done((f32[1536,256]{1,0:T(8,128)S(1)}, f32[1536,256]{1,0:T(8,128)S(1)}, u32[]{:S(2)}, u32[]{:S(2)}) %collective-permute-start.1) | collective-permute-done | bytes 1572896 | tf_op jit(solution)/shard_map/ppermute | solution.py:475
  52.5 4.6 %pairs.1.after_ref.mine_ref = f32[96,256]{1,0:T(8,128)S(1)} custom-call(s32[3,4]{1,0:T(4,128)S(1)} %copy-done.1, s32[1]{0:T(128)} %bitcast.p_ref, bf16[96,512]{1,0:T(8,128)(2,1)S(1)} %table1.1.hot_ref, f32[1536,256]{1,0:T(8,128)S(1)} %collective-permute-done.1.a_ref, f32[1536,256]{1,0:T(8,128)S(1)} %collective-permute-done.2.b_ref), custom_call_target="tpu_custom_call" | custom-call | flops 5000000000 | bytes 15000000 | tf_op jit(solution)/shard_map/pairs/pallas_call | solution.py:351
  57.1 7.1 %collective-permute-start.3 = (f32[96,256]{1,0:T(8,128)S(1)}, f32[96,256]{1,0:T(8,128)S(1)}, u32[]{:S(2)}, u32[]{:S(2)}) collective-permute-start(f32[96,256]{1,0:T(8,128)S(1)} %pairs.1.after_ref.mine_ref), channel_id=1, source_target_pairs={{0,1},{1,0},{2,3},{3,2},{4,5},{5,4},{6,7},{7,6},{8,9},{9,8},{10,11... | collective-permute-start | bytes 294920 | tf_op jit(solution)/shard_map/ppermute | solution.py:479
  64.2 0.6 table2.1.hot_ref
  64.9 1.9 %collective-permute-start.6 = (f32[1536,256]{1,0:T(8,128)S(1)}, f32[1536,256]{1,0:T(8,128)S(1)}, u32[]{:S(2)}, u32[]{:S(2)}) collective-permute-start(f32[1536,256]{1,0:T(8,128)S(1)} %get-tuple-element.26), channel_id=1, source_target_pairs={{0,6},{4,10},{8,14},{12,18},{16,22},{20,26},{24,30},{28,34},{32,38... | collective-permute-start | bytes 4718600 | tf_op jit(solution)/shard_map/ppermute | solution.py:482
  66.8 0.6 collective-permute-done.3.other_ref
  67.4 3.7 %turn1.1 = (f32[1536,256]{1,0:T(8,128)S(1)}, f32[1536,256]{1,0:T(8,128)S(1)}, f32[16,256]{1,0:T(8,128)S(1)}) custom-call(s32[3,4]{1,0:T(4,128)S(1)} %copy-done.1, s32[1]{0:T(128)} %bitcast.p_ref, f32[96,256]{1,0:T(8,128)S(1)} %pairs.1.after_ref.mine_ref, f32[96,256]{1,0:T(8,128)S(1)} %collective-permute-done.3.other_ref, ...), custom_call_target="tpu_custom_call" | custom-call | flops 40000000000 | bytes 120000000 | tf_op jit(solution)/shard_map/turn1/pallas_call | solution.py:335
  71.1 6.4 %collective-permute-start.4 = (f32[16,256]{1,0:T(8,128)S(1)}, f32[16,256]{1,0:T(8,128)S(1)}, u32[]{:S(2)}, u32[]{:S(2)}) collective-permute-start(f32[16,256]{1,0:T(8,128)S(1)} %get-tuple-element.24.b_ref), channel_id=1, source_target_pairs={{4,0},{8,4},{12,8},{16,12},{20,16},{24,20},{28,24},{32,28},{36,32}... | collective-permute-start | bytes 49160 | tf_op jit(solution)/shard_map/ppermute | solution.py:484
  77.6 1.5 %collective-permute-done.4.coef_ref = f32[16,256]{1,0:T(8,128)S(1)} collective-permute-done((f32[16,256]{1,0:T(8,128)S(1)}, f32[16,256]{1,0:T(8,128)S(1)}, u32[]{:S(2)}, u32[]{:S(2)}) %collective-permute-start.4) | collective-permute-done | bytes 16416 | tf_op jit(solution)/shard_map/ppermute | solution.py:484
  79.1 7.7 %collective-permute-done.6.ry_ref = f32[1536,256]{1,0:T(8,128)S(1)} collective-permute-done((f32[1536,256]{1,0:T(8,128)S(1)}, f32[1536,256]{1,0:T(8,128)S(1)}, u32[]{:S(2)}, u32[]{:S(2)}) %collective-permute-start.6) | collective-permute-done | bytes 1572896 | tf_op jit(solution)/shard_map/ppermute | solution.py:482
  86.8 7.3 %side.1 = (f32[1536,256]{1,0:T(8,128)S(1)}, f32[96,256]{1,0:T(8,128)S(1)}) custom-call(s32[3,4]{1,0:T(4,128)S(1)} %copy-done.1, s32[1]{0:T(128)} %bitcast.p_ref, bf16[96,512]{1,0:T(8,128)(2,1)S(1)} %table2.1.hot_ref, f32[16,256]{1,0:T(8,128)S(1)} %collective-permute-done.4.coef_ref, f32[1536,256]{1,0:T(8,128)S(1)} %collective-permute-done.5.sx_ref, ...), custom_call_target="tpu_custom_call" | custom-call | flops 8000000000 | bytes 24000000 | tf_op jit(solution)/shard_map/side/pallas_call | solution.py:375
  94.5 9.5 %collective-permute-done.7.other_ref = f32[96,256]{1,0:T(8,128)S(1)} collective-permute-done((f32[96,256]{1,0:T(8,128)S(1)}, f32[96,256]{1,0:T(8,128)S(1)}, u32[]{:S(2)}, u32[]{:S(2)}) %collective-permute-start.7) | collective-permute-done | bytes 98336 | tf_op jit(solution)/shard_map/ppermute | solution.py:488
  104.0 1.1 solve.1.coef_ref
  105.1 3.9 %collective-permute-start.9 = (f32[16,256]{1,0:T(8,128)S(1)}, f32[16,256]{1,0:T(8,128)S(1)}, u32[]{:S(2)}, u32[]{:S(2)}) collective-permute-start(f32[16,256]{1,0:T(8,128)S(1)} %solve.1.coef_ref), channel_id=1, source_target_pairs={{0,2},{2,0},{4,6},{6,4},{8,10},{10,8},{12,14},{14,12},{16,18},{18,... | collective-permute-start | bytes 49160 | tf_op jit(solution)/shard_map/ppermute | solution.py:491
  109.0 3.2 %own.1.own_ref = f32[1536,256]{1,0:T(8,128)S(1)} custom-call(s32[3,4]{1,0:T(4,128)S(1)} %copy-done.1, s32[1]{0:T(128)} %bitcast.p_ref, f32[16,256]{1,0:T(8,128)S(1)} %solve.1.coef_ref, f32[1536,256]{1,0:T(8,128)S(1)} %get-tuple-element.27.z_ref, f32[1536,256]{1,0:T(8,128)S(1)} %get-tuple-element.30.q_ref), custom_call_target="tpu_custom_call" | custom-call | flops 4000000000 | bytes 12000000 | tf_op jit(solution)/shard_map/own/pallas_call | solution.py:409
  112.2 3.5 %collective-permute-done.8.coef_ref = f32[16,256]{1,0:T(8,128)S(1)} collective-permute-done((f32[16,256]{1,0:T(8,128)S(1)}, f32[16,256]{1,0:T(8,128)S(1)}, u32[]{:S(2)}, u32[]{:S(2)}) %collective-permute-start.8) | collective-permute-done | bytes 16416 | tf_op jit(solution)/shard_map/ppermute | solution.py:490
  115.7 4.8 %finish.1 = (f32[2,1536,256]{2,1,0:T(8,128)}, f32[3,2,256]{2,1,0:T(2,128)}) custom-call(s32[3,4]{1,0:T(4,128)S(1)} %copy-done.1, s32[1]{0:T(128)} %bitcast.p_ref, f32[16,256]{1,0:T(8,128)S(1)} %collective-permute-done.8.coef_ref, f32[16,256]{1,0:T(8,128)S(1)} %get-tuple-element.29.a_ref, f32[16,256]{1,0:T(8,128)S(1)} %get-tuple-element.24.b_ref, ...), custom_call_target="tpu_custom_call" | custom-call | flops 5000000000 | bytes 15000000 | tf_op jit(solution)/shard_map/finish/pallas_call | solution.py:444
  (12 shorter events, 0.7 us)
Async XLA Ops:
  0.6 0.7 copy-start
  1.3 20.9 %copy-start.1 = (s32[3,4]{1,0:T(4,128)S(1)}, s32[3,4]{1,0:T(4,128)}, u32[]{:S(2)}) copy-start(s32[3,4]{1,0:T(4,128)} %o_ref.17) | copy-start | bytes 148
  12.0 10.2 %collective-permute-start = (f32[96,256]{1,0:T(8,128)S(1)}, f32[96,256]{1,0:T(8,128)S(1)}, u32[]{:S(2)}, u32[]{:S(2)}) collective-permute-start(f32[96,256]{1,0:T(8,128)S(1)} %get-tuple-element.17.mine_ref.after_ref), channel_id=1, source_target_pairs={{0,1},{1,0},{2,3},{3,2},{4,5},{5,4},{6,7},{7,6},{8,9},{9,8},{10,11... | collective-permute-start | bytes 294920 | tf_op jit(solution)/shard_map/ppermute | solution.py:472
  26.0 26.5 %collective-permute-start.1 = (f32[1536,256]{1,0:T(8,128)S(1)}, f32[1536,256]{1,0:T(8,128)S(1)}, u32[]{:S(2)}, u32[]{:S(2)}) collective-permute-start(f32[1536,256]{1,0:T(8,128)S(1)} %get-tuple-element.21), channel_id=1, source_target_pairs={{2,4},{6,8},{10,12},{14,16},{18,20},{22,24},{26,28},{30,32},{34,36... | collective-permute-start | bytes 4718600 | tf_op jit(solution)/shard_map/ppermute | solution.py:475
  31.8 20.7 %collective-permute-start.2 = (f32[1536,256]{1,0:T(8,128)S(1)}, f32[1536,256]{1,0:T(8,128)S(1)}, u32[]{:S(2)}, u32[]{:S(2)}) collective-permute-start(f32[1536,256]{1,0:T(8,128)S(1)} %get-tuple-element.26), channel_id=1, source_target_pairs={{0,2},{2,0},{4,6},{6,4},{8,10},{10,8},{12,14},{14,12},{16,18},{18,... | collective-permute-start | bytes 4718600 | tf_op jit(solution)/shard_map/ppermute | solution.py:476
  57.1 10.2 %collective-permute-start.3 = (f32[96,256]{1,0:T(8,128)S(1)}, f32[96,256]{1,0:T(8,128)S(1)}, u32[]{:S(2)}, u32[]{:S(2)}) collective-permute-start(f32[96,256]{1,0:T(8,128)S(1)} %pairs.1.after_ref.mine_ref), channel_id=1, source_target_pairs={{0,1},{1,0},{2,3},{3,2},{4,5},{5,4},{6,7},{7,6},{8,9},{9,8},{10,11... | collective-permute-start | bytes 294920 | tf_op jit(solution)/shard_map/ppermute | solution.py:479
  64.2 14.8 %collective-permute-start.5 = (f32[1536,256]{1,0:T(8,128)S(1)}, f32[1536,256]{1,0:T(8,128)S(1)}, u32[]{:S(2)}, u32[]{:S(2)}) collective-permute-start(f32[1536,256]{1,0:T(8,128)S(1)} %get-tuple-element.21), channel_id=1, source_target_pairs={{0,2},{2,0},{4,6},{6,4},{8,10},{10,8},{12,14},{14,12},{16,18},{18,... | collective-permute-start | bytes 4718600 | tf_op jit(solution)/shard_map/ppermute | solution.py:477
  64.9 21.9 %collective-permute-start.6 = (f32[1536,256]{1,0:T(8,128)S(1)}, f32[1536,256]{1,0:T(8,128)S(1)}, u32[]{:S(2)}, u32[]{:S(2)}) collective-permute-start(f32[1536,256]{1,0:T(8,128)S(1)} %get-tuple-element.26), channel_id=1, source_target_pairs={{0,6},{4,10},{8,14},{12,18},{16,22},{20,26},{24,30},{28,34},{32,38... | collective-permute-start | bytes 4718600 | tf_op jit(solution)/shard_map/ppermute | solution.py:482
  71.1 7.9 %collective-permute-start.4 = (f32[16,256]{1,0:T(8,128)S(1)}, f32[16,256]{1,0:T(8,128)S(1)}, u32[]{:S(2)}, u32[]{:S(2)}) collective-permute-start(f32[16,256]{1,0:T(8,128)S(1)} %get-tuple-element.24.b_ref), channel_id=1, source_target_pairs={{4,0},{8,4},{12,8},{16,12},{20,16},{24,20},{28,24},{32,28},{36,32}... | collective-permute-start | bytes 49160 | tf_op jit(solution)/shard_map/ppermute | solution.py:484
  79.0 36.7 %collective-permute-start.10 = (f32[1536,256]{1,0:T(8,128)S(1)}, f32[1536,256]{1,0:T(8,128)S(1)}, u32[]{:S(2)}, u32[]{:S(2)}) collective-permute-start(f32[1536,256]{1,0:T(8,128)S(1)} %get-tuple-element.27.z_ref), channel_id=1, source_target_pairs={{0,4},{4,8},{8,12},{12,16},{16,20},{20,24},{24,28},{28,32},{32,36}... | collective-permute-start | bytes 4718600 | tf_op jit(solution)/shard_map/ppermute | solution.py:486
  94.1 9.9 %collective-permute-start.7 = (f32[96,256]{1,0:T(8,128)S(1)}, f32[96,256]{1,0:T(8,128)S(1)}, u32[]{:S(2)}, u32[]{:S(2)}) collective-permute-start(f32[96,256]{1,0:T(8,128)S(1)} %get-tuple-element.28.mine_ref), channel_id=1, source_target_pairs={{0,1},{1,0},{2,3},{3,2},{4,5},{5,4},{6,7},{7,6},{8,9},{9,8},{10,11... | collective-permute-start | bytes 294920 | tf_op jit(solution)/shard_map/ppermute | solution.py:488
  105.1 10.6 %collective-permute-start.8 = (f32[16,256]{1,0:T(8,128)S(1)}, f32[16,256]{1,0:T(8,128)S(1)}, u32[]{:S(2)}, u32[]{:S(2)}) collective-permute-start(f32[16,256]{1,0:T(8,128)S(1)} %solve.1.coef_ref), channel_id=1, source_target_pairs={{0,4},{4,8},{8,12},{12,16},{16,20},{20,24},{24,28},{28,32},{32,36}... | collective-permute-start | bytes 49160 | tf_op jit(solution)/shard_map/ppermute | solution.py:490
  105.1 10.6 %collective-permute-start.9 = (f32[16,256]{1,0:T(8,128)S(1)}, f32[16,256]{1,0:T(8,128)S(1)}, u32[]{:S(2)}, u32[]{:S(2)}) collective-permute-start(f32[16,256]{1,0:T(8,128)S(1)} %solve.1.coef_ref), channel_id=1, source_target_pairs={{0,2},{2,0},{4,6},{6,4},{8,10},{10,8},{12,14},{14,12},{16,18},{18,... | collective-permute-start | bytes 49160 | tf_op jit(solution)/shard_map/ppermute | solution.py:491

commit v2 on v1

--- a/solution.py
+++ b/solution.py
@@ -223,14 +223,6 @@
 def write(ref, rows, x):
     ref[rows, :H] = x[0]
     ref[rows, H:] = x[1]
-
-
-def by_tiles(rows, go):
-    r = tile_rows(rows)
-
-    @pl.loop(0, rows // r)
-    def _(i):
-        go(pl.ds(pl.multiple_of(i * r, r), r))
 
 
 def first_kernel(
@@ -308,111 +300,172 @@
     )(offsets, after)
 
 
-def turn_kernel(round_index, o_ref, p_ref, mine_ref, other_ref, a_ref, b_ref, first_ref, second_ref, coef_ref):
+def by_parts(total, go):
+    part = total // 2
+    r = tile_rows(part, 384)
+    for k in range(2):
+
+        @pl.loop(0, part // r)
+        def _(i):
+            start = pl.multiple_of(i * r, r)
+            go(pl.ds(pl.multiple_of(k * part + i * r, r), r), k, pl.ds(start, r))
+
+
+def turn_first_kernel(o_ref, p_ref, mine_ref, other_ref, a_ref, b_ref, xa, xb, ya, yb, coef_ref):
+    p = p_ref[0]
+    o = offsets_of(o_ref, 0)
+    angles(mine_ref[...] + other_ref[...], o, coef_ref)
+    coef = coef_ref[...]
+    keep = ((p & 1) == 1) | (p == 0)
+
+    def go(rows, k, rows_part):
+        upper, lower = rotate(read(a_ref, rows), read(b_ref, rows), coef, o)
+        x, y = pick_halves(keep, upper, lower)
+        write((xa, xb)[k], rows_part, x)
+        write((ya, yb)[k], rows_part, y)
+
+    by_parts(a_ref.shape[0], go)
+
+
+def turn_first(offsets, p, mine, other, a, b):
+    rows = a.shape[0]
+    part = block(rows // 2)
+    return call(
+        turn_first_kernel,
+        "turn0",
+        [SMEM, SMEM] + [VMEM] * 4,
+        (VMEM,) * 5,
+        (part, part, part, part, COEF_SHAPE),
+        us=5,
+    )(offsets, p, mine, other, a, b)
+
+
+def pairs_start_kernel(p_ref, a_ref, b_ref, gram_ref):
+    upper, lower = pick((p_ref[0] & 1) == 0, a_ref[...], b_ref[...])
+    gram_ref[...] = gram_of(upper, lower)
+
+
+def pairs_start(p, a, b):
+    return call(
+        pairs_start_kernel, "pairs0", [SMEM, VMEM, VMEM], VMEM, jax.ShapeDtypeStruct((2 * W, 2 * W), F32), us=3
+    )(p, a, b)
+
+
+def pairs_kernel(o_ref, p_ref, hot_ref, gram_ref, a_ref, b_ref, lag_ref):
+    upper, lower = pick((p_ref[0] & 1) == 0, a_ref[...], b_ref[...])
+    lag_products(gram_ref[...] + gram_of(upper, lower), offsets_of(o_ref, 1), hot_ref[...], lag_ref)
+
+
+def pairs(offsets, p, hot, gram, a, b):
+    return call(
+        pairs_kernel, "pairs1", [SMEM, SMEM] + [VMEM] * 4, VMEM, LAG_SHAPE, us=4
+    )(offsets, p, hot, gram, a, b)
+
+
+def turn_second_kernel(o_ref, p_ref, mine_ref, other_ref, rxa, rxb, sya, syb, za, zb, v_ref, coef_ref):
     p = p_ref[0]
     core = p & 1
-    o = offsets_of(o_ref, round_index)
+    o = offsets_of(o_ref, 1)
     angles(mine_ref[...] + other_ref[...], o, coef_ref)
     coef = coef_ref[...]
 
-    def go(rows):
-        upper, lower = read(a_ref, rows), read(b_ref, rows)
-        if round_index == 0:
-            keep = (core == 1) | (p == 0)
-        else:
-            upper, lower = pick_halves(core == 0, upper, lower)
-            keep = (core == 0) & (p != 0)
+    def go(rows, k, rows_part):
+        upper, lower = pick_halves(core == 0, read((rxa, rxb)[k], rows_part), read((sya, syb)[k], rows_part))
         upper, lower = rotate(upper, lower, coef, o)
-        upper, lower = pick_halves(keep, upper, lower)
-        write(first_ref, rows, upper)
-        write(second_ref, rows, lower)
-
-    by_tiles(a_ref.shape[0], go)
-
-
-def turn(round_index, offsets, p, mine, other, a, b):
-    rows = a.shape[0]
-    return call(
-        functools.partial(turn_kernel, round_index),
-        "turn%d" % round_index,
-        [SMEM, SMEM] + [VMEM] * 4,
-        (VMEM, VMEM, VMEM),
-        (block(rows), block(rows), COEF_SHAPE),
+        z, v = pick_halves((core == 0) & (p != 0), upper, lower)
+        write((za, zb)[k], rows_part, z)
+        write(v_ref, rows, v)
+
+    by_parts(v_ref.shape[0], go)
+
+
+def turn_second(offsets, p, mine, other, rxa, rxb, sya, syb):
+    rows = rxa.shape[0] * 2
+    part = block(rows // 2)
+    return call(
+        turn_second_kernel,
+        "turn1",
+        [SMEM, SMEM] + [VMEM] * 6,
+        (VMEM,) * 4,
+        (part, part, block(rows), COEF_SHAPE),
         us=40,
-    )(offsets, p, mine, other, a, b)
-
-
-def pairs_kernel(o_ref, p_ref, hot_ref, a_ref, b_ref, lag_ref):
-    upper, lower = pick((p_ref[0] & 1) == 0, a_ref[...], b_ref[...])
-    lag_products(gram_of(upper, lower), offsets_of(o_ref, 1), hot_ref[...], lag_ref)
-
-
-def pairs(offsets, p, hot, a, b):
-    return call(
-        pairs_kernel, "pairs", [SMEM, SMEM] + [VMEM] * 3, VMEM, LAG_SHAPE, us=5
-    )(offsets, p, hot, a, b)
-
-
-def side_kernel(last, o_ref, p_ref, hot_ref, coef_ref, sx_ref, ry_ref, z_ref, q_ref, lag_ref):
+    )(offsets, p, mine, other, rxa, rxb, sya, syb)
+
+
+def side_kernel(last, o_ref, p_ref, hot_ref, coef_ref, sxa, sxb, rya, ryb, za, zb, q_ref, lag_ref):
     p = p_ref[0]
     core = p & 1
     o = offsets_of(o_ref, 1)
     coef = coef_ref[...]
     near_end = (p == 1) | (p == last - 1)
-
-    def go(rows):
-        upper, lower = pick_halves((core == 0) != near_end, read(sx_ref, rows), read(ry_ref, rows))
+    part = za.shape[0]
+
+    def go(rows, k, rows_part):
+        upper, lower = pick_halves(
+            (core == 0) != near_end, read((sxa, sxb)[k], rows_part), read((rya, ryb)[k], rows_part)
+        )
         upper, lower = rotate(upper, lower, coef, o)
         wanted, _ = pick_halves((core == 1) | (p == last - 1), upper, lower)
         write(q_ref, rows, wanted)
 
-    by_tiles(sx_ref.shape[0], go)
-    upper, lower = pick(core == 0, z_ref[...], q_ref[...])
+    by_parts(q_ref.shape[0], go)
+    z = jnp.concatenate([za[...], zb[...]], axis=0)
+    upper, lower = pick(core == 0, z, q_ref[...])
     lag_products(gram_of(upper, lower), offsets_of(o_ref, 2), hot_ref[...], lag_ref)
 
 
-def side(last, offsets, p, hot, coef, sx, ry, z):
+def side(last, offsets, p, hot, coef, sxa, sxb, rya, ryb, za, zb):
     return call(
         functools.partial(side_kernel, last),
         "side",
-        [SMEM, SMEM] + [VMEM] * 5,
+        [SMEM, SMEM] + [VMEM] * 8,
         (VMEM, VMEM),
-        (block(sx.shape[0]), LAG_SHAPE),
+        (block(2 * za.shape[0]), LAG_SHAPE),
         us=8,
-    )(offsets, p, hot, coef, sx, ry, z)
-
-
-def solve_kernel(o_ref, mine_ref, other_ref, coef_ref):
-    angles(mine_ref[...] + other_ref[...], offsets_of(o_ref, 2), coef_ref)
-
-
-def solve(offsets, mine, other):
-    return call(solve_kernel, "solve", [SMEM, VMEM, VMEM], VMEM, COEF_SHAPE)(offsets, mine, other)
-
-
-def own_kernel(o_ref, p_ref, coef_ref, z_ref, q_ref, out_ref):
+    )(offsets, p, hot, coef, sxa, sxb, rya, ryb, za, zb)
+
+
+def solve_kernel(round_index, o_ref, *refs):
+    count = len(refs) // 3
+    for k in range(count):
+        angles(refs[2 * k][...] + refs[2 * k + 1][...], offsets_of(o_ref, round_index), refs[2 * count + k])
+
+
+def solve(round_index, offsets, *lags):
+    count = len(lags) // 2
+    return call(
+        functools.partial(solve_kernel, round_index),
+        "solve%d" % round_index,
+        [SMEM] + [VMEM] * len(lags),
+        (VMEM,) * count,
+        (COEF_SHAPE,) * count,
+        us=2,
+    )(offsets, *lags)
+
+
+def own_kernel(o_ref, p_ref, coef_ref, za, zb, q_ref, out_ref):
     p = p_ref[0]
     core = p & 1
     o = offsets_of(o_ref, 2)
     coef = coef_ref[...]
 
-    def go(rows):
-        upper, lower = pick_halves(core == 0, read(z_ref, rows), read(q_ref, rows))
+    def go(rows, k, rows_part):
+        upper, lower = pick_halves(core == 0, read((za, zb)[k], rows_part), read(q_ref, rows))
         upper, lower = rotate(upper, lower, coef, o)
         wanted, _ = pick_halves((core == 1) & (p != 1), upper, lower)
         write(out_ref, rows, [x * x for x in wanted])
 
-    by_tiles(z_ref.shape[0], go)
-
-
-def own(offsets, p, coef, z, q):
-    return call(own_kernel, "own", [SMEM, SMEM] + [VMEM] * 3, VMEM, block(z.shape[0]), us=4)(
-        offsets, p, coef, z, q
+    by_parts(q_ref.shape[0], go)
+
+
+def own(offsets, p, coef, za, zb, q):
+    return call(own_kernel, "own", [SMEM, SMEM] + [VMEM] * 4, VMEM, block(q.shape[0]), us=40)(
+        offsets, p, coef, za, zb, q
     )
 
 
 def finish_kernel(
-    last, row_total, o_ref, p_ref, coef_ref, a_ref, b_ref, c_ref, own_ref, r_ref, v_ref, out_hbm, norm_ref, e_ref, sem
+    last, row_total, o_ref, p_ref, coef_ref, a_ref, b_ref, c_ref, own_ref, ra, rb, v_ref, out_hbm, norm_ref, e_ref, sem
 ):
     p = p_ref[0]
     core = p & 1
@@ -422,13 +475,14 @@
     coef = coef_ref[...]
     for k, ref in enumerate((a_ref, b_ref, c_ref)):
         norm_ref[k] = ref[8:10, :] / row_total
-    total = r_ref.shape[0]
-    r = tile_rows(total)
+    part = ra.shape[0]
+    r = tile_rows(part, 384)
+    tiles = part // r
     sends = []
-    for t in range(total // r):
+    for t in range(2 * tiles):
         rows = pl.ds(t * r, r)
         swap = (p == 0) | (p == last)
-        upper, lower = pick_halves((core == 0) != swap, read(r_ref, rows), read(v_ref, rows))
+        upper, lower = pick_halves((core == 0) != swap, read((ra, rb)[t // tiles], pl.ds(t % tiles * r, r)), read(v_ref, rows))
         upper, lower = rotate(upper, lower, coef, o)
         wanted, _ = pick_halves((core == 0) | (p == last), upper, lower)
         write(e_ref, rows, [x * x for x in wanted])
@@ -439,17 +493,17 @@
         copy.wait()
 
 
-def finish(last, row_total, offsets, p, coef, coefs, own_block, r_block, v):
+def finish(last, row_total, offsets, p, coef, coefs, own_block, ra, rb, v):
     rows = v.shape[0]
     return call(
         functools.partial(finish_kernel, last, row_total),
         "finish",
-        [SMEM, SMEM] + [VMEM] * 7,
+        [SMEM, SMEM] + [VMEM] * 8,
         (ANY, VMEM),
         (jax.ShapeDtypeStruct((2, rows, W), F32), jax.ShapeDtypeStruct((3, 2, W), F32)),
         [pltpu.VMEM((rows, W), F32), pltpu.SemaphoreType.DMA((16,))],
         us=5,
-    )(offsets, p, coef, *coefs, own_block, r_block, v)
+    )(offsets, p, coef, *coefs, own_block, ra, rb, v)
 
 
 def body(row_feats, col_feats, offsets):
@@ -468,29 +522,47 @@
     tell = [(2 * j, 2 * j - 2) for j in range(1, chips)] + [(2 * j + 1, 2 * j + 3) for j in range(chips - 1)]
     tell += [(0, 1), (n - 1, n - 2)]
 
+    def exchange(lag, perm):
+        flipped = [(2 * i + r, 2 * j + 1 - r) for i, j in perm for r in (0, 1)]
+        return (
+            lax.ppermute(lag, "row", across),
+            lax.ppermute(lag, "blk", perm),
+            lax.ppermute(lag, ("blk", "row"), flipped),
+        )
+
     upper, lower, lag = first(offsets, row_feats, col_feats)
     lag_other = lax.ppermute(lag, "row", across)
-    hot = table(1, offsets, lag)
-    x, y, coef_a = turn(0, offsets, p, lag, lag_other, upper, lower)
-    rx = lax.ppermute(x, "blk", meet)
-    sy = lax.ppermute(y, "blk", sibling)
-    sx = lax.ppermute(x, "blk", sibling)
-    lag = pairs(offsets, p, hot, rx, sy)
-    lag_other = lax.ppermute(lag, "row", across)
+    xa, xb, ya, yb, coef_a = turn_first(offsets, p, lag, lag_other, upper, lower)
+    hot = table(1, offsets, coef_a)
+    rxa = lax.ppermute(xa, "blk", meet)
+    rxb = lax.ppermute(xb, "blk", meet)
+    xa, xb, ya, yb, hot = lax.optimization_barrier((xa, xb, ya, yb, hot))
+    sya = lax.ppermute(ya, "blk", sibling)
+    syb = lax.ppermute(yb, "blk", sibling)
+    sxa = lax.ppermute(xa, "blk", sibling)
+    sxb = lax.ppermute(xb, "blk", sibling)
+    gram = pairs_start(p, rxa, sya)
+    ya, gram = lax.optimization_barrier((ya, gram))
+    rya = lax.ppermute(ya, "blk", lend)
+    lag = pairs(offsets, p, hot, gram, rxb, syb)
+    lag_other, lag_told, lag_told_other = exchange(lag, tell)
     hot = table(2, offsets, lag)
-    y, hot = lax.optimization_barrier((y, hot))
-    ry = lax.ppermute(y, "blk", lend)
-    z, v, coef_b = turn(1, offsets, p, lag, lag_other, rx, sy)
-    coef_side = lax.ppermute(coef_b, "blk", tell)
-    z, coef_side = lax.optimization_barrier((z, coef_side))
-    r_block = lax.ppermute(z, "blk", deal)
-    q, lag = side(n - 1, offsets, p, hot, coef_side, sx, ry, z)
-    lag_other = lax.ppermute(lag, "row", across)
-    coef_c = solve(offsets, lag, lag_other)
-    coef_got = lax.ppermute(coef_c, "blk", deal)
+    yb, hot = lax.optimization_barrier((yb, hot))
+    ryb = lax.ppermute(yb, "blk", lend)
+    rxa, rya, sxa, sxb = lax.optimization_barrier((rxa, rya, sxa, sxb))
+    za, zb, v, coef_b = turn_second(offsets, p, lag, lag_other, rxa, rxb, sya, syb)
+    ra = lax.ppermute(za, "blk", deal)
+    lag_told, lag_told_other, coef_b = lax.optimization_barrier((lag_told, lag_told_other, coef_b))
+    (coef_side,) = solve(1, offsets, lag_told, lag_told_other)
+    q, lag = side(n - 1, offsets, p, hot, coef_side, sxa, sxb, rya, ryb, za, zb)
+    lag_other, lag_got, lag_got_other = exchange(lag, deal)
+    later, _ = lax.optimization_barrier((zb, lag))
+    rb = lax.ppermute(later, "blk", deal)
+    coef_c, coef_got = solve(2, offsets, lag, lag_other, lag_got, lag_got_other)
     coef_norm = lax.ppermute(coef_c, "blk", sibling)
-    own_block = own(offsets, p, coef_c, z, q)
-    return finish(n - 1, row_total, offsets, p, coef_got, (coef_a, coef_b, coef_norm), own_block, r_block, v)
+    coef_own, ra = lax.optimization_barrier((coef_c, ra))
+    own_block = own(offsets, p, coef_own, za, zb, q)
+    return finish(n - 1, row_total, offsets, p, coef_got, (coef_a, coef_b, coef_norm), own_block, ra, rb, v)
 
 
 def solution(mesh):

time: 121 us -> 126 us (1.041)
  the two profiles are of different devices: /device:TPU:4 before, /device:TPU:97 now
where the time goes in v2:
time: 126 us
  starting transfers between devices  61.8 us (49%)
  Pallas kernels  43.6 us (35%)
  waiting for transfers between devices  19 us (15%)
    ppermute x1, starting transfers between devices, body(): coef_norm = lax.ppermute(coef_c, 'blk', sibling)  14.4 us
    pallas_call x1, Pallas kernels, first(): call(first_kernel, 'first', [ANY, ANY, ANY], (VMEM, VMEM, VMEM), (block(r...  10.7 us
    ppermute x2, starting transfers between devices, exchange(): lax.ppermute(lag, 'row', across)  8.07 us
    pallas_call x1, Pallas kernels, side(): call(functools.partial(side_kernel, last), 'side', [SMEM, SMEM] + [VMEM]...  7.63 us
    ppermute x2, starting transfers between devices, exchange(): lax.ppermute(lag, 'blk', perm)  6.29 us
    ppermute x1, starting transfers between devices, body(): rya = lax.ppermute(ya, 'blk', lend)  5.93 us
    ppermute x2, waiting for transfers between devices, exchange(): lax.ppermute(lag, ('blk', 'row'), flipped)  5.11 us
    pallas_call x1, Pallas kernels, finish(): call(functools.partial(finish_kernel, last, row_total), 'finish', [SMEM,...  4.96 us
  transfers between devices with their start and end apart: 18, of which 8 were waited for; matrix products, arithmetic and copies ran while one was open for 0% of the time, Pallas kernels for 18%

profile of v2, /device:TPU:97, one launch (start us, length us, event | category | flops | bytes accessed | tf_op | source)
XLA Modules:
  0.0 126.0 jit_solution(3005444937911345653)
XLA Ops:
  1.3 10.7 %first.1 = (f32[1536,256]{1,0:T(8,128)S(1)}, f32[1536,256]{1,0:T(8,128)S(1)}, f32[96,256]{1,0:T(8,128)S(1)}) custom-call(s32[3,4]{1,0:T(4,128)S(1)} %copy-done, bf16[1536,2048]{1,0:T(8,128)(2,1)} %rows_hbm.1, bf16[512,2048]{1,0:T(8,128)(2,1)} %cols_hbm.1), custom_call_target="tpu_custom_call" | custom-call | flops 10000000000 | bytes 30000000 | tf_op jit(solution)/shard_map/first/pallas_call | solution.py:274
  12.0 4.3 %collective-permute-start = (f32[96,256]{1,0:T(8,128)S(1)}, f32[96,256]{1,0:T(8,128)S(1)}, u32[]{:S(2)}, u32[]{:S(2)}) collective-permute-start(f32[96,256]{1,0:T(8,128)S(1)} %get-tuple-element.37.mine_ref), channel_id=1, source_target_pairs={{0,1},{1,0},{2,3},{3,2},{4,5},{5,4},{6,7},{7,6},{8,9},{9,8},{10,11... | collective-permute-start | bytes 294920 | tf_op jit(solution)/shard_map/ppermute | solution.py:534
  16.3 3.3 %collective-permute-done.other_ref = f32[96,256]{1,0:T(8,128)S(1)} collective-permute-done((f32[96,256]{1,0:T(8,128)S(1)}, f32[96,256]{1,0:T(8,128)S(1)}, u32[]{:S(2)}, u32[]{:S(2)}) %collective-permute-start) | collective-permute-done | bytes 98336 | tf_op jit(solution)/shard_map/ppermute | solution.py:534
  19.7 4.1 %turn0.1 = (f32[768,256]{1,0:T(8,128)S(1)}, f32[768,256]{1,0:T(8,128)S(1)}, f32[768,256]{1,0:T(8,128)S(1)}, f32[768,256]{1,0:T(8,128)S(1)}, f32[16,256]{1,0:T(8,128)S(1)}) custom-call(s32[3,4]{1,0:T(4,128)S(1)} %copy-done.1, s32[1]{0:T(128)} %bitcast.p_ref, f32[96,256]{1,0:T(8,128)S(1)} %get-tuple-element.37.mine_ref, ...), custom_call_target="tpu_custom_call" | custom-call | flops 5000000000 | bytes 15000000 | tf_op jit(solution)/shard_map/turn0/pallas_call | solution.py:333
  24.4 1.8 %collective-permute-start.2 = (f32[768,256]{1,0:T(8,128)S(1)}, f32[768,256]{1,0:T(8,128)S(1)}, u32[]{:S(2)}, u32[]{:S(2)}) collective-permute-start(f32[768,256]{1,0:T(8,128)S(1)} %get-tuple-element.50), channel_id=1, source_target_pairs={{0,2},{2,0},{4,6},{6,4},{8,10},{10,8},{12,14},{14,12},{16,18},{18,... | collective-permute-start | bytes 2359304 | tf_op jit(solution)/shard_map/ppermute | solution.py:540
  26.1 3.1 %collective-permute-start.1 = (f32[768,256]{1,0:T(8,128)S(1)}, f32[768,256]{1,0:T(8,128)S(1)}, u32[]{:S(2)}, u32[]{:S(2)}) collective-permute-start(f32[768,256]{1,0:T(8,128)S(1)} %get-tuple-element.51), channel_id=1, source_target_pairs={{2,4},{6,8},{10,12},{14,16},{18,20},{22,24},{26,28},{30,32},{34,36... | collective-permute-start | bytes 2359304 | tf_op jit(solution)/shard_map/ppermute | solution.py:537
  29.2 3.7 %collective-permute-start.4 = (f32[768,256]{1,0:T(8,128)S(1)}, f32[768,256]{1,0:T(8,128)S(1)}, u32[]{:S(2)}, u32[]{:S(2)}) collective-permute-start(f32[768,256]{1,0:T(8,128)S(1)} %get-tuple-element.60), channel_id=1, source_target_pairs={{0,2},{2,0},{4,6},{6,4},{8,10},{10,8},{12,14},{14,12},{16,18},{18,... | collective-permute-start | bytes 2359304 | tf_op jit(solution)/shard_map/ppermute | solution.py:541
  32.9 1.9 %collective-permute-start.3 = (f32[768,256]{1,0:T(8,128)S(1)}, f32[768,256]{1,0:T(8,128)S(1)}, u32[]{:S(2)}, u32[]{:S(2)}) collective-permute-start(f32[768,256]{1,0:T(8,128)S(1)} %get-tuple-element.52), channel_id=1, source_target_pairs={{2,4},{6,8},{10,12},{14,16},{18,20},{22,24},{26,28},{30,32},{34,36... | collective-permute-start | bytes 2359304 | tf_op jit(solution)/shard_map/ppermute | solution.py:538
  36.1 3.7 %collective-permute-done.1.a_ref.rxa = f32[768,256]{1,0:T(8,128)S(1)} collective-permute-done((f32[768,256]{1,0:T(8,128)S(1)}, f32[768,256]{1,0:T(8,128)S(1)}, u32[]{:S(2)}, u32[]{:S(2)}) %collective-permute-start.1) | collective-permute-done | bytes 786464 | tf_op jit(solution)/shard_map/ppermute | solution.py:537
  41.2 5.9 %collective-permute-start.8 = (f32[768,256]{1,0:T(8,128)S(1)}, f32[768,256]{1,0:T(8,128)S(1)}, u32[]{:S(2)}, u32[]{:S(2)}) collective-permute-start(f32[768,256]{1,0:T(8,128)S(1)} %get-tuple-element.50), channel_id=1, source_target_pairs={{0,6},{4,10},{8,14},{12,18},{16,22},{20,26},{24,30},{28,34},{32,38... | collective-permute-start | bytes 2359304 | tf_op jit(solution)/shard_map/ppermute | solution.py:546
  48.2 3.4 %pairs1.1.after_ref.mine_ref = f32[96,256]{1,0:T(8,128)S(1)} custom-call(s32[3,4]{1,0:T(4,128)S(1)} %copy-done.1, s32[1]{0:T(128)} %bitcast.p_ref, bf16[96,512]{1,0:T(8,128)(2,1)S(1)} %table1.1.hot_ref, f32[512,512]{1,0:T(8,128)S(1)} %pairs0.1.gram_ref, f32[768,256]{1,0:T(8,128)S(1)} %collective-permute-done.3.a_ref.rxb, ...), custom_call_target="tpu_custom_call" | custom-call | flops 4000000000 | bytes 12000000 | tf_op jit(solution)/shard_map/pairs1/pallas_call | solution.py:360
  51.6 5.2 %collective-permute-start.7 = (f32[96,256]{1,0:T(8,128)S(1)}, f32[96,256]{1,0:T(8,128)S(1)}, u32[]{:S(2)}, u32[]{:S(2)}) collective-permute-start(f32[96,256]{1,0:T(8,128)S(1)} %pairs1.1.after_ref.mine_ref), channel_id=1, source_target_pairs={{0,1},{1,0},{2,3},{3,2},{4,5},{5,4},{6,7},{7,6},{8,9},{9,8},{10,11... | collective-permute-start | bytes 294920 | tf_op jit(solution)/shard_map/ppermute | solution.py:528
  56.8 3.8 %collective-permute-start.5 = (f32[96,256]{1,0:T(8,128)S(1)}, f32[96,256]{1,0:T(8,128)S(1)}, u32[]{:S(2)}, u32[]{:S(2)}) collective-permute-start(f32[96,256]{1,0:T(8,128)S(1)} %pairs1.1.after_ref.mine_ref), channel_id=1, source_target_pairs={{4,0},{8,4},{12,8},{16,12},{20,16},{24,20},{28,24},{32,28},{36,32}... | collective-permute-start | bytes 294920 | tf_op jit(solution)/shard_map/ppermute | solution.py:529
  61.3 4.4 %collective-permute-start.11 = (f32[768,256]{1,0:T(8,128)S(1)}, f32[768,256]{1,0:T(8,128)S(1)}, u32[]{:S(2)}, u32[]{:S(2)}) collective-permute-start(f32[768,256]{1,0:T(8,128)S(1)} %get-tuple-element.60), channel_id=1, source_target_pairs={{0,6},{4,10},{8,14},{12,18},{16,22},{20,26},{24,30},{28,34},{32,38... | collective-permute-start | bytes 2359304 | tf_op jit(solution)/shard_map/ppermute | solution.py:551
  65.7 3.0 %collective-permute-done.7.other_ref = f32[96,256]{1,0:T(8,128)S(1)} collective-permute-done((f32[96,256]{1,0:T(8,128)S(1)}, f32[96,256]{1,0:T(8,128)S(1)}, u32[]{:S(2)}, u32[]{:S(2)}) %collective-permute-start.7) | collective-permute-done | bytes 98336 | tf_op jit(solution)/shard_map/ppermute | solution.py:528
  68.7 4.1 %turn1.1 = (f32[768,256]{1,0:T(8,128)S(1)}, f32[768,256]{1,0:T(8,128)S(1)}, f32[1536,256]{1,0:T(8,128)S(1)}, f32[16,256]{1,0:T(8,128)S(1)}) custom-call(s32[3,4]{1,0:T(4,128)S(1)} %copy-done.1, s32[1]{0:T(128)} %bitcast.p_ref, f32[96,256]{1,0:T(8,128)S(1)} %pairs1.1.after_ref.mine_ref, f32[96,256]{1,0:T(8,128)S(1)} %collective-permute-done.7.other_ref, ...), custom_call_target="tpu_custom_call" | custom-call | flops 40000000000 | bytes 120000000 | tf_op jit(solution)/shard_map/turn1/pallas_call | solution.py:385
  73.5 3.4 %collective-permute-start.16 = (f32[768,256]{1,0:T(8,128)S(1)}, f32[768,256]{1,0:T(8,128)S(1)}, u32[]{:S(2)}, u32[]{:S(2)}) collective-permute-start(f32[768,256]{1,0:T(8,128)S(1)} %get-tuple-element.61.za), channel_id=1, source_target_pairs={{0,4},{4,8},{8,12},{12,16},{16,20},{20,24},{24,28},{28,32},{32,36}... | collective-permute-start | bytes 2359304 | tf_op jit(solution)/shard_map/ppermute | solution.py:554
  79.7 7.6 %side.1 = (f32[1536,256]{1,0:T(8,128)S(1)}, f32[96,256]{1,0:T(8,128)S(1)}) custom-call(s32[3,4]{1,0:T(4,128)S(1)} %copy-done.1, s32[1]{0:T(128)} %bitcast.p_ref, bf16[96,512]{1,0:T(8,128)(2,1)S(1)} %table2.1.hot_ref, f32[16,256]{1,0:T(8,128)S(1)} %solve1.1.coef_ref, f32[768,256]{1,0:T(8,128)S(1)} %collective-permute-done.9.sxa, ...), custom_call_target="tpu_custom_call" | custom-call | flops 8000000000 | bytes 24000000 | tf_op jit(solution)/shard_map/side/pallas_call | solution.py:418
  87.3 2.8 %collective-permute-start.12 = (f32[96,256]{1,0:T(8,128)S(1)}, f32[96,256]{1,0:T(8,128)S(1)}, u32[]{:S(2)}, u32[]{:S(2)}) collective-permute-start(f32[96,256]{1,0:T(8,128)S(1)} %get-tuple-element.63.refs_0_), channel_id=1, source_target_pairs={{0,1},{1,0},{2,3},{3,2},{4,5},{5,4},{6,7},{7,6},{8,9},{9,8},{10,11... | collective-permute-start | bytes 294920 | tf_op jit(solution)/shard_map/ppermute | solution.py:528
  90.2 2.5 %collective-permute-start.13 = (f32[96,256]{1,0:T(8,128)S(1)}, f32[96,256]{1,0:T(8,128)S(1)}, u32[]{:S(2)}, u32[]{:S(2)}) collective-permute-start(f32[96,256]{1,0:T(8,128)S(1)} %get-tuple-element.63.refs_0_), channel_id=1, source_target_pairs={{0,4},{4,8},{8,12},{12,16},{16,20},{20,24},{24,28},{28,32},{32,36}... | collective-permute-start | bytes 294920 | tf_op jit(solution)/shard_map/ppermute | solution.py:529
  97.0 4.4 %collective-permute-done.14.refs_3_ = f32[96,256]{1,0:T(8,128)S(1)} collective-permute-done((f32[96,256]{1,0:T(8,128)S(1)}, f32[96,256]{1,0:T(8,128)S(1)}, u32[]{:S(2)}, u32[]{:S(2)}) %collective-permute-start.14) | collective-permute-done | bytes 98336 | tf_op jit(solution)/shard_map/ppermute | solution.py:530
  102.8 14.4 %collective-permute-start.15 = (f32[16,256]{1,0:T(8,128)S(1)}, f32[16,256]{1,0:T(8,128)S(1)}, u32[]{:S(2)}, u32[]{:S(2)}) collective-permute-start(f32[16,256]{1,0:T(8,128)S(1)} %get-tuple-element.67.coef_ref), channel_id=1, source_target_pairs={{0,2},{2,0},{4,6},{6,4},{8,10},{10,8},{12,14},{14,12},{16,18},{18,... | collective-permute-start | bytes 49160 | tf_op jit(solution)/shard_map/ppermute | solution.py:562
  117.3 3.6 %own.1.own_ref = f32[1536,256]{1,0:T(8,128)S(1)} custom-call(s32[3,4]{1,0:T(4,128)S(1)} %copy-done.1, s32[1]{0:T(128)} %bitcast.p_ref, f32[16,256]{1,0:T(8,128)S(1)} %get-tuple-element.67.coef_ref, f32[768,256]{1,0:T(8,128)S(1)} %get-tuple-element.61.za, f32[768,256]{1,0:T(8,128)S(1)} %get-tuple-element.70.zb, f32[1536,256]{1,0:T(8,128)S(1)} %get-tuple-element.68.q_ref), custom_call_target="tpu_custom_call" | custom-call | flops 40000000000 | bytes 120000000 | tf_op jit(solution)/shard_map/own/pallas_call | solution.py:462
  120.9 5.0 %finish.1 = (f32[2,1536,256]{2,1,0:T(8,128)}, f32[3,2,256]{2,1,0:T(2,128)}) custom-call(s32[3,4]{1,0:T(4,128)S(1)} %copy-done.1, s32[1]{0:T(128)} %bitcast.p_ref, f32[16,256]{1,0:T(8,128)S(1)} %get-tuple-element.64.coef_ref, f32[16,256]{1,0:T(8,128)S(1)} %get-tuple-element.44.after_ref.a_ref, f32[16,256]{1,0:T(8,128)S(1)} %get-tuple-element.65.b_ref, ...), custom_call_target="tpu_custom_call" | custom-call | flops 5000000000 | bytes 15000000 | tf_op jit(solution)/shard_map/finish/pallas_call | solution.py:498
  (28 shorter events, 14.9 us)
Async XLA Ops:
  0.6 0.7 copy-start
  1.3 18.3 %copy-start.1 = (s32[3,4]{1,0:T(4,128)S(1)}, s32[3,4]{1,0:T(4,128)}, u32[]{:S(2)}) copy-start(s32[3,4]{1,0:T(4,128)} %o_ref.19) | copy-start | bytes 148
  12.0 7.6 %collective-permute-start = (f32[96,256]{1,0:T(8,128)S(1)}, f32[96,256]{1,0:T(8,128)S(1)}, u32[]{:S(2)}, u32[]{:S(2)}) collective-permute-start(f32[96,256]{1,0:T(8,128)S(1)} %get-tuple-element.37.mine_ref), channel_id=1, source_target_pairs={{0,1},{1,0},{2,3},{3,2},{4,5},{5,4},{6,7},{7,6},{8,9},{9,8},{10,11... | collective-permute-start | bytes 294920 | tf_op jit(solution)/shard_map/ppermute | solution.py:534
  24.4 11.4 %collective-permute-start.2 = (f32[768,256]{1,0:T(8,128)S(1)}, f32[768,256]{1,0:T(8,128)S(1)}, u32[]{:S(2)}, u32[]{:S(2)}) collective-permute-start(f32[768,256]{1,0:T(8,128)S(1)} %get-tuple-element.50), channel_id=1, source_target_pairs={{0,2},{2,0},{4,6},{6,4},{8,10},{10,8},{12,14},{14,12},{16,18},{18,... | collective-permute-start | bytes 2359304 | tf_op jit(solution)/shard_map/ppermute | solution.py:540
  26.1 13.6 %collective-permute-start.1 = (f32[768,256]{1,0:T(8,128)S(1)}, f32[768,256]{1,0:T(8,128)S(1)}, u32[]{:S(2)}, u32[]{:S(2)}) collective-permute-start(f32[768,256]{1,0:T(8,128)S(1)} %get-tuple-element.51), channel_id=1, source_target_pairs={{2,4},{6,8},{10,12},{14,16},{18,20},{22,24},{26,28},{30,32},{34,36... | collective-permute-start | bytes 2359304 | tf_op jit(solution)/shard_map/ppermute | solution.py:537
  29.2 17.9 %collective-permute-start.4 = (f32[768,256]{1,0:T(8,128)S(1)}, f32[768,256]{1,0:T(8,128)S(1)}, u32[]{:S(2)}, u32[]{:S(2)}) collective-permute-start(f32[768,256]{1,0:T(8,128)S(1)} %get-tuple-element.60), channel_id=1, source_target_pairs={{0,2},{2,0},{4,6},{6,4},{8,10},{10,8},{12,14},{14,12},{16,18},{18,... | collective-permute-start | bytes 2359304 | tf_op jit(solution)/shard_map/ppermute | solution.py:541
  32.9 15.2 %collective-permute-start.3 = (f32[768,256]{1,0:T(8,128)S(1)}, f32[768,256]{1,0:T(8,128)S(1)}, u32[]{:S(2)}, u32[]{:S(2)}) collective-permute-start(f32[768,256]{1,0:T(8,128)S(1)} %get-tuple-element.52), channel_id=1, source_target_pairs={{2,4},{6,8},{10,12},{14,16},{18,20},{22,24},{26,28},{30,32},{34,36... | collective-permute-start | bytes 2359304 | tf_op jit(solution)/shard_map/ppermute | solution.py:538
  34.8 26.4 %collective-permute-start.10 = (f32[768,256]{1,0:T(8,128)S(1)}, f32[768,256]{1,0:T(8,128)S(1)}, u32[]{:S(2)}, u32[]{:S(2)}) collective-permute-start(f32[768,256]{1,0:T(8,128)S(1)} %get-tuple-element.52), channel_id=1, source_target_pairs={{0,2},{2,0},{4,6},{6,4},{8,10},{10,8},{12,14},{14,12},{16,18},{18,... | collective-permute-start | bytes 2359304 | tf_op jit(solution)/shard_map/ppermute | solution.py:543
  35.8 25.5 %collective-permute-start.9 = (f32[768,256]{1,0:T(8,128)S(1)}, f32[768,256]{1,0:T(8,128)S(1)}, u32[]{:S(2)}, u32[]{:S(2)}) collective-permute-start(f32[768,256]{1,0:T(8,128)S(1)} %get-tuple-element.51), channel_id=1, source_target_pairs={{0,2},{2,0},{4,6},{6,4},{8,10},{10,8},{12,14},{14,12},{16,18},{18,... | collective-permute-start | bytes 2359304 | tf_op jit(solution)/shard_map/ppermute | solution.py:542
  41.2 24.6 %collective-permute-start.8 = (f32[768,256]{1,0:T(8,128)S(1)}, f32[768,256]{1,0:T(8,128)S(1)}, u32[]{:S(2)}, u32[]{:S(2)}) collective-permute-start(f32[768,256]{1,0:T(8,128)S(1)} %get-tuple-element.50), channel_id=1, source_target_pairs={{0,6},{4,10},{8,14},{12,18},{16,22},{20,26},{24,30},{28,34},{32,38... | collective-permute-start | bytes 2359304 | tf_op jit(solution)/shard_map/ppermute | solution.py:546
  51.6 17.2 %collective-permute-start.7 = (f32[96,256]{1,0:T(8,128)S(1)}, f32[96,256]{1,0:T(8,128)S(1)}, u32[]{:S(2)}, u32[]{:S(2)}) collective-permute-start(f32[96,256]{1,0:T(8,128)S(1)} %pairs1.1.after_ref.mine_ref), channel_id=1, source_target_pairs={{0,1},{1,0},{2,3},{3,2},{4,5},{5,4},{6,7},{7,6},{8,9},{9,8},{10,11... | collective-permute-start | bytes 294920 | tf_op jit(solution)/shard_map/ppermute | solution.py:528
  56.8 16.0 %collective-permute-start.5 = (f32[96,256]{1,0:T(8,128)S(1)}, f32[96,256]{1,0:T(8,128)S(1)}, u32[]{:S(2)}, u32[]{:S(2)}) collective-permute-start(f32[96,256]{1,0:T(8,128)S(1)} %pairs1.1.after_ref.mine_ref), channel_id=1, source_target_pairs={{4,0},{8,4},{12,8},{16,12},{20,16},{24,20},{28,24},{32,28},{36,32}... | collective-permute-start | bytes 294920 | tf_op jit(solution)/shard_map/ppermute | solution.py:529
  61.2 12.3 %collective-permute-start.6 = (f32[96,256]{1,0:T(8,128)S(1)}, f32[96,256]{1,0:T(8,128)S(1)}, u32[]{:S(2)}, u32[]{:S(2)}) collective-permute-start(f32[96,256]{1,0:T(8,128)S(1)} %pairs1.1.after_ref.mine_ref), channel_id=1, source_target_pairs={{4,1},{5,0},{8,5},{9,4},{12,9},{13,8},{16,13},{17,12},{20,17},{21,... | collective-permute-start | bytes 294920 | tf_op jit(solution)/shard_map/ppermute | solution.py:530
  61.3 18.4 %collective-permute-start.11 = (f32[768,256]{1,0:T(8,128)S(1)}, f32[768,256]{1,0:T(8,128)S(1)}, u32[]{:S(2)}, u32[]{:S(2)}) collective-permute-start(f32[768,256]{1,0:T(8,128)S(1)} %get-tuple-element.60), channel_id=1, source_target_pairs={{0,6},{4,10},{8,14},{12,18},{16,22},{20,26},{24,30},{28,34},{32,38... | collective-permute-start | bytes 2359304 | tf_op jit(solution)/shard_map/ppermute | solution.py:551
  73.5 43.8 %collective-permute-start.16 = (f32[768,256]{1,0:T(8,128)S(1)}, f32[768,256]{1,0:T(8,128)S(1)}, u32[]{:S(2)}, u32[]{:S(2)}) collective-permute-start(f32[768,256]{1,0:T(8,128)S(1)} %get-tuple-element.61.za), channel_id=1, source_target_pairs={{0,4},{4,8},{8,12},{12,16},{16,20},{20,24},{24,28},{28,32},{32,36}... | collective-permute-start | bytes 2359304 | tf_op jit(solution)/shard_map/ppermute | solution.py:554
  87.3 8.5 %collective-permute-start.12 = (f32[96,256]{1,0:T(8,128)S(1)}, f32[96,256]{1,0:T(8,128)S(1)}, u32[]{:S(2)}, u32[]{:S(2)}) collective-permute-start(f32[96,256]{1,0:T(8,128)S(1)} %get-tuple-element.63.refs_0_), channel_id=1, source_target_pairs={{0,1},{1,0},{2,3},{3,2},{4,5},{5,4},{6,7},{7,6},{8,9},{9,8},{10,11... | collective-permute-start | bytes 294920 | tf_op jit(solution)/shard_map/ppermute | solution.py:528
  90.2 6.9 %collective-permute-start.13 = (f32[96,256]{1,0:T(8,128)S(1)}, f32[96,256]{1,0:T(8,128)S(1)}, u32[]{:S(2)}, u32[]{:S(2)}) collective-permute-start(f32[96,256]{1,0:T(8,128)S(1)} %get-tuple-element.63.refs_0_), channel_id=1, source_target_pairs={{0,4},{4,8},{8,12},{12,16},{16,20},{20,24},{24,28},{28,32},{32,36}... | collective-permute-start | bytes 294920 | tf_op jit(solution)/shard_map/ppermute | solution.py:529
  92.7 8.8 %collective-permute-start.14 = (f32[96,256]{1,0:T(8,128)S(1)}, f32[96,256]{1,0:T(8,128)S(1)}, u32[]{:S(2)}, u32[]{:S(2)}) collective-permute-start(f32[96,256]{1,0:T(8,128)S(1)} %get-tuple-element.63.refs_0_), channel_id=1, source_target_pairs={{0,5},{1,4},{4,9},{5,8},{8,13},{9,12},{12,17},{13,16},{16,21},{17,... | collective-permute-start | bytes 294920 | tf_op jit(solution)/shard_map/ppermute | solution.py:530
  94.4 26.5 %collective-permute-start.17 = (f32[768,256]{1,0:T(8,128)S(1)}, f32[768,256]{1,0:T(8,128)S(1)}, u32[]{:S(2)}, u32[]{:S(2)}) collective-permute-start(f32[768,256]{1,0:T(8,128)S(1)} %get-tuple-element.70.zb), channel_id=1, source_target_pairs={{0,4},{4,8},{8,12},{12,16},{16,20},{20,24},{24,28},{28,32},{32,36}... | collective-permute-start | bytes 2359304 | tf_op jit(solution)/shard_map/ppermute | solution.py:560
  102.8 18.0 %collective-permute-start.15 = (f32[16,256]{1,0:T(8,128)S(1)}, f32[16,256]{1,0:T(8,128)S(1)}, u32[]{:S(2)}, u32[]{:S(2)}) collective-permute-start(f32[16,256]{1,0:T(8,128)S(1)} %get-tuple-element.67.coef_ref), channel_id=1, source_target_pairs={{0,2},{2,0},{4,6},{6,4},{8,10},{10,8},{12,14},{14,12},{16,18},{18,... | collective-permute-start | bytes 49160 | tf_op jit(solution)/shard_map/ppermute | solution.py:562

commit v3 on v1

--- a/solution.py
+++ b/solution.py
@@ -223,14 +223,6 @@
 def write(ref, rows, x):
     ref[rows, :H] = x[0]
     ref[rows, H:] = x[1]
-
-
-def by_tiles(rows, go):
-    r = tile_rows(rows)
-
-    @pl.loop(0, rows // r)
-    def _(i):
-        go(pl.ds(pl.multiple_of(i * r, r), r))
 
 
 def first_kernel(
@@ -298,59 +290,111 @@
     )(offsets, row_feats, col_feats)
 
 
-def table_kernel(round_index, o_ref, after_ref, out_ref, table_ref):
-    out_ref[...] = build_onehot(offsets_of(o_ref, round_index), table_ref)
-
-
-def table(round_index, offsets, after):
-    return call(
-        functools.partial(table_kernel, round_index), "table%d" % round_index, [SMEM, ANY], VMEM, ONEHOT_SHAPE, [TABLE]
-    )(offsets, after)
-
-
-def turn_kernel(round_index, o_ref, p_ref, mine_ref, other_ref, a_ref, b_ref, first_ref, second_ref, coef_ref):
+def tables_kernel(o_ref, after_ref, one_ref, two_ref, table_ref):
+    one_ref[...] = build_onehot(offsets_of(o_ref, 1), table_ref)
+    two_ref[...] = build_onehot(offsets_of(o_ref, 2), table_ref)
+
+
+def tables(offsets, after):
+    return call(tables_kernel, "tables", [SMEM, ANY], (VMEM, VMEM), (ONEHOT_SHAPE, ONEHOT_SHAPE), [TABLE])(
+        offsets, after
+    )
+
+
+def by_parts(total, go):
+    part = total // 2
+    r = tile_rows(part, 384)
+    for k in range(2):
+
+        @pl.loop(0, part // r)
+        def _(i):
+            start = pl.multiple_of(i * r, r)
+            go(pl.ds(pl.multiple_of(k * part + i * r, r), r), k, pl.ds(start, r))
+
+
+def turn_first_kernel(o_ref, p_ref, mine_ref, other_ref, a_ref, b_ref, xa, xb, x_ref, y_ref, coef_ref):
+    p = p_ref[0]
+    o = offsets_of(o_ref, 0)
+    angles(mine_ref[...] + other_ref[...], o, coef_ref)
+    coef = coef_ref[...]
+    keep = ((p & 1) == 1) | (p == 0)
+
+    def go(rows, k, rows_part):
+        upper, lower = rotate(read(a_ref, rows), read(b_ref, rows), coef, o)
+        x, y = pick_halves(keep, upper, lower)
+        write((xa, xb)[k], rows_part, x)
+        write(x_ref, rows, x)
+        write(y_ref, rows, y)
+
+    by_parts(a_ref.shape[0], go)
+
+
+def turn_first(offsets, p, mine, other, a, b):
+    rows = a.shape[0]
+    part = block(rows // 2)
+    return call(
+        turn_first_kernel,
+        "turn0",
+        [SMEM, SMEM] + [VMEM] * 4,
+        (VMEM,) * 5,
+        (part, part, block(rows), block(rows), COEF_SHAPE),
+        us=5,
+    )(offsets, p, mine, other, a, b)
+
+
+def pairs_start_kernel(p_ref, a_ref, b_ref, gram_ref):
+    part = a_ref.shape[0]
+    upper, lower = pick((p_ref[0] & 1) == 0, a_ref[...], b_ref[:part])
+    gram_ref[...] = gram_of(upper, lower)
+
+
+def pairs_start(p, a, b):
+    return call(
+        pairs_start_kernel, "pairs0", [SMEM, VMEM, VMEM], VMEM, jax.ShapeDtypeStruct((2 * W, 2 * W), F32), us=3
+    )(p, a, b)
+
+
+def pairs_kernel(o_ref, p_ref, hot_ref, gram_ref, a_ref, b_ref, lag_ref):
+    part = a_ref.shape[0]
+    upper, lower = pick((p_ref[0] & 1) == 0, a_ref[...], b_ref[part:])
+    lag_products(gram_ref[...] + gram_of(upper, lower), offsets_of(o_ref, 1), hot_ref[...], lag_ref)
+
+
+def pairs(offsets, p, hot, gram, a, b):
+    return call(
+        pairs_kernel, "pairs1", [SMEM, SMEM] + [VMEM] * 4, VMEM, LAG_SHAPE, us=20
+    )(offsets, p, hot, gram, a, b)
+
+
+def turn_second_kernel(o_ref, p_ref, coef_ref, rxa, rxb, sy_ref, z_ref, v_ref):
     p = p_ref[0]
     core = p & 1
-    o = offsets_of(o_ref, round_index)
-    angles(mine_ref[...] + other_ref[...], o, coef_ref)
+    o = offsets_of(o_ref, 1)
     coef = coef_ref[...]
 
-    def go(rows):
-        upper, lower = read(a_ref, rows), read(b_ref, rows)
-        if round_index == 0:
-            keep = (core == 1) | (p == 0)
-        else:
-            upper, lower = pick_halves(core == 0, upper, lower)
-            keep = (core == 0) & (p != 0)
+    def go(rows, k, rows_part):
+        upper, lower = pick_halves(core == 0, read((rxa, rxb)[k], rows_part), read(sy_ref, rows))
         upper, lower = rotate(upper, lower, coef, o)
-        upper, lower = pick_halves(keep, upper, lower)
-        write(first_ref, rows, upper)
-        write(second_ref, rows, lower)
-
-    by_tiles(a_ref.shape[0], go)
-
-
-def turn(round_index, offsets, p, mine, other, a, b):
-    rows = a.shape[0]
-    return call(
-        functools.partial(turn_kernel, round_index),
-        "turn%d" % round_index,
-        [SMEM, SMEM] + [VMEM] * 4,
-        (VMEM, VMEM, VMEM),
-        (block(rows), block(rows), COEF_SHAPE),
-        us=40,
-    )(offsets, p, mine, other, a, b)
-
-
-def pairs_kernel(o_ref, p_ref, hot_ref, a_ref, b_ref, lag_ref):
-    upper, lower = pick((p_ref[0] & 1) == 0, a_ref[...], b_ref[...])
-    lag_products(gram_of(upper, lower), offsets_of(o_ref, 1), hot_ref[...], lag_ref)
-
-
-def pairs(offsets, p, hot, a, b):
-    return call(
-        pairs_kernel, "pairs", [SMEM, SMEM] + [VMEM] * 3, VMEM, LAG_SHAPE, us=5
-    )(offsets, p, hot, a, b)
+        z, v = pick_halves((core == 0) & (p != 0), upper, lower)
+        write(z_ref, rows, z)
+        write(v_ref, rows, v)
+
+    by_parts(v_ref.shape[0], go)
+
+
+def turn_second(offsets, p, coef, rxa, rxb, sy):
+    whole = block(sy.shape[0])
+    return call(
+        turn_second_kernel, "turn1", [SMEM, SMEM] + [VMEM] * 4, (VMEM, VMEM), (whole, whole), us=8
+    )(offsets, p, coef, rxa, rxb, sy)
+
+
+def by_tiles(rows, go):
+    r = tile_rows(rows)
+
+    @pl.loop(0, rows // r)
+    def _(i):
+        go(pl.ds(pl.multiple_of(i * r, r), r))
 
 
 def side_kernel(last, o_ref, p_ref, hot_ref, coef_ref, sx_ref, ry_ref, z_ref, q_ref, lag_ref):
@@ -377,17 +421,27 @@
         "side",
         [SMEM, SMEM] + [VMEM] * 5,
         (VMEM, VMEM),
-        (block(sx.shape[0]), LAG_SHAPE),
+        (block(z.shape[0]), LAG_SHAPE),
         us=8,
     )(offsets, p, hot, coef, sx, ry, z)
 
 
-def solve_kernel(o_ref, mine_ref, other_ref, coef_ref):
-    angles(mine_ref[...] + other_ref[...], offsets_of(o_ref, 2), coef_ref)
-
-
-def solve(offsets, mine, other):
-    return call(solve_kernel, "solve", [SMEM, VMEM, VMEM], VMEM, COEF_SHAPE)(offsets, mine, other)
+def solve_kernel(round_index, o_ref, *refs):
+    count = len(refs) // 3
+    for k in range(count):
+        angles(refs[2 * k][...] + refs[2 * k + 1][...], offsets_of(o_ref, round_index), refs[2 * count + k])
+
+
+def solve(round_index, offsets, *lags):
+    count = len(lags) // 2
+    return call(
+        functools.partial(solve_kernel, round_index),
+        "solve%d" % round_index,
+        [SMEM] + [VMEM] * len(lags),
+        (VMEM,) * count,
+        (COEF_SHAPE,) * count,
+        us=2,
+    )(offsets, *lags)
 
 
 def own_kernel(o_ref, p_ref, coef_ref, z_ref, q_ref, out_ref):
@@ -406,7 +460,7 @@
 
 
 def own(offsets, p, coef, z, q):
-    return call(own_kernel, "own", [SMEM, SMEM] + [VMEM] * 3, VMEM, block(z.shape[0]), us=4)(
+    return call(own_kernel, "own", [SMEM, SMEM] + [VMEM] * 3, VMEM, block(z.shape[0]), us=5)(
         offsets, p, coef, z, q
     )
 
@@ -470,23 +524,25 @@
 
     upper, lower, lag = first(offsets, row_feats, col_feats)
     lag_other = lax.ppermute(lag, "row", across)
-    hot = table(1, offsets, lag)
-    x, y, coef_a = turn(0, offsets, p, lag, lag_other, upper, lower)
-    rx = lax.ppermute(x, "blk", meet)
+    xa, xb, x, y, coef_a = turn_first(offsets, p, lag, lag_other, upper, lower)
+    rxa = lax.ppermute(xa, "blk", meet)
+    rxb = lax.ppermute(xb, "blk", meet)
     sy = lax.ppermute(y, "blk", sibling)
     sx = lax.ppermute(x, "blk", sibling)
-    lag = pairs(offsets, p, hot, rx, sy)
+    hot, hot_later = tables(offsets, coef_a)
+    gram = pairs_start(p, rxa, sy)
+    y, gram = lax.optimization_barrier((y, gram))
+    ry = lax.ppermute(y, "blk", lend)
+    lag = pairs(offsets, p, hot, gram, rxb, sy)
     lag_other = lax.ppermute(lag, "row", across)
-    hot = table(2, offsets, lag)
-    y, hot = lax.optimization_barrier((y, hot))
-    ry = lax.ppermute(y, "blk", lend)
-    z, v, coef_b = turn(1, offsets, p, lag, lag_other, rx, sy)
+    (coef_b,) = solve(1, offsets, lag, lag_other)
     coef_side = lax.ppermute(coef_b, "blk", tell)
+    z, v = turn_second(offsets, p, coef_b, rxa, rxb, sy)
     z, coef_side = lax.optimization_barrier((z, coef_side))
     r_block = lax.ppermute(z, "blk", deal)
-    q, lag = side(n - 1, offsets, p, hot, coef_side, sx, ry, z)
+    q, lag = side(n - 1, offsets, p, hot_later, coef_side, sx, ry, z)
     lag_other = lax.ppermute(lag, "row", across)
-    coef_c = solve(offsets, lag, lag_other)
+    (coef_c,) = solve(2, offsets, lag, lag_other)
     coef_got = lax.ppermute(coef_c, "blk", deal)
     coef_norm = lax.ppermute(coef_c, "blk", sibling)
     own_block = own(offsets, p, coef_c, z, q)

time: 121 us -> 123 us (1.017)
  starting transfers between devices: 33.1 us -> 44.9 us
  waiting for transfers between devices: 45.5 us -> 34.7 us
    ppermute x1, waiting for transfers between devices: 7.72 us -> 0.01 us  [body(): ry = lax.ppermute(y, 'blk', lend)]
    ppermute x1 -> x2, waiting for transfers between devices: 19.8 us -> 13.3 us  [the longest x1 6.72 us: body(): rxa = lax.ppermute(xa, 'blk', meet)]
    ppermute x1, starting transfers between devices: 6.44 us -> 12.8 us  [body(): coef_side = lax.ppermute(coef_b, 'blk', tell)]
    ppermute x1 -> x2, starting transfers between devices: 5.83 us -> 10.4 us  [the longest x1 7.48 us: body(): rxa = lax.ppermute(xa, 'blk', meet)]
    ppermute x3, waiting for transfers between devices: 13 us -> 16.4 us  [body(): lag_other = lax.ppermute(lag, 'row', across)]
    ppermute x1, waiting for transfers between devices: 1.49 us -> 0.01 us  [body(): coef_side = lax.ppermute(coef_b, 'blk', tell)]
    ppermute x1, waiting for transfers between devices: 3.53 us -> 4.94 us  [body(): coef_got = lax.ppermute(coef_c, 'blk', deal)]
    ppermute x1, starting transfers between devices: 3.85 us -> 5.17 us  [body(): coef_norm = lax.ppermute(coef_c, 'blk', sibling)]
  transfers between devices with their start and end apart: 11 -> 12, of which waited for: 7 -> 6; matrix products, arithmetic and copies ran while one was open for 0% -> 0% of each run, Pallas kernels for 14% -> 18%
where the time goes in v3:
time: 123 us
  starting transfers between devices  44.9 us (37%)
  Pallas kernels  41.5 us (34%)
  waiting for transfers between devices  34.7 us (28%)
    ppermute x3, waiting for transfers between devices, body(): lag_other = lax.ppermute(lag, 'row', across)  16.4 us
    ppermute x3, starting transfers between devices, body(): lag_other = lax.ppermute(lag, 'row', across)  14.2 us
    ppermute x1, starting transfers between devices, body(): coef_side = lax.ppermute(coef_b, 'blk', tell)  12.8 us
    pallas_call x1, Pallas kernels, first(): call(first_kernel, 'first', [ANY, ANY, ANY], (VMEM, VMEM, VMEM), (block(r...  10.7 us
    ppermute x1, starting transfers between devices, body(): rxa = lax.ppermute(xa, 'blk', meet)  7.48 us
    pallas_call x1, Pallas kernels, side(): call(functools.partial(side_kernel, last), 'side', [SMEM, SMEM] + [VMEM]...  7.29 us
    ppermute x1, waiting for transfers between devices, body(): rxa = lax.ppermute(xa, 'blk', meet)  6.72 us
    ppermute x1, waiting for transfers between devices, body(): rxb = lax.ppermute(xb, 'blk', meet)  6.58 us
  transfers between devices with their start and end apart: 12, of which 6 were waited for; matrix products, arithmetic and copies ran while one was open for 0% of the time, Pallas kernels for 18%

profile of v3, /device:TPU:4, one launch (start us, length us, event | category | flops | bytes accessed | tf_op | source)
XLA Modules:
  0.0 122.7 jit_solution(12114080830622760450)
XLA Ops:
  1.3 10.7 %first.1 = (f32[1536,256]{1,0:T(8,128)S(1)}, f32[1536,256]{1,0:T(8,128)S(1)}, f32[96,256]{1,0:T(8,128)S(1)}) custom-call(s32[3,4]{1,0:T(4,128)S(1)} %copy-done, bf16[1536,2048]{1,0:T(8,128)(2,1)} %rows_hbm.1, bf16[512,2048]{1,0:T(8,128)(2,1)} %cols_hbm.1), custom_call_target="tpu_custom_call" | custom-call | flops 10000000000 | bytes 30000000 | tf_op jit(solution)/shard_map/first/pallas_call | solution.py:274
  12.0 7.3 %collective-permute-start = (f32[96,256]{1,0:T(8,128)S(1)}, f32[96,256]{1,0:T(8,128)S(1)}, u32[]{:S(2)}, u32[]{:S(2)}) collective-permute-start(f32[96,256]{1,0:T(8,128)S(1)} %get-tuple-element.20.mine_ref), channel_id=1, source_target_pairs={{0,1},{1,0},{2,3},{3,2},{4,5},{5,4},{6,7},{7,6},{8,9},{9,8},{10,11... | collective-permute-start | bytes 294920 | tf_op jit(solution)/shard_map/ppermute | solution.py:526
  19.3 2.9 %collective-permute-done.other_ref = f32[96,256]{1,0:T(8,128)S(1)} collective-permute-done((f32[96,256]{1,0:T(8,128)S(1)}, f32[96,256]{1,0:T(8,128)S(1)}, u32[]{:S(2)}, u32[]{:S(2)}) %collective-permute-start) | collective-permute-done | bytes 98336 | tf_op jit(solution)/shard_map/ppermute | solution.py:526
  22.2 4.2 %turn0.1 = (f32[768,256]{1,0:T(8,128)S(1)}, f32[768,256]{1,0:T(8,128)S(1)}, f32[1536,256]{1,0:T(8,128)S(1)}, f32[1536,256]{1,0:T(8,128)S(1)}, f32[16,256]{1,0:T(8,128)S(1)}) custom-call(s32[3,4]{1,0:T(4,128)S(1)} %copy-done.1, s32[1]{0:T(128)} %bitcast.p_ref, f32[96,256]{1,0:T(8,128)S(1)} %get-tuple-element.20.mine_ref, ...), custom_call_target="tpu_custom_call" | custom-call | flops 5000000000 | bytes 15000000 | tf_op jit(solution)/shard_map/turn0/pallas_call | solution.py:335
  26.5 7.5 %collective-permute-start.1 = (f32[768,256]{1,0:T(8,128)S(1)}, f32[768,256]{1,0:T(8,128)S(1)}, u32[]{:S(2)}, u32[]{:S(2)}) collective-permute-start(f32[768,256]{1,0:T(8,128)S(1)} %get-tuple-element.27), channel_id=1, source_target_pairs={{2,4},{6,8},{10,12},{14,16},{18,20},{22,24},{26,28},{30,32},{34,36... | collective-permute-start | bytes 2359304 | tf_op jit(solution)/shard_map/ppermute | solution.py:528
  34.0 2.9 %collective-permute-start.3 = (f32[768,256]{1,0:T(8,128)S(1)}, f32[768,256]{1,0:T(8,128)S(1)}, u32[]{:S(2)}, u32[]{:S(2)}) collective-permute-start(f32[768,256]{1,0:T(8,128)S(1)} %get-tuple-element.29), channel_id=1, source_target_pairs={{2,4},{6,8},{10,12},{14,16},{18,20},{22,24},{26,28},{30,32},{34,36... | collective-permute-start | bytes 2359304 | tf_op jit(solution)/shard_map/ppermute | solution.py:529
  37.1 0.7 tables.1
  37.9 6.7 %collective-permute-done.1.a_ref.rxa = f32[768,256]{1,0:T(8,128)S(1)} collective-permute-done((f32[768,256]{1,0:T(8,128)S(1)}, f32[768,256]{1,0:T(8,128)S(1)}, u32[]{:S(2)}, u32[]{:S(2)}) %collective-permute-start.1) | collective-permute-done | bytes 786464 | tf_op jit(solution)/shard_map/ppermute | solution.py:528
  44.6 1.5 %pairs0.1.gram_ref = f32[512,512]{1,0:T(8,128)S(1)} custom-call(s32[1]{0:T(128)} %bitcast.p_ref, f32[768,256]{1,0:T(8,128)S(1)} %collective-permute-done.1.a_ref.rxa, f32[1536,256]{1,0:T(8,128)S(1)} %collective-permute-done.2.b_ref.sy_ref), custom_call_target="tpu_custom_call" | custom-call | flops 3000000000 | bytes 9000000 | tf_op jit(solution)/shard_map/pairs0/pallas_call | solution.py:352
  46.1 1.9 %collective-permute-start.7 = (f32[1536,256]{1,0:T(8,128)S(1)}, f32[1536,256]{1,0:T(8,128)S(1)}, u32[]{:S(2)}, u32[]{:S(2)}) collective-permute-start(f32[1536,256]{1,0:T(8,128)S(1)} %get-tuple-element.33), channel_id=1, source_target_pairs={{0,6},{4,10},{8,14},{12,18},{16,22},{20,26},{24,30},{28,34},{32,38... | collective-permute-start | bytes 4718600 | tf_op jit(solution)/shard_map/ppermute | solution.py:535
  48.0 6.6 %collective-permute-done.3.a_ref.rxb = f32[768,256]{1,0:T(8,128)S(1)} collective-permute-done((f32[768,256]{1,0:T(8,128)S(1)}, f32[768,256]{1,0:T(8,128)S(1)}, u32[]{:S(2)}, u32[]{:S(2)}) %collective-permute-start.3) | collective-permute-done | bytes 786464 | tf_op jit(solution)/shard_map/ppermute | solution.py:529
  54.6 3.4 %pairs1.1.refs_0_ = f32[96,256]{1,0:T(8,128)S(1)} custom-call(s32[3,4]{1,0:T(4,128)S(1)} %copy-done.1, s32[1]{0:T(128)} %bitcast.p_ref, bf16[96,512]{1,0:T(8,128)(2,1)S(1)} %get-tuple-element.25.hot_ref, f32[512,512]{1,0:T(8,128)S(1)} %pairs0.1.gram_ref, f32[768,256]{1,0:T(8,128)S(1)} %collective-permute-done.3.a_ref.rxb, ...), custom_call_target="tpu_custom_call" | custom-call | flops 20000000000 | bytes 60000000 | tf_op jit(solution)/shard_map/pairs1/pallas_call | solution.py:364
  58.0 6.6 %collective-permute-start.4 = (f32[96,256]{1,0:T(8,128)S(1)}, f32[96,256]{1,0:T(8,128)S(1)}, u32[]{:S(2)}, u32[]{:S(2)}) collective-permute-start(f32[96,256]{1,0:T(8,128)S(1)} %pairs1.1.refs_0_), channel_id=1, source_target_pairs={{0,1},{1,0},{2,3},{3,2},{4,5},{5,4},{6,7},{7,6},{8,9},{9,8},{10,11... | collective-permute-start | bytes 294920 | tf_op jit(solution)/shard_map/ppermute | solution.py:537
  64.6 3.8 %collective-permute-done.4.refs_1_ = f32[96,256]{1,0:T(8,128)S(1)} collective-permute-done((f32[96,256]{1,0:T(8,128)S(1)}, f32[96,256]{1,0:T(8,128)S(1)}, u32[]{:S(2)}, u32[]{:S(2)}) %collective-permute-start.4) | collective-permute-done | bytes 98336 | tf_op jit(solution)/shard_map/ppermute | solution.py:537
  68.4 1.1 solve1.1.coef_ref.b_ref
  69.5 12.8 %collective-permute-start.5 = (f32[16,256]{1,0:T(8,128)S(1)}, f32[16,256]{1,0:T(8,128)S(1)}, u32[]{:S(2)}, u32[]{:S(2)}) collective-permute-start(f32[16,256]{1,0:T(8,128)S(1)} %solve1.1.coef_ref.b_ref), channel_id=1, source_target_pairs={{4,0},{8,4},{12,8},{16,12},{20,16},{24,20},{28,24},{32,28},{36,32}... | collective-permute-start | bytes 49160 | tf_op jit(solution)/shard_map/ppermute | solution.py:539
  82.2 3.6 %turn1.1 = (f32[1536,256]{1,0:T(8,128)S(1)}, f32[1536,256]{1,0:T(8,128)S(1)}) custom-call(s32[3,4]{1,0:T(4,128)S(1)} %copy-done.1, s32[1]{0:T(128)} %bitcast.p_ref, f32[16,256]{1,0:T(8,128)S(1)} %solve1.1.coef_ref.b_ref, f32[768,256]{1,0:T(8,128)S(1)} %collective-permute-done.1.a_ref.rxa, f32[768,256]{1,0:T(8,128)S(1)} %collective-permute-done.3.a_ref.rxb, ...), custom_call_target="tpu_custom_call" | custom-call | flops 8000000000 | bytes 24000000 | tf_op jit(solution)/shard_map/turn1/pallas_call | solution.py:387
  85.9 7.3 %side.1 = (f32[1536,256]{1,0:T(8,128)S(1)}, f32[96,256]{1,0:T(8,128)S(1)}) custom-call(s32[3,4]{1,0:T(4,128)S(1)} %copy-done.1, s32[1]{0:T(128)} %bitcast.p_ref, bf16[96,512]{1,0:T(8,128)(2,1)S(1)} %get-tuple-element.24.hot_ref, f32[16,256]{1,0:T(8,128)S(1)} %collective-permute-done.5.coef_ref, f32[1536,256]{1,0:T(8,128)S(1)} %collective-permute-done.6.sx_ref, ...), custom_call_target="tpu_custom_call" | custom-call | flops 8000000000 | bytes 24000000 | tf_op jit(solution)/shard_map/side/pallas_call | solution.py:419
  93.6 9.7 %collective-permute-done.8.refs_1_ = f32[96,256]{1,0:T(8,128)S(1)} collective-permute-done((f32[96,256]{1,0:T(8,128)S(1)}, f32[96,256]{1,0:T(8,128)S(1)}, u32[]{:S(2)}, u32[]{:S(2)}) %collective-permute-start.8) | collective-permute-done | bytes 98336 | tf_op jit(solution)/shard_map/ppermute | solution.py:544
  103.3 1.1 solve2.1.coef_ref
  104.4 5.2 %collective-permute-start.10 = (f32[16,256]{1,0:T(8,128)S(1)}, f32[16,256]{1,0:T(8,128)S(1)}, u32[]{:S(2)}, u32[]{:S(2)}) collective-permute-start(f32[16,256]{1,0:T(8,128)S(1)} %solve2.1.coef_ref), channel_id=1, source_target_pairs={{0,2},{2,0},{4,6},{6,4},{8,10},{10,8},{12,14},{14,12},{16,18},{18,... | collective-permute-start | bytes 49160 | tf_op jit(solution)/shard_map/ppermute | solution.py:547
  109.6 3.2 %own.1.own_ref = f32[1536,256]{1,0:T(8,128)S(1)} custom-call(s32[3,4]{1,0:T(4,128)S(1)} %copy-done.1, s32[1]{0:T(128)} %bitcast.p_ref, f32[16,256]{1,0:T(8,128)S(1)} %solve2.1.coef_ref, f32[1536,256]{1,0:T(8,128)S(1)} %get-tuple-element.34.z_ref, f32[1536,256]{1,0:T(8,128)S(1)} %get-tuple-element.36.q_ref), custom_call_target="tpu_custom_call" | custom-call | flops 5000000000 | bytes 15000000 | tf_op jit(solution)/shard_map/own/pallas_call | solution.py:463
  112.8 4.9 %collective-permute-done.9.coef_ref = f32[16,256]{1,0:T(8,128)S(1)} collective-permute-done((f32[16,256]{1,0:T(8,128)S(1)}, f32[16,256]{1,0:T(8,128)S(1)}, u32[]{:S(2)}, u32[]{:S(2)}) %collective-permute-start.9) | collective-permute-done | bytes 16416 | tf_op jit(solution)/shard_map/ppermute | solution.py:546
  117.7 4.8 %finish.1 = (f32[2,1536,256]{2,1,0:T(8,128)}, f32[3,2,256]{2,1,0:T(2,128)}) custom-call(s32[3,4]{1,0:T(4,128)S(1)} %copy-done.1, s32[1]{0:T(128)} %bitcast.p_ref, f32[16,256]{1,0:T(8,128)S(1)} %collective-permute-done.9.coef_ref, f32[16,256]{1,0:T(8,128)S(1)} %get-tuple-element.23.after_ref.a_ref, f32[16,256]{1,0:T(8,128)S(1)} %solve1.1.coef_ref.b_ref, ...), custom_call_target="tpu_custom_call" | custom-call | flops 5000000000 | bytes 15000000 | tf_op jit(solution)/shard_map/finish/pallas_call | solution.py:498
  (15 shorter events, 1.5 us)
Async XLA Ops:
  0.6 0.7 copy-start
  1.3 20.9 %copy-start.1 = (s32[3,4]{1,0:T(4,128)S(1)}, s32[3,4]{1,0:T(4,128)}, u32[]{:S(2)}) copy-start(s32[3,4]{1,0:T(4,128)} %o_ref.17) | copy-start | bytes 148
  12.0 10.2 %collective-permute-start = (f32[96,256]{1,0:T(8,128)S(1)}, f32[96,256]{1,0:T(8,128)S(1)}, u32[]{:S(2)}, u32[]{:S(2)}) collective-permute-start(f32[96,256]{1,0:T(8,128)S(1)} %get-tuple-element.20.mine_ref), channel_id=1, source_target_pairs={{0,1},{1,0},{2,3},{3,2},{4,5},{5,4},{6,7},{7,6},{8,9},{9,8},{10,11... | collective-permute-start | bytes 294920 | tf_op jit(solution)/shard_map/ppermute | solution.py:526
  26.4 18.2 %collective-permute-start.2 = (f32[1536,256]{1,0:T(8,128)S(1)}, f32[1536,256]{1,0:T(8,128)S(1)}, u32[]{:S(2)}, u32[]{:S(2)}) collective-permute-start(f32[1536,256]{1,0:T(8,128)S(1)} %get-tuple-element.33), channel_id=1, source_target_pairs={{0,2},{2,0},{4,6},{6,4},{8,10},{10,8},{12,14},{14,12},{16,18},{18,... | collective-permute-start | bytes 4718600 | tf_op jit(solution)/shard_map/ppermute | solution.py:530
  26.5 18.1 %collective-permute-start.1 = (f32[768,256]{1,0:T(8,128)S(1)}, f32[768,256]{1,0:T(8,128)S(1)}, u32[]{:S(2)}, u32[]{:S(2)}) collective-permute-start(f32[768,256]{1,0:T(8,128)S(1)} %get-tuple-element.27), channel_id=1, source_target_pairs={{2,4},{6,8},{10,12},{14,16},{18,20},{22,24},{26,28},{30,32},{34,36... | collective-permute-start | bytes 2359304 | tf_op jit(solution)/shard_map/ppermute | solution.py:528
  34.0 20.6 %collective-permute-start.3 = (f32[768,256]{1,0:T(8,128)S(1)}, f32[768,256]{1,0:T(8,128)S(1)}, u32[]{:S(2)}, u32[]{:S(2)}) collective-permute-start(f32[768,256]{1,0:T(8,128)S(1)} %get-tuple-element.29), channel_id=1, source_target_pairs={{2,4},{6,8},{10,12},{14,16},{18,20},{22,24},{26,28},{30,32},{34,36... | collective-permute-start | bytes 2359304 | tf_op jit(solution)/shard_map/ppermute | solution.py:529
  36.9 49.1 %collective-permute-start.6 = (f32[1536,256]{1,0:T(8,128)S(1)}, f32[1536,256]{1,0:T(8,128)S(1)}, u32[]{:S(2)}, u32[]{:S(2)}) collective-permute-start(f32[1536,256]{1,0:T(8,128)S(1)} %get-tuple-element.32), channel_id=1, source_target_pairs={{0,2},{2,0},{4,6},{6,4},{8,10},{10,8},{12,14},{14,12},{16,18},{18,... | collective-permute-start | bytes 4718600 | tf_op jit(solution)/shard_map/ppermute | solution.py:531
  46.1 39.9 %collective-permute-start.7 = (f32[1536,256]{1,0:T(8,128)S(1)}, f32[1536,256]{1,0:T(8,128)S(1)}, u32[]{:S(2)}, u32[]{:S(2)}) collective-permute-start(f32[1536,256]{1,0:T(8,128)S(1)} %get-tuple-element.33), channel_id=1, source_target_pairs={{0,6},{4,10},{8,14},{12,18},{16,22},{20,26},{24,30},{28,34},{32,38... | collective-permute-start | bytes 4718600 | tf_op jit(solution)/shard_map/ppermute | solution.py:535
  58.0 10.4 %collective-permute-start.4 = (f32[96,256]{1,0:T(8,128)S(1)}, f32[96,256]{1,0:T(8,128)S(1)}, u32[]{:S(2)}, u32[]{:S(2)}) collective-permute-start(f32[96,256]{1,0:T(8,128)S(1)} %pairs1.1.refs_0_), channel_id=1, source_target_pairs={{0,1},{1,0},{2,3},{3,2},{4,5},{5,4},{6,7},{7,6},{8,9},{9,8},{10,11... | collective-permute-start | bytes 294920 | tf_op jit(solution)/shard_map/ppermute | solution.py:537
  69.5 16.3 %collective-permute-start.5 = (f32[16,256]{1,0:T(8,128)S(1)}, f32[16,256]{1,0:T(8,128)S(1)}, u32[]{:S(2)}, u32[]{:S(2)}) collective-permute-start(f32[16,256]{1,0:T(8,128)S(1)} %solve1.1.coef_ref.b_ref), channel_id=1, source_target_pairs={{4,0},{8,4},{12,8},{16,12},{20,16},{24,20},{28,24},{32,28},{36,32}... | collective-permute-start | bytes 49160 | tf_op jit(solution)/shard_map/ppermute | solution.py:539
  85.8 31.9 %collective-permute-start.11 = (f32[1536,256]{1,0:T(8,128)S(1)}, f32[1536,256]{1,0:T(8,128)S(1)}, u32[]{:S(2)}, u32[]{:S(2)}) collective-permute-start(f32[1536,256]{1,0:T(8,128)S(1)} %get-tuple-element.34.z_ref), channel_id=1, source_target_pairs={{0,4},{4,8},{8,12},{12,16},{16,20},{20,24},{24,28},{28,32},{32,36}... | collective-permute-start | bytes 4718600 | tf_op jit(solution)/shard_map/ppermute | solution.py:542
  93.2 10.0 %collective-permute-start.8 = (f32[96,256]{1,0:T(8,128)S(1)}, f32[96,256]{1,0:T(8,128)S(1)}, u32[]{:S(2)}, u32[]{:S(2)}) collective-permute-start(f32[96,256]{1,0:T(8,128)S(1)} %get-tuple-element.35.refs_0_), channel_id=1, source_target_pairs={{0,1},{1,0},{2,3},{3,2},{4,5},{5,4},{6,7},{7,6},{8,9},{9,8},{10,11... | collective-permute-start | bytes 294920 | tf_op jit(solution)/shard_map/ppermute | solution.py:544
  104.3 13.4 %collective-permute-start.9 = (f32[16,256]{1,0:T(8,128)S(1)}, f32[16,256]{1,0:T(8,128)S(1)}, u32[]{:S(2)}, u32[]{:S(2)}) collective-permute-start(f32[16,256]{1,0:T(8,128)S(1)} %solve2.1.coef_ref), channel_id=1, source_target_pairs={{0,4},{4,8},{8,12},{12,16},{16,20},{20,24},{24,28},{28,32},{32,36}... | collective-permute-start | bytes 49160 | tf_op jit(solution)/shard_map/ppermute | solution.py:546
  104.4 13.3 %collective-permute-start.10 = (f32[16,256]{1,0:T(8,128)S(1)}, f32[16,256]{1,0:T(8,128)S(1)}, u32[]{:S(2)}, u32[]{:S(2)}) collective-permute-start(f32[16,256]{1,0:T(8,128)S(1)} %solve2.1.coef_ref), channel_id=1, source_target_pairs={{0,2},{2,0},{4,6},{6,4},{8,10},{10,8},{12,14},{14,12},{16,18},{18,... | collective-permute-start | bytes 49160 | tf_op jit(solution)/shard_map/ppermute | solution.py:547

commit v4 on v3

--- a/solution.py
+++ b/solution.py
@@ -426,22 +426,20 @@
     )(offsets, p, hot, coef, sx, ry, z)
 
 
-def solve_kernel(round_index, o_ref, *refs):
-    count = len(refs) // 3
-    for k in range(count):
-        angles(refs[2 * k][...] + refs[2 * k + 1][...], offsets_of(o_ref, round_index), refs[2 * count + k])
-
-
-def solve(round_index, offsets, *lags):
-    count = len(lags) // 2
+def solve_kernel(round_index, o_ref, mine_ref, direct_ref, relayed_ref, coef_ref):
+    lags = mine_ref[...] + direct_ref[...] + relayed_ref[...]
+    angles(lags, offsets_of(o_ref, round_index), coef_ref)
+
+
+def solve(round_index, offsets, mine, direct, relayed):
     return call(
         functools.partial(solve_kernel, round_index),
         "solve%d" % round_index,
-        [SMEM] + [VMEM] * len(lags),
-        (VMEM,) * count,
-        (COEF_SHAPE,) * count,
+        [SMEM] + [VMEM] * 3,
+        VMEM,
+        COEF_SHAPE,
         us=2,
-    )(offsets, *lags)
+    )(offsets, mine, direct, relayed)
 
 
 def own_kernel(o_ref, p_ref, coef_ref, z_ref, q_ref, out_ref):
@@ -522,6 +520,16 @@
     tell = [(2 * j, 2 * j - 2) for j in range(1, chips)] + [(2 * j + 1, 2 * j + 3) for j in range(chips - 1)]
     tell += [(0, 1), (n - 1, n - 2)]
 
+    busy = [i for i in range(n) if i % 8 in (1, 6)]
+    hand = [(i, i ^ 1) for i in busy]
+    free = [(2 * i + r, 2 * i + 1 - r) for i in range(n) if i not in busy for r in (0, 1)]
+    relay = [(2 * (i ^ 1) + r, 2 * i + 1 - r) for i in busy for r in (0, 1)]
+
+    def swap(lag):
+        handed = lax.ppermute(lag, "blk", hand)
+        lag, handed = lax.optimization_barrier((lag, handed))
+        return lag, lax.ppermute(lag, ("blk", "row"), free), lax.ppermute(handed, ("blk", "row"), relay)
+
     upper, lower, lag = first(offsets, row_feats, col_feats)
     lag_other = lax.ppermute(lag, "row", across)
     xa, xb, x, y, coef_a = turn_first(offsets, p, lag, lag_other, upper, lower)
@@ -534,15 +542,13 @@
     y, gram = lax.optimization_barrier((y, gram))
     ry = lax.ppermute(y, "blk", lend)
     lag = pairs(offsets, p, hot, gram, rxb, sy)
-    lag_other = lax.ppermute(lag, "row", across)
-    (coef_b,) = solve(1, offsets, lag, lag_other)
+    coef_b = solve(1, offsets, *swap(lag))
     coef_side = lax.ppermute(coef_b, "blk", tell)
     z, v = turn_second(offsets, p, coef_b, rxa, rxb, sy)
     z, coef_side = lax.optimization_barrier((z, coef_side))
     r_block = lax.ppermute(z, "blk", deal)
     q, lag = side(n - 1, offsets, p, hot_later, coef_side, sx, ry, z)
-    lag_other = lax.ppermute(lag, "row", across)
-    (coef_c,) = solve(2, offsets, lag, lag_other)
+    coef_c = solve(2, offsets, *swap(lag))
     coef_got = lax.ppermute(coef_c, "blk", deal)
     coef_norm = lax.ppermute(coef_c, "blk", sibling)
     own_block = own(offsets, p, coef_c, z, q)

time: 123 us -> 126 us (1.024)
  the two profiles are of different devices: /device:TPU:4 before, /device:TPU:53 now
where the time goes in v4:
time: 126 us
  starting transfers between devices  57.9 us (46%)
  Pallas kernels  41.5 us (33%)
  waiting for transfers between devices  25.1 us (20%)
    ppermute x1, starting transfers between devices, body(): coef_norm = lax.ppermute(coef_c, 'blk', sibling)  18.1 us
    ppermute x2, starting transfers between devices, swap(): lax.ppermute(lag, ('blk', 'row'), free)  10.8 us
    pallas_call x1, Pallas kernels, first(): call(first_kernel, 'first', [ANY, ANY, ANY], (VMEM, VMEM, VMEM), (block(r...  10.7 us
    ppermute x2, waiting for transfers between devices, swap(): lax.ppermute(lag, ('blk', 'row'), free)  9.57 us
    ppermute x1, starting transfers between devices, body(): coef_side = lax.ppermute(coef_b, 'blk', tell)  9.35 us
    pallas_call x1, Pallas kernels, side(): call(functools.partial(side_kernel, last), 'side', [SMEM, SMEM] + [VMEM]...  7.29 us
    ppermute x1, waiting for transfers between devices, body(): rxa = lax.ppermute(xa, 'blk', meet)  7.01 us
    ppermute x1, starting transfers between devices, body(): lag_other = lax.ppermute(lag, 'row', across)  6.1 us
  transfers between devices with their start and end apart: 16, of which 5 were waited for; matrix products, arithmetic and copies ran while one was open for 0% of the time, Pallas kernels for 17%

profile of v4, /device:TPU:53, one launch (start us, length us, event | category | flops | bytes accessed | tf_op | source)
XLA Modules:
  0.0 126.1 jit_solution(3806548516547974268)
XLA Ops:
  1.3 10.7 %first.1 = (f32[1536,256]{1,0:T(8,128)S(1)}, f32[1536,256]{1,0:T(8,128)S(1)}, f32[96,256]{1,0:T(8,128)S(1)}) custom-call(s32[3,4]{1,0:T(4,128)S(1)} %copy-done, bf16[1536,2048]{1,0:T(8,128)(2,1)} %rows_hbm.1, bf16[512,2048]{1,0:T(8,128)(2,1)} %cols_hbm.1), custom_call_target="tpu_custom_call" | custom-call | flops 10000000000 | bytes 30000000 | tf_op jit(solution)/shard_map/first/pallas_call | solution.py:274
  12.0 6.1 %collective-permute-start = (f32[96,256]{1,0:T(8,128)S(1)}, f32[96,256]{1,0:T(8,128)S(1)}, u32[]{:S(2)}, u32[]{:S(2)}) collective-permute-start(f32[96,256]{1,0:T(8,128)S(1)} %get-tuple-element.24.mine_ref), channel_id=1, source_target_pairs={{0,1},{1,0},{2,3},{3,2},{4,5},{5,4},{6,7},{7,6},{8,9},{9,8},{10,11... | collective-permute-start | bytes 294920 | tf_op jit(solution)/shard_map/ppermute | solution.py:534
  18.1 2.5 %collective-permute-done.other_ref = f32[96,256]{1,0:T(8,128)S(1)} collective-permute-done((f32[96,256]{1,0:T(8,128)S(1)}, f32[96,256]{1,0:T(8,128)S(1)}, u32[]{:S(2)}, u32[]{:S(2)}) %collective-permute-start) | collective-permute-done | bytes 98336 | tf_op jit(solution)/shard_map/ppermute | solution.py:534
  20.7 4.2 %turn0.1 = (f32[768,256]{1,0:T(8,128)S(1)}, f32[768,256]{1,0:T(8,128)S(1)}, f32[1536,256]{1,0:T(8,128)S(1)}, f32[1536,256]{1,0:T(8,128)S(1)}, f32[16,256]{1,0:T(8,128)S(1)}) custom-call(s32[3,4]{1,0:T(4,128)S(1)} %copy-done.1, s32[1]{0:T(128)} %bitcast.p_ref, f32[96,256]{1,0:T(8,128)S(1)} %get-tuple-element.24.mine_ref, ...), custom_call_target="tpu_custom_call" | custom-call | flops 5000000000 | bytes 15000000 | tf_op jit(solution)/shard_map/turn0/pallas_call | solution.py:335
  24.8 2.8 %collective-permute-start.2 = (f32[1536,256]{1,0:T(8,128)S(1)}, f32[1536,256]{1,0:T(8,128)S(1)}, u32[]{:S(2)}, u32[]{:S(2)}) collective-permute-start(f32[1536,256]{1,0:T(8,128)S(1)} %get-tuple-element.39), channel_id=1, source_target_pairs={{0,2},{2,0},{4,6},{6,4},{8,10},{10,8},{12,14},{14,12},{16,18},{18,... | collective-permute-start | bytes 4718600 | tf_op jit(solution)/shard_map/ppermute | solution.py:538
  27.6 2.8 %collective-permute-start.1 = (f32[768,256]{1,0:T(8,128)S(1)}, f32[768,256]{1,0:T(8,128)S(1)}, u32[]{:S(2)}, u32[]{:S(2)}) collective-permute-start(f32[768,256]{1,0:T(8,128)S(1)} %get-tuple-element.31), channel_id=1, source_target_pairs={{2,4},{6,8},{10,12},{14,16},{18,20},{22,24},{26,28},{30,32},{34,36... | collective-permute-start | bytes 2359304 | tf_op jit(solution)/shard_map/ppermute | solution.py:536
  30.4 2.7 %collective-permute-start.3 = (f32[768,256]{1,0:T(8,128)S(1)}, f32[768,256]{1,0:T(8,128)S(1)}, u32[]{:S(2)}, u32[]{:S(2)}) collective-permute-start(f32[768,256]{1,0:T(8,128)S(1)} %get-tuple-element.33), channel_id=1, source_target_pairs={{2,4},{6,8},{10,12},{14,16},{18,20},{22,24},{26,28},{30,32},{34,36... | collective-permute-start | bytes 2359304 | tf_op jit(solution)/shard_map/ppermute | solution.py:537
  34.2 7.0 %collective-permute-done.1.a_ref.rxa = f32[768,256]{1,0:T(8,128)S(1)} collective-permute-done((f32[768,256]{1,0:T(8,128)S(1)}, f32[768,256]{1,0:T(8,128)S(1)}, u32[]{:S(2)}, u32[]{:S(2)}) %collective-permute-start.1) | collective-permute-done | bytes 786464 | tf_op jit(solution)/shard_map/ppermute | solution.py:536
  41.2 1.5 %pairs0.1.gram_ref = f32[512,512]{1,0:T(8,128)S(1)} custom-call(s32[1]{0:T(128)} %bitcast.p_ref, f32[768,256]{1,0:T(8,128)S(1)} %collective-permute-done.1.a_ref.rxa, f32[1536,256]{1,0:T(8,128)S(1)} %collective-permute-done.2.b_ref.sy_ref), custom_call_target="tpu_custom_call" | custom-call | flops 3000000000 | bytes 9000000 | tf_op jit(solution)/shard_map/pairs0/pallas_call | solution.py:352
  42.6 1.9 %collective-permute-start.9 = (f32[1536,256]{1,0:T(8,128)S(1)}, f32[1536,256]{1,0:T(8,128)S(1)}, u32[]{:S(2)}, u32[]{:S(2)}) collective-permute-start(f32[1536,256]{1,0:T(8,128)S(1)} %get-tuple-element.39), channel_id=1, source_target_pairs={{0,6},{4,10},{8,14},{12,18},{16,22},{20,26},{24,30},{28,34},{32,38... | collective-permute-start | bytes 4718600 | tf_op jit(solution)/shard_map/ppermute | solution.py:543
  44.6 6.0 %collective-permute-done.3.a_ref.rxb = f32[768,256]{1,0:T(8,128)S(1)} collective-permute-done((f32[768,256]{1,0:T(8,128)S(1)}, f32[768,256]{1,0:T(8,128)S(1)}, u32[]{:S(2)}, u32[]{:S(2)}) %collective-permute-start.3) | collective-permute-done | bytes 786464 | tf_op jit(solution)/shard_map/ppermute | solution.py:537
  50.5 3.4 %pairs1.1.mine_ref = f32[96,256]{1,0:T(8,128)S(1)} custom-call(s32[3,4]{1,0:T(4,128)S(1)} %copy-done.1, s32[1]{0:T(128)} %bitcast.p_ref, bf16[96,512]{1,0:T(8,128)(2,1)S(1)} %get-tuple-element.29.hot_ref, f32[512,512]{1,0:T(8,128)S(1)} %pairs0.1.gram_ref, f32[768,256]{1,0:T(8,128)S(1)} %collective-permute-done.3.a_ref.rxb, ...), custom_call_target="tpu_custom_call" | custom-call | flops 20000000000 | bytes 60000000 | tf_op jit(solution)/shard_map/pairs1/pallas_call | solution.py:364
  54.7 8.0 %collective-permute-start.5 = (f32[96,256]{1,0:T(8,128)S(1)}, f32[96,256]{1,0:T(8,128)S(1)}, u32[]{:S(2)}, u32[]{:S(2)}) collective-permute-start(f32[96,256]{1,0:T(8,128)S(1)} %pairs1.1.mine_ref), channel_id=1, source_target_pairs={{0,1},{1,0},{4,5},{5,4},{6,7},{7,6},{8,9},{9,8},{10,11},{11,10},{1... | collective-permute-start | bytes 294920 | tf_op jit(solution)/shard_map/ppermute | solution.py:531
  63.3 3.8 %collective-permute-done.5.direct_ref = f32[96,256]{1,0:T(8,128)S(1)} collective-permute-done((f32[96,256]{1,0:T(8,128)S(1)}, f32[96,256]{1,0:T(8,128)S(1)}, u32[]{:S(2)}, u32[]{:S(2)}) %collective-permute-start.5) | collective-permute-done | bytes 98336 | tf_op jit(solution)/shard_map/ppermute | solution.py:531
  67.1 1.1 solve1.1.coef_ref.b_ref
  68.2 9.3 %collective-permute-start.7 = (f32[16,256]{1,0:T(8,128)S(1)}, f32[16,256]{1,0:T(8,128)S(1)}, u32[]{:S(2)}, u32[]{:S(2)}) collective-permute-start(f32[16,256]{1,0:T(8,128)S(1)} %solve1.1.coef_ref.b_ref), channel_id=1, source_target_pairs={{4,0},{8,4},{12,8},{16,12},{20,16},{24,20},{28,24},{32,28},{36,32}... | collective-permute-start | bytes 49160 | tf_op jit(solution)/shard_map/ppermute | solution.py:546
  77.6 3.6 %turn1.1 = (f32[1536,256]{1,0:T(8,128)S(1)}, f32[1536,256]{1,0:T(8,128)S(1)}) custom-call(s32[3,4]{1,0:T(4,128)S(1)} %copy-done.1, s32[1]{0:T(128)} %bitcast.p_ref, f32[16,256]{1,0:T(8,128)S(1)} %solve1.1.coef_ref.b_ref, f32[768,256]{1,0:T(8,128)S(1)} %collective-permute-done.1.a_ref.rxa, f32[768,256]{1,0:T(8,128)S(1)} %collective-permute-done.3.a_ref.rxb, ...), custom_call_target="tpu_custom_call" | custom-call | flops 8000000000 | bytes 24000000 | tf_op jit(solution)/shard_map/turn1/pallas_call | solution.py:387
  81.3 7.3 %side.1 = (f32[1536,256]{1,0:T(8,128)S(1)}, f32[96,256]{1,0:T(8,128)S(1)}) custom-call(s32[3,4]{1,0:T(4,128)S(1)} %copy-done.1, s32[1]{0:T(128)} %bitcast.p_ref, bf16[96,512]{1,0:T(8,128)(2,1)S(1)} %get-tuple-element.28.hot_ref, f32[16,256]{1,0:T(8,128)S(1)} %collective-permute-done.7.coef_ref, f32[1536,256]{1,0:T(8,128)S(1)} %collective-permute-done.8.sx_ref, ...), custom_call_target="tpu_custom_call" | custom-call | flops 8000000000 | bytes 24000000 | tf_op jit(solution)/shard_map/side/pallas_call | solution.py:419
  89.3 2.8 %collective-permute-start.11 = (f32[96,256]{1,0:T(8,128)S(1)}, f32[96,256]{1,0:T(8,128)S(1)}, u32[]{:S(2)}, u32[]{:S(2)}) collective-permute-start(f32[96,256]{1,0:T(8,128)S(1)} %get-tuple-element.42.mine_ref), channel_id=1, source_target_pairs={{0,1},{1,0},{4,5},{5,4},{6,7},{7,6},{8,9},{9,8},{10,11},{11,10},{1... | collective-permute-start | bytes 294920 | tf_op jit(solution)/shard_map/ppermute | solution.py:531
  92.8 5.8 %collective-permute-done.11.direct_ref = f32[96,256]{1,0:T(8,128)S(1)} collective-permute-done((f32[96,256]{1,0:T(8,128)S(1)}, f32[96,256]{1,0:T(8,128)S(1)}, u32[]{:S(2)}, u32[]{:S(2)}) %collective-permute-start.11) | collective-permute-done | bytes 98336 | tf_op jit(solution)/shard_map/ppermute | solution.py:531
  98.5 1.1 solve2.1.coef_ref
  99.9 18.1 %collective-permute-start.14 = (f32[16,256]{1,0:T(8,128)S(1)}, f32[16,256]{1,0:T(8,128)S(1)}, u32[]{:S(2)}, u32[]{:S(2)}) collective-permute-start(f32[16,256]{1,0:T(8,128)S(1)} %solve2.1.coef_ref), channel_id=1, source_target_pairs={{0,2},{2,0},{4,6},{6,4},{8,10},{10,8},{12,14},{14,12},{16,18},{18,... | collective-permute-start | bytes 49160 | tf_op jit(solution)/shard_map/ppermute | solution.py:553
  117.9 3.2 %own.1.own_ref = f32[1536,256]{1,0:T(8,128)S(1)} custom-call(s32[3,4]{1,0:T(4,128)S(1)} %copy-done.1, s32[1]{0:T(128)} %bitcast.p_ref, f32[16,256]{1,0:T(8,128)S(1)} %solve2.1.coef_ref, f32[1536,256]{1,0:T(8,128)S(1)} %get-tuple-element.40.z_ref, f32[1536,256]{1,0:T(8,128)S(1)} %get-tuple-element.44.q_ref), custom_call_target="tpu_custom_call" | custom-call | flops 5000000000 | bytes 15000000 | tf_op jit(solution)/shard_map/own/pallas_call | solution.py:461
  121.2 4.8 %finish.1 = (f32[2,1536,256]{2,1,0:T(8,128)}, f32[3,2,256]{2,1,0:T(2,128)}) custom-call(s32[3,4]{1,0:T(4,128)S(1)} %copy-done.1, s32[1]{0:T(128)} %bitcast.p_ref, f32[16,256]{1,0:T(8,128)S(1)} %collective-permute-done.13.coef_ref, f32[16,256]{1,0:T(8,128)S(1)} %get-tuple-element.27.after_ref.a_ref, f32[16,256]{1,0:T(8,128)S(1)} %solve1.1.coef_ref.b_ref, ...), custom_call_target="tpu_custom_call" | custom-call | flops 5000000000 | bytes 15000000 | tf_op jit(solution)/shard_map/finish/pallas_call | solution.py:496
  (23 shorter events, 4.7 us)
Async XLA Ops:
  0.6 0.7 copy-start
  1.3 19.3 %copy-start.1 = (s32[3,4]{1,0:T(4,128)S(1)}, s32[3,4]{1,0:T(4,128)}, u32[]{:S(2)}) copy-start(s32[3,4]{1,0:T(4,128)} %o_ref.17) | copy-start | bytes 148
  12.0 8.6 %collective-permute-start = (f32[96,256]{1,0:T(8,128)S(1)}, f32[96,256]{1,0:T(8,128)S(1)}, u32[]{:S(2)}, u32[]{:S(2)}) collective-permute-start(f32[96,256]{1,0:T(8,128)S(1)} %get-tuple-element.24.mine_ref), channel_id=1, source_target_pairs={{0,1},{1,0},{2,3},{3,2},{4,5},{5,4},{6,7},{7,6},{8,9},{9,8},{10,11... | collective-permute-start | bytes 294920 | tf_op jit(solution)/shard_map/ppermute | solution.py:534
  24.8 16.4 %collective-permute-start.2 = (f32[1536,256]{1,0:T(8,128)S(1)}, f32[1536,256]{1,0:T(8,128)S(1)}, u32[]{:S(2)}, u32[]{:S(2)}) collective-permute-start(f32[1536,256]{1,0:T(8,128)S(1)} %get-tuple-element.39), channel_id=1, source_target_pairs={{0,2},{2,0},{4,6},{6,4},{8,10},{10,8},{12,14},{14,12},{16,18},{18,... | collective-permute-start | bytes 4718600 | tf_op jit(solution)/shard_map/ppermute | solution.py:538
  27.6 13.6 %collective-permute-start.1 = (f32[768,256]{1,0:T(8,128)S(1)}, f32[768,256]{1,0:T(8,128)S(1)}, u32[]{:S(2)}, u32[]{:S(2)}) collective-permute-start(f32[768,256]{1,0:T(8,128)S(1)} %get-tuple-element.31), channel_id=1, source_target_pairs={{2,4},{6,8},{10,12},{14,16},{18,20},{22,24},{26,28},{30,32},{34,36... | collective-permute-start | bytes 2359304 | tf_op jit(solution)/shard_map/ppermute | solution.py:536
  30.4 20.1 %collective-permute-start.3 = (f32[768,256]{1,0:T(8,128)S(1)}, f32[768,256]{1,0:T(8,128)S(1)}, u32[]{:S(2)}, u32[]{:S(2)}) collective-permute-start(f32[768,256]{1,0:T(8,128)S(1)} %get-tuple-element.33), channel_id=1, source_target_pairs={{2,4},{6,8},{10,12},{14,16},{18,20},{22,24},{26,28},{30,32},{34,36... | collective-permute-start | bytes 2359304 | tf_op jit(solution)/shard_map/ppermute | solution.py:537
  33.2 48.1 %collective-permute-start.8 = (f32[1536,256]{1,0:T(8,128)S(1)}, f32[1536,256]{1,0:T(8,128)S(1)}, u32[]{:S(2)}, u32[]{:S(2)}) collective-permute-start(f32[1536,256]{1,0:T(8,128)S(1)} %get-tuple-element.38), channel_id=1, source_target_pairs={{0,2},{2,0},{4,6},{6,4},{8,10},{10,8},{12,14},{14,12},{16,18},{18,... | collective-permute-start | bytes 4718600 | tf_op jit(solution)/shard_map/ppermute | solution.py:539
  42.6 38.6 %collective-permute-start.9 = (f32[1536,256]{1,0:T(8,128)S(1)}, f32[1536,256]{1,0:T(8,128)S(1)}, u32[]{:S(2)}, u32[]{:S(2)}) collective-permute-start(f32[1536,256]{1,0:T(8,128)S(1)} %get-tuple-element.39), channel_id=1, source_target_pairs={{0,6},{4,10},{8,14},{12,18},{16,22},{20,26},{24,30},{28,34},{32,38... | collective-permute-start | bytes 4718600 | tf_op jit(solution)/shard_map/ppermute | solution.py:543
  54.0 0.7 collective-permute-start.4
  54.7 12.5 %collective-permute-start.5 = (f32[96,256]{1,0:T(8,128)S(1)}, f32[96,256]{1,0:T(8,128)S(1)}, u32[]{:S(2)}, u32[]{:S(2)}) collective-permute-start(f32[96,256]{1,0:T(8,128)S(1)} %pairs1.1.mine_ref), channel_id=1, source_target_pairs={{0,1},{1,0},{4,5},{5,4},{6,7},{7,6},{8,9},{9,8},{10,11},{11,10},{1... | collective-permute-start | bytes 294920 | tf_op jit(solution)/shard_map/ppermute | solution.py:531
  62.6 4.5 %collective-permute-start.6 = (f32[96,256]{1,0:T(8,128)S(1)}, f32[96,256]{1,0:T(8,128)S(1)}, u32[]{:S(2)}, u32[]{:S(2)}) collective-permute-start(f32[96,256]{1,0:T(8,128)S(1)} %collective-permute-done.4), channel_id=1, source_target_pairs={{0,3},{1,2},{14,13},{15,12},{16,19},{17,18},{30,29},{31,28},{32,35... | collective-permute-start | bytes 294920 | tf_op jit(solution)/shard_map/ppermute | solution.py:531
  68.2 12.9 %collective-permute-start.7 = (f32[16,256]{1,0:T(8,128)S(1)}, f32[16,256]{1,0:T(8,128)S(1)}, u32[]{:S(2)}, u32[]{:S(2)}) collective-permute-start(f32[16,256]{1,0:T(8,128)S(1)} %solve1.1.coef_ref.b_ref), channel_id=1, source_target_pairs={{4,0},{8,4},{12,8},{16,12},{20,16},{24,20},{28,24},{32,28},{36,32}... | collective-permute-start | bytes 49160 | tf_op jit(solution)/shard_map/ppermute | solution.py:546
  81.2 40.0 %collective-permute-start.15 = (f32[1536,256]{1,0:T(8,128)S(1)}, f32[1536,256]{1,0:T(8,128)S(1)}, u32[]{:S(2)}, u32[]{:S(2)}) collective-permute-start(f32[1536,256]{1,0:T(8,128)S(1)} %get-tuple-element.40.z_ref), channel_id=1, source_target_pairs={{0,4},{4,8},{8,12},{12,16},{16,20},{20,24},{24,28},{28,32},{32,36}... | collective-permute-start | bytes 4718600 | tf_op jit(solution)/shard_map/ppermute | solution.py:549
  88.6 0.7 collective-permute-start.10
  89.3 9.3 %collective-permute-start.11 = (f32[96,256]{1,0:T(8,128)S(1)}, f32[96,256]{1,0:T(8,128)S(1)}, u32[]{:S(2)}, u32[]{:S(2)}) collective-permute-start(f32[96,256]{1,0:T(8,128)S(1)} %get-tuple-element.42.mine_ref), channel_id=1, source_target_pairs={{0,1},{1,0},{4,5},{5,4},{6,7},{7,6},{8,9},{9,8},{10,11},{11,10},{1... | collective-permute-start | bytes 294920 | tf_op jit(solution)/shard_map/ppermute | solution.py:531
  92.1 6.4 %collective-permute-start.12 = (f32[96,256]{1,0:T(8,128)S(1)}, f32[96,256]{1,0:T(8,128)S(1)}, u32[]{:S(2)}, u32[]{:S(2)}) collective-permute-start(f32[96,256]{1,0:T(8,128)S(1)} %collective-permute-done.10), channel_id=1, source_target_pairs={{0,3},{1,2},{14,13},{15,12},{16,19},{17,18},{30,29},{31,28},{32,35... | collective-permute-start | bytes 294920 | tf_op jit(solution)/shard_map/ppermute | solution.py:531
  99.6 21.5 %collective-permute-start.13 = (f32[16,256]{1,0:T(8,128)S(1)}, f32[16,256]{1,0:T(8,128)S(1)}, u32[]{:S(2)}, u32[]{:S(2)}) collective-permute-start(f32[16,256]{1,0:T(8,128)S(1)} %solve2.1.coef_ref), channel_id=1, source_target_pairs={{0,4},{4,8},{8,12},{12,16},{16,20},{20,24},{24,28},{28,32},{32,36}... | collective-permute-start | bytes 49160 | tf_op jit(solution)/shard_map/ppermute | solution.py:552
  99.9 21.3 %collective-permute-start.14 = (f32[16,256]{1,0:T(8,128)S(1)}, f32[16,256]{1,0:T(8,128)S(1)}, u32[]{:S(2)}, u32[]{:S(2)}) collective-permute-start(f32[16,256]{1,0:T(8,128)S(1)} %solve2.1.coef_ref), channel_id=1, source_target_pairs={{0,2},{2,0},{4,6},{6,4},{8,10},{10,8},{12,14},{14,12},{16,18},{18,... | collective-permute-start | bytes 49160 | tf_op jit(solution)/shard_map/ppermute | solution.py:553

commit v5 on v2

--- a/solution.py
+++ b/solution.py
@@ -362,11 +362,10 @@
     )(offsets, p, hot, gram, a, b)
 
 
-def turn_second_kernel(o_ref, p_ref, mine_ref, other_ref, rxa, rxb, sya, syb, za, zb, v_ref, coef_ref):
+def turn_second_kernel(o_ref, p_ref, coef_ref, rxa, rxb, sya, syb, za, zb, v_ref):
     p = p_ref[0]
     core = p & 1
     o = offsets_of(o_ref, 1)
-    angles(mine_ref[...] + other_ref[...], o, coef_ref)
     coef = coef_ref[...]
 
     def go(rows, k, rows_part):
@@ -379,17 +378,17 @@
     by_parts(v_ref.shape[0], go)
 
 
-def turn_second(offsets, p, mine, other, rxa, rxb, sya, syb):
+def turn_second(offsets, p, coef, rxa, rxb, sya, syb):
     rows = rxa.shape[0] * 2
     part = block(rows // 2)
     return call(
         turn_second_kernel,
         "turn1",
-        [SMEM, SMEM] + [VMEM] * 6,
-        (VMEM,) * 4,
-        (part, part, block(rows), COEF_SHAPE),
+        [SMEM, SMEM] + [VMEM] * 5,
+        (VMEM,) * 3,
+        (part, part, block(rows)),
         us=40,
-    )(offsets, p, mine, other, rxa, rxb, sya, syb)
+    )(offsets, p, coef, rxa, rxb, sya, syb)
 
 
 def side_kernel(last, o_ref, p_ref, hot_ref, coef_ref, sxa, sxb, rya, ryb, za, zb, q_ref, lag_ref):
@@ -425,22 +424,19 @@
     )(offsets, p, hot, coef, sxa, sxb, rya, ryb, za, zb)
 
 
-def solve_kernel(round_index, o_ref, *refs):
-    count = len(refs) // 3
-    for k in range(count):
-        angles(refs[2 * k][...] + refs[2 * k + 1][...], offsets_of(o_ref, round_index), refs[2 * count + k])
-
-
-def solve(round_index, offsets, *lags):
-    count = len(lags) // 2
+def solve_kernel(round_index, o_ref, mine_ref, other_ref, coef_ref):
+    angles(mine_ref[...] + other_ref[...], offsets_of(o_ref, round_index), coef_ref)
+
+
+def solve(round_index, offsets, mine, other):
     return call(
         functools.partial(solve_kernel, round_index),
         "solve%d" % round_index,
-        [SMEM] + [VMEM] * len(lags),
-        (VMEM,) * count,
-        (COEF_SHAPE,) * count,
+        [SMEM] + [VMEM] * 2,
+        VMEM,
+        COEF_SHAPE,
         us=2,
-    )(offsets, *lags)
+    )(offsets, mine, other)
 
 
 def own_kernel(o_ref, p_ref, coef_ref, za, zb, q_ref, out_ref):
@@ -522,21 +518,12 @@
     tell = [(2 * j, 2 * j - 2) for j in range(1, chips)] + [(2 * j + 1, 2 * j + 3) for j in range(chips - 1)]
     tell += [(0, 1), (n - 1, n - 2)]
 
-    def exchange(lag, perm):
-        flipped = [(2 * i + r, 2 * j + 1 - r) for i, j in perm for r in (0, 1)]
-        return (
-            lax.ppermute(lag, "row", across),
-            lax.ppermute(lag, "blk", perm),
-            lax.ppermute(lag, ("blk", "row"), flipped),
-        )
-
     upper, lower, lag = first(offsets, row_feats, col_feats)
     lag_other = lax.ppermute(lag, "row", across)
     xa, xb, ya, yb, coef_a = turn_first(offsets, p, lag, lag_other, upper, lower)
     hot = table(1, offsets, coef_a)
     rxa = lax.ppermute(xa, "blk", meet)
     rxb = lax.ppermute(xb, "blk", meet)
-    xa, xb, ya, yb, hot = lax.optimization_barrier((xa, xb, ya, yb, hot))
     sya = lax.ppermute(ya, "blk", sibling)
     syb = lax.ppermute(yb, "blk", sibling)
     sxa = lax.ppermute(xa, "blk", sibling)
@@ -545,20 +532,22 @@
     ya, gram = lax.optimization_barrier((ya, gram))
     rya = lax.ppermute(ya, "blk", lend)
     lag = pairs(offsets, p, hot, gram, rxb, syb)
-    lag_other, lag_told, lag_told_other = exchange(lag, tell)
+    lag_other = lax.ppermute(lag, "row", across)
     hot = table(2, offsets, lag)
     yb, hot = lax.optimization_barrier((yb, hot))
     ryb = lax.ppermute(yb, "blk", lend)
+    coef_b = solve(1, offsets, lag, lag_other)
+    coef_side = lax.ppermute(coef_b, "blk", tell)
     rxa, rya, sxa, sxb = lax.optimization_barrier((rxa, rya, sxa, sxb))
-    za, zb, v, coef_b = turn_second(offsets, p, lag, lag_other, rxa, rxb, sya, syb)
+    za, zb, v = turn_second(offsets, p, coef_b, rxa, rxb, sya, syb)
+    za, zb, coef_side = lax.optimization_barrier((za, zb, coef_side))
     ra = lax.ppermute(za, "blk", deal)
-    lag_told, lag_told_other, coef_b = lax.optimization_barrier((lag_told, lag_told_other, coef_b))
-    (coef_side,) = solve(1, offsets, lag_told, lag_told_other)
     q, lag = side(n - 1, offsets, p, hot, coef_side, sxa, sxb, rya, ryb, za, zb)
-    lag_other, lag_got, lag_got_other = exchange(lag, deal)
+    lag_other = lax.ppermute(lag, "row", across)
     later, _ = lax.optimization_barrier((zb, lag))
     rb = lax.ppermute(later, "blk", deal)
-    coef_c, coef_got = solve(2, offsets, lag, lag_other, lag_got, lag_got_other)
+    coef_c = solve(2, offsets, lag, lag_other)
+    coef_got = lax.ppermute(coef_c, "blk", deal)
     coef_norm = lax.ppermute(coef_c, "blk", sibling)
     coef_own, ra = lax.optimization_barrier((coef_c, ra))
     own_block = own(offsets, p, coef_own, za, zb, q)

time: 126 us -> 116 us (0.921)
  the two profiles are of different devices: /device:TPU:97 before, /device:TPU:4 now
where the time goes in v5:
time: 116 us
  Pallas kernels  42.8 us (37%)
  starting transfers between devices  39.9 us (34%)
  waiting for transfers between devices  31.3 us (27%)
    ppermute x3, waiting for transfers between devices, body(): lag_other = lax.ppermute(lag, 'row', across)  14.6 us
    ppermute x3, starting transfers between devices, body(): lag_other = lax.ppermute(lag, 'row', across)  14.5 us
    pallas_call x1, Pallas kernels, first(): call(first_kernel, 'first', [ANY, ANY, ANY], (VMEM, VMEM, VMEM), (block(r...  10.7 us
    pallas_call x1, Pallas kernels, side(): call(functools.partial(side_kernel, last), 'side', [SMEM, SMEM] + [VMEM]...  7.64 us
    ppermute x1, waiting for transfers between devices, body(): rxa = lax.ppermute(xa, 'blk', meet)  7.03 us
    ppermute x1, starting transfers between devices, body(): coef_side = lax.ppermute(coef_b, 'blk', tell)  6.85 us
    ppermute x1, starting transfers between devices, body(): rxa = lax.ppermute(xa, 'blk', meet)  5.83 us
    ppermute x1, waiting for transfers between devices, body(): coef_got = lax.ppermute(coef_c, 'blk', deal)  5.26 us
  transfers between devices with their start and end apart: 16, of which 6 were waited for; matrix products, arithmetic and copies ran while one was open for 0% of the time, Pallas kernels for 20%

profile of v5, /device:TPU:4, one launch (start us, length us, event | category | flops | bytes accessed | tf_op | source)
XLA Modules:
  0.0 115.7 jit_solution(7925196566899229619)
XLA Ops:
  1.3 10.7 %first.1 = (f32[1536,256]{1,0:T(8,128)S(1)}, f32[1536,256]{1,0:T(8,128)S(1)}, f32[96,256]{1,0:T(8,128)S(1)}) custom-call(s32[3,4]{1,0:T(4,128)S(1)} %copy-done, bf16[1536,2048]{1,0:T(8,128)(2,1)} %rows_hbm.1, bf16[512,2048]{1,0:T(8,128)(2,1)} %cols_hbm.1), custom_call_target="tpu_custom_call" | custom-call | flops 10000000000 | bytes 30000000 | tf_op jit(solution)/shard_map/first/pallas_call | solution.py:274
  12.0 7.3 %collective-permute-start = (f32[96,256]{1,0:T(8,128)S(1)}, f32[96,256]{1,0:T(8,128)S(1)}, u32[]{:S(2)}, u32[]{:S(2)}) collective-permute-start(f32[96,256]{1,0:T(8,128)S(1)} %get-tuple-element.29.mine_ref), channel_id=1, source_target_pairs={{0,1},{1,0},{2,3},{3,2},{4,5},{5,4},{6,7},{7,6},{8,9},{9,8},{10,11... | collective-permute-start | bytes 294920 | tf_op jit(solution)/shard_map/ppermute | solution.py:522
  19.3 2.9 %collective-permute-done.other_ref = f32[96,256]{1,0:T(8,128)S(1)} collective-permute-done((f32[96,256]{1,0:T(8,128)S(1)}, f32[96,256]{1,0:T(8,128)S(1)}, u32[]{:S(2)}, u32[]{:S(2)}) %collective-permute-start) | collective-permute-done | bytes 98336 | tf_op jit(solution)/shard_map/ppermute | solution.py:522
  22.2 4.1 %turn0.1 = (f32[768,256]{1,0:T(8,128)S(1)}, f32[768,256]{1,0:T(8,128)S(1)}, f32[768,256]{1,0:T(8,128)S(1)}, f32[768,256]{1,0:T(8,128)S(1)}, f32[16,256]{1,0:T(8,128)S(1)}) custom-call(s32[3,4]{1,0:T(4,128)S(1)} %copy-done.1, s32[1]{0:T(128)} %bitcast.p_ref, f32[96,256]{1,0:T(8,128)S(1)} %get-tuple-element.29.mine_ref, ...), custom_call_target="tpu_custom_call" | custom-call | flops 5000000000 | bytes 15000000 | tf_op jit(solution)/shard_map/turn0/pallas_call | solution.py:333
  26.3 5.8 %collective-permute-start.1 = (f32[768,256]{1,0:T(8,128)S(1)}, f32[768,256]{1,0:T(8,128)S(1)}, u32[]{:S(2)}, u32[]{:S(2)}) collective-permute-start(f32[768,256]{1,0:T(8,128)S(1)} %get-tuple-element.35), channel_id=1, source_target_pairs={{2,4},{6,8},{10,12},{14,16},{18,20},{22,24},{26,28},{30,32},{34,36... | collective-permute-start | bytes 2359304 | tf_op jit(solution)/shard_map/ppermute | solution.py:525
  32.2 4.5 %collective-permute-start.3 = (f32[768,256]{1,0:T(8,128)S(1)}, f32[768,256]{1,0:T(8,128)S(1)}, u32[]{:S(2)}, u32[]{:S(2)}) collective-permute-start(f32[768,256]{1,0:T(8,128)S(1)} %get-tuple-element.37), channel_id=1, source_target_pairs={{2,4},{6,8},{10,12},{14,16},{18,20},{22,24},{26,28},{30,32},{34,36... | collective-permute-start | bytes 2359304 | tf_op jit(solution)/shard_map/ppermute | solution.py:526
  37.4 7.0 %collective-permute-done.1.a_ref.rxa = f32[768,256]{1,0:T(8,128)S(1)} collective-permute-done((f32[768,256]{1,0:T(8,128)S(1)}, f32[768,256]{1,0:T(8,128)S(1)}, u32[]{:S(2)}, u32[]{:S(2)}) %collective-permute-start.1) | collective-permute-done | bytes 786464 | tf_op jit(solution)/shard_map/ppermute | solution.py:525
  44.4 1.5 %pairs0.1.gram_ref = f32[512,512]{1,0:T(8,128)S(1)} custom-call(s32[1]{0:T(128)} %bitcast.p_ref, f32[768,256]{1,0:T(8,128)S(1)} %collective-permute-done.1.a_ref.rxa, f32[768,256]{1,0:T(8,128)S(1)} %collective-permute-done.2.b_ref.sya), custom_call_target="tpu_custom_call" | custom-call | flops 3000000000 | bytes 9000000 | tf_op jit(solution)/shard_map/pairs0/pallas_call | solution.py:349
  45.9 1.9 %collective-permute-start.6 = (f32[768,256]{1,0:T(8,128)S(1)}, f32[768,256]{1,0:T(8,128)S(1)}, u32[]{:S(2)}, u32[]{:S(2)}) collective-permute-start(f32[768,256]{1,0:T(8,128)S(1)} %get-tuple-element.39), channel_id=1, source_target_pairs={{0,6},{4,10},{8,14},{12,18},{16,22},{20,26},{24,30},{28,34},{32,38... | collective-permute-start | bytes 2359304 | tf_op jit(solution)/shard_map/ppermute | solution.py:533
  48.4 4.4 %collective-permute-done.3.a_ref.rxb = f32[768,256]{1,0:T(8,128)S(1)} collective-permute-done((f32[768,256]{1,0:T(8,128)S(1)}, f32[768,256]{1,0:T(8,128)S(1)}, u32[]{:S(2)}, u32[]{:S(2)}) %collective-permute-start.3) | collective-permute-done | bytes 786464 | tf_op jit(solution)/shard_map/ppermute | solution.py:526
  52.8 3.4 %pairs1.1.after_ref.mine_ref = f32[96,256]{1,0:T(8,128)S(1)} custom-call(s32[3,4]{1,0:T(4,128)S(1)} %copy-done.1, s32[1]{0:T(128)} %bitcast.p_ref, bf16[96,512]{1,0:T(8,128)(2,1)S(1)} %table1.1.hot_ref, f32[512,512]{1,0:T(8,128)S(1)} %pairs0.1.gram_ref, f32[768,256]{1,0:T(8,128)S(1)} %collective-permute-done.3.a_ref.rxb, ...), custom_call_target="tpu_custom_call" | custom-call | flops 4000000000 | bytes 12000000 | tf_op jit(solution)/shard_map/pairs1/pallas_call | solution.py:360
  56.2 7.1 %collective-permute-start.5 = (f32[96,256]{1,0:T(8,128)S(1)}, f32[96,256]{1,0:T(8,128)S(1)}, u32[]{:S(2)}, u32[]{:S(2)}) collective-permute-start(f32[96,256]{1,0:T(8,128)S(1)} %pairs1.1.after_ref.mine_ref), channel_id=1, source_target_pairs={{0,1},{1,0},{2,3},{3,2},{4,5},{5,4},{6,7},{7,6},{8,9},{9,8},{10,11... | collective-permute-start | bytes 294920 | tf_op jit(solution)/shard_map/ppermute | solution.py:535
  64.0 1.9 %collective-permute-start.10 = (f32[768,256]{1,0:T(8,128)S(1)}, f32[768,256]{1,0:T(8,128)S(1)}, u32[]{:S(2)}, u32[]{:S(2)}) collective-permute-start(f32[768,256]{1,0:T(8,128)S(1)} %get-tuple-element.47), channel_id=1, source_target_pairs={{0,6},{4,10},{8,14},{12,18},{16,22},{20,26},{24,30},{28,34},{32,38... | collective-permute-start | bytes 2359304 | tf_op jit(solution)/shard_map/ppermute | solution.py:538
  65.9 3.2 %collective-permute-done.5.other_ref = f32[96,256]{1,0:T(8,128)S(1)} collective-permute-done((f32[96,256]{1,0:T(8,128)S(1)}, f32[96,256]{1,0:T(8,128)S(1)}, u32[]{:S(2)}, u32[]{:S(2)}) %collective-permute-start.5) | collective-permute-done | bytes 98336 | tf_op jit(solution)/shard_map/ppermute | solution.py:535
  69.1 1.1 solve1.1.coef_ref.b_ref
  70.2 6.8 %collective-permute-start.9 = (f32[16,256]{1,0:T(8,128)S(1)}, f32[16,256]{1,0:T(8,128)S(1)}, u32[]{:S(2)}, u32[]{:S(2)}) collective-permute-start(f32[16,256]{1,0:T(8,128)S(1)} %solve1.1.coef_ref.b_ref), channel_id=1, source_target_pairs={{4,0},{8,4},{12,8},{16,12},{20,16},{24,20},{28,24},{32,28},{36,32}... | collective-permute-start | bytes 49160 | tf_op jit(solution)/shard_map/ppermute | solution.py:540
  77.0 3.6 %turn1.1 = (f32[768,256]{1,0:T(8,128)S(1)}, f32[768,256]{1,0:T(8,128)S(1)}, f32[1536,256]{1,0:T(8,128)S(1)}) custom-call(s32[3,4]{1,0:T(4,128)S(1)} %copy-done.1, s32[1]{0:T(128)} %bitcast.p_ref, f32[16,256]{1,0:T(8,128)S(1)} %solve1.1.coef_ref.b_ref, f32[768,256]{1,0:T(8,128)S(1)} %collective-permute-done.1.a_ref.rxa, ...), custom_call_target="tpu_custom_call" | custom-call | flops 40000000000 | bytes 120000000 | tf_op jit(solution)/shard_map/turn1/pallas_call | solution.py:384
  81.0 7.6 %side.1 = (f32[1536,256]{1,0:T(8,128)S(1)}, f32[96,256]{1,0:T(8,128)S(1)}) custom-call(s32[3,4]{1,0:T(4,128)S(1)} %copy-done.1, s32[1]{0:T(128)} %bitcast.p_ref, bf16[96,512]{1,0:T(8,128)(2,1)S(1)} %table2.1.hot_ref, f32[16,256]{1,0:T(8,128)S(1)} %collective-permute-done.9.coef_ref, f32[768,256]{1,0:T(8,128)S(1)} %collective-permute-done.7.sxa, ...), custom_call_target="tpu_custom_call" | custom-call | flops 8000000000 | bytes 24000000 | tf_op jit(solution)/shard_map/side/pallas_call | solution.py:417
  88.8 8.5 %collective-permute-done.11.other_ref = f32[96,256]{1,0:T(8,128)S(1)} collective-permute-done((f32[96,256]{1,0:T(8,128)S(1)}, f32[96,256]{1,0:T(8,128)S(1)}, u32[]{:S(2)}, u32[]{:S(2)}) %collective-permute-start.11) | collective-permute-done | bytes 98336 | tf_op jit(solution)/shard_map/ppermute | solution.py:546
  97.3 1.1 solve2.1.coef_ref
  98.4 3.3 %collective-permute-start.13 = (f32[16,256]{1,0:T(8,128)S(1)}, f32[16,256]{1,0:T(8,128)S(1)}, u32[]{:S(2)}, u32[]{:S(2)}) collective-permute-start(f32[16,256]{1,0:T(8,128)S(1)} %solve2.1.coef_ref), channel_id=1, source_target_pairs={{0,2},{2,0},{4,6},{6,4},{8,10},{10,8},{12,14},{14,12},{16,18},{18,... | collective-permute-start | bytes 49160 | tf_op jit(solution)/shard_map/ppermute | solution.py:551
  101.7 3.6 %own.1.own_ref = f32[1536,256]{1,0:T(8,128)S(1)} custom-call(s32[3,4]{1,0:T(4,128)S(1)} %copy-done.1, s32[1]{0:T(128)} %bitcast.p_ref, f32[16,256]{1,0:T(8,128)S(1)} %solve2.1.coef_ref, f32[768,256]{1,0:T(8,128)S(1)} %get-tuple-element.48.za, f32[768,256]{1,0:T(8,128)S(1)} %get-tuple-element.54.zb, f32[1536,256]{1,0:T(8,128)S(1)} %get-tuple-element.52.q_ref), custom_call_target="tpu_custom_call" | custom-call | flops 40000000000 | bytes 120000000 | tf_op jit(solution)/shard_map/own/pallas_call | solution.py:458
  105.3 5.3 %collective-permute-done.12.coef_ref = f32[16,256]{1,0:T(8,128)S(1)} collective-permute-done((f32[16,256]{1,0:T(8,128)S(1)}, f32[16,256]{1,0:T(8,128)S(1)}, u32[]{:S(2)}, u32[]{:S(2)}) %collective-permute-start.12) | collective-permute-done | bytes 16416 | tf_op jit(solution)/shard_map/ppermute | solution.py:550
  110.5 5.0 %finish.1 = (f32[2,1536,256]{2,1,0:T(8,128)}, f32[3,2,256]{2,1,0:T(2,128)}) custom-call(s32[3,4]{1,0:T(4,128)S(1)} %copy-done.1, s32[1]{0:T(128)} %bitcast.p_ref, f32[16,256]{1,0:T(8,128)S(1)} %collective-permute-done.12.coef_ref, f32[16,256]{1,0:T(8,128)S(1)} %get-tuple-element.33.after_ref.a_ref, f32[16,256]{1,0:T(8,128)S(1)} %solve1.1.coef_ref.b_ref, ...), custom_call_target="tpu_custom_call" | custom-call | flops 5000000000 | bytes 15000000 | tf_op jit(solution)/shard_map/finish/pallas_call | solution.py:494
  (24 shorter events, 3.2 us)
Async XLA Ops:
  0.6 0.7 copy-start
  1.3 20.9 %copy-start.1 = (s32[3,4]{1,0:T(4,128)S(1)}, s32[3,4]{1,0:T(4,128)}, u32[]{:S(2)}) copy-start(s32[3,4]{1,0:T(4,128)} %o_ref.19) | copy-start | bytes 148
  12.0 10.2 %collective-permute-start = (f32[96,256]{1,0:T(8,128)S(1)}, f32[96,256]{1,0:T(8,128)S(1)}, u32[]{:S(2)}, u32[]{:S(2)}) collective-permute-start(f32[96,256]{1,0:T(8,128)S(1)} %get-tuple-element.29.mine_ref), channel_id=1, source_target_pairs={{0,1},{1,0},{2,3},{3,2},{4,5},{5,4},{6,7},{7,6},{8,9},{9,8},{10,11... | collective-permute-start | bytes 294920 | tf_op jit(solution)/shard_map/ppermute | solution.py:522
  26.3 18.1 %collective-permute-start.1 = (f32[768,256]{1,0:T(8,128)S(1)}, f32[768,256]{1,0:T(8,128)S(1)}, u32[]{:S(2)}, u32[]{:S(2)}) collective-permute-start(f32[768,256]{1,0:T(8,128)S(1)} %get-tuple-element.35), channel_id=1, source_target_pairs={{2,4},{6,8},{10,12},{14,16},{18,20},{22,24},{26,28},{30,32},{34,36... | collective-permute-start | bytes 2359304 | tf_op jit(solution)/shard_map/ppermute | solution.py:525
  32.1 12.3 %collective-permute-start.2 = (f32[768,256]{1,0:T(8,128)S(1)}, f32[768,256]{1,0:T(8,128)S(1)}, u32[]{:S(2)}, u32[]{:S(2)}) collective-permute-start(f32[768,256]{1,0:T(8,128)S(1)} %get-tuple-element.39), channel_id=1, source_target_pairs={{0,2},{2,0},{4,6},{6,4},{8,10},{10,8},{12,14},{14,12},{16,18},{18,... | collective-permute-start | bytes 2359304 | tf_op jit(solution)/shard_map/ppermute | solution.py:527
  32.2 20.6 %collective-permute-start.3 = (f32[768,256]{1,0:T(8,128)S(1)}, f32[768,256]{1,0:T(8,128)S(1)}, u32[]{:S(2)}, u32[]{:S(2)}) collective-permute-start(f32[768,256]{1,0:T(8,128)S(1)} %get-tuple-element.37), channel_id=1, source_target_pairs={{2,4},{6,8},{10,12},{14,16},{18,20},{22,24},{26,28},{30,32},{34,36... | collective-permute-start | bytes 2359304 | tf_op jit(solution)/shard_map/ppermute | solution.py:526
  36.8 16.1 %collective-permute-start.4 = (f32[768,256]{1,0:T(8,128)S(1)}, f32[768,256]{1,0:T(8,128)S(1)}, u32[]{:S(2)}, u32[]{:S(2)}) collective-permute-start(f32[768,256]{1,0:T(8,128)S(1)} %get-tuple-element.47), channel_id=1, source_target_pairs={{0,2},{2,0},{4,6},{6,4},{8,10},{10,8},{12,14},{14,12},{16,18},{18,... | collective-permute-start | bytes 2359304 | tf_op jit(solution)/shard_map/ppermute | solution.py:528
  36.9 40.2 %collective-permute-start.7 = (f32[768,256]{1,0:T(8,128)S(1)}, f32[768,256]{1,0:T(8,128)S(1)}, u32[]{:S(2)}, u32[]{:S(2)}) collective-permute-start(f32[768,256]{1,0:T(8,128)S(1)} %get-tuple-element.35), channel_id=1, source_target_pairs={{0,2},{2,0},{4,6},{6,4},{8,10},{10,8},{12,14},{14,12},{16,18},{18,... | collective-permute-start | bytes 2359304 | tf_op jit(solution)/shard_map/ppermute | solution.py:529
  44.4 32.6 %collective-permute-start.8 = (f32[768,256]{1,0:T(8,128)S(1)}, f32[768,256]{1,0:T(8,128)S(1)}, u32[]{:S(2)}, u32[]{:S(2)}) collective-permute-start(f32[768,256]{1,0:T(8,128)S(1)} %get-tuple-element.37), channel_id=1, source_target_pairs={{0,2},{2,0},{4,6},{6,4},{8,10},{10,8},{12,14},{14,12},{16,18},{18,... | collective-permute-start | bytes 2359304 | tf_op jit(solution)/shard_map/ppermute | solution.py:530
  45.9 31.2 %collective-permute-start.6 = (f32[768,256]{1,0:T(8,128)S(1)}, f32[768,256]{1,0:T(8,128)S(1)}, u32[]{:S(2)}, u32[]{:S(2)}) collective-permute-start(f32[768,256]{1,0:T(8,128)S(1)} %get-tuple-element.39), channel_id=1, source_target_pairs={{0,6},{4,10},{8,14},{12,18},{16,22},{20,26},{24,30},{28,34},{32,38... | collective-permute-start | bytes 2359304 | tf_op jit(solution)/shard_map/ppermute | solution.py:533
  56.2 12.8 %collective-permute-start.5 = (f32[96,256]{1,0:T(8,128)S(1)}, f32[96,256]{1,0:T(8,128)S(1)}, u32[]{:S(2)}, u32[]{:S(2)}) collective-permute-start(f32[96,256]{1,0:T(8,128)S(1)} %pairs1.1.after_ref.mine_ref), channel_id=1, source_target_pairs={{0,1},{1,0},{2,3},{3,2},{4,5},{5,4},{6,7},{7,6},{8,9},{9,8},{10,11... | collective-permute-start | bytes 294920 | tf_op jit(solution)/shard_map/ppermute | solution.py:535
  64.0 17.0 %collective-permute-start.10 = (f32[768,256]{1,0:T(8,128)S(1)}, f32[768,256]{1,0:T(8,128)S(1)}, u32[]{:S(2)}, u32[]{:S(2)}) collective-permute-start(f32[768,256]{1,0:T(8,128)S(1)} %get-tuple-element.47), channel_id=1, source_target_pairs={{0,6},{4,10},{8,14},{12,18},{16,22},{20,26},{24,30},{28,34},{32,38... | collective-permute-start | bytes 2359304 | tf_op jit(solution)/shard_map/ppermute | solution.py:538
  70.2 10.4 %collective-permute-start.9 = (f32[16,256]{1,0:T(8,128)S(1)}, f32[16,256]{1,0:T(8,128)S(1)}, u32[]{:S(2)}, u32[]{:S(2)}) collective-permute-start(f32[16,256]{1,0:T(8,128)S(1)} %solve1.1.coef_ref.b_ref), channel_id=1, source_target_pairs={{4,0},{8,4},{12,8},{16,12},{20,16},{24,20},{28,24},{32,28},{36,32}... | collective-permute-start | bytes 49160 | tf_op jit(solution)/shard_map/ppermute | solution.py:540
  80.6 21.1 %collective-permute-start.14 = (f32[768,256]{1,0:T(8,128)S(1)}, f32[768,256]{1,0:T(8,128)S(1)}, u32[]{:S(2)}, u32[]{:S(2)}) collective-permute-start(f32[768,256]{1,0:T(8,128)S(1)} %get-tuple-element.48.za), channel_id=1, source_target_pairs={{0,4},{4,8},{8,12},{12,16},{16,20},{20,24},{24,28},{28,32},{32,36}... | collective-permute-start | bytes 2359304 | tf_op jit(solution)/shard_map/ppermute | solution.py:544
  88.6 8.7 %collective-permute-start.11 = (f32[96,256]{1,0:T(8,128)S(1)}, f32[96,256]{1,0:T(8,128)S(1)}, u32[]{:S(2)}, u32[]{:S(2)}) collective-permute-start(f32[96,256]{1,0:T(8,128)S(1)} %get-tuple-element.50.mine_ref), channel_id=1, source_target_pairs={{0,1},{1,0},{2,3},{3,2},{4,5},{5,4},{6,7},{7,6},{8,9},{9,8},{10,11... | collective-permute-start | bytes 294920 | tf_op jit(solution)/shard_map/ppermute | solution.py:546
  88.7 21.8 %collective-permute-start.15 = (f32[768,256]{1,0:T(8,128)S(1)}, f32[768,256]{1,0:T(8,128)S(1)}, u32[]{:S(2)}, u32[]{:S(2)}) collective-permute-start(f32[768,256]{1,0:T(8,128)S(1)} %get-tuple-element.54.zb), channel_id=1, source_target_pairs={{0,4},{4,8},{8,12},{12,16},{16,20},{20,24},{24,28},{28,32},{32,36}... | collective-permute-start | bytes 2359304 | tf_op jit(solution)/shard_map/ppermute | solution.py:548
  98.3 12.2 %collective-permute-start.12 = (f32[16,256]{1,0:T(8,128)S(1)}, f32[16,256]{1,0:T(8,128)S(1)}, u32[]{:S(2)}, u32[]{:S(2)}) collective-permute-start(f32[16,256]{1,0:T(8,128)S(1)} %solve2.1.coef_ref), channel_id=1, source_target_pairs={{0,4},{4,8},{8,12},{12,16},{16,20},{20,24},{24,28},{28,32},{32,36}... | collective-permute-start | bytes 49160 | tf_op jit(solution)/shard_map/ppermute | solution.py:550
  98.4 12.2 %collective-permute-start.13 = (f32[16,256]{1,0:T(8,128)S(1)}, f32[16,256]{1,0:T(8,128)S(1)}, u32[]{:S(2)}, u32[]{:S(2)}) collective-permute-start(f32[16,256]{1,0:T(8,128)S(1)} %solve2.1.coef_ref), channel_id=1, source_target_pairs={{0,2},{2,0},{4,6},{6,4},{8,10},{10,8},{12,14},{14,12},{16,18},{18,... | collective-permute-start | bytes 49160 | tf_op jit(solution)/shard_map/ppermute | solution.py:551

commit v6 on v5

--- a/solution.py
+++ b/solution.py
@@ -12,7 +12,8 @@
 BF16 = jnp.bfloat16
 W = 256
 H = 128
-LAGS = 96
+LAGS = 56
+WIDE = 96
 VMEM_LIMIT = 24 * 1024 * 1024
 FIRST_LIMIT = 50 * 1024 * 1024
 
@@ -21,24 +22,40 @@
     return (16 * m, 16) if m < 4 else (64 + 8 * (m - 4), 8)
 
 
-def lag_targets(o):
-    t, s = [0], [0]
+def lag_plan():
+    unit = [tuple(int(i == j) for j in range(4)) for i in range(4)]
+    zero = (0, 0, 0, 0)
+
+    def plus(a, b, sign=1):
+        return tuple(x + sign * y for x, y in zip(a, b))
+
+    t, s = [zero], [zero]
     first, second = [0], [1]
-    rows = {}
+    wide = {15: (0, 0, zero), 30: (1, 1, zero)}
     for step in range(4):
         count = 1 << step
         for m in range(count):
             start, _ = group_rows(m)
             place = {3: 0, 2: 8, 1: 12, 0: 14}[step]
             for n in range(count):
-                lag = (o[step] + s[n] - t[m]) & (W - 1)
-                rows[start + place + n] = lag + W * second[n]
+                lag = plus(plus(unit[step], s[n]), t[m], -1)
+                wide[start + place + n] = (first[m], second[n], lag)
         if step < 3:
-            t, s = t + [x + o[step] for x in s], s + [x - o[step] for x in t]
+            t, s = t + [plus(x, unit[step]) for x in s], s + [plus(x, unit[step], -1) for x in t]
             first, second = first + second, second + first
-    rows[15] = 0
-    rows[16 + 14] = W
-    return rows, t, first
+    table = sorted(set(wide.values()))
+    return table, {r: table.index(key) for r, key in wide.items()}, t
+
+
+TABLE_ROWS, USES, BASES = lag_plan()
+UPPER_ROWS = sum(1 for row in TABLE_ROWS if row[0] == 0)
+
+
+def shift_of(coefs, o):
+    total = 0
+    for k, value in zip(coefs, o):
+        total = total + k * value if k else total
+    return total & (W - 1)
 
 
 def split(x):
@@ -59,29 +76,24 @@
 
 
 def build_onehot(o, table_ref):
-    rows, _, _ = lag_targets(o)
-    table_ref[...] = jnp.full((LAGS, 128), -1, jnp.int32)
-    for r, target in rows.items():
-        table_ref[r : r + 1, :] = jnp.full((1, 128), target, jnp.int32)
+    table_ref[...] = jnp.full((LAGS, H), -1, jnp.int32)
+    for r, (_, side, lag) in enumerate(TABLE_ROWS):
+        table_ref[r : r + 1, :] = jnp.full((1, H), shift_of(lag, o) + W * side, jnp.int32)
     table = jnp.concatenate([table_ref[...]] * 4, axis=1)
     return (table == lax.broadcasted_iota(jnp.int32, (LAGS, 2 * W), 1)).astype(F32).astype(BF16)
 
 
-def lag_products(gram, o, onehot, out_ref):
-    _, bases, first = lag_targets(o)
-    diags = {}
+def lag_products(gram, onehot, out_ref):
+    diags = []
     for kind in (0, 1):
         sheets = [skew(gram[kind * W : (kind + 1) * W, side * W : (side + 1) * W]) for side in (0, 1)]
         hi, lo = split(jnp.concatenate(sheets, axis=1))
-        diags[kind] = lax.dot_general(onehot, lo, NT, preferred_element_type=F32) + lax.dot_general(
-            onehot, hi, NT, preferred_element_type=F32
+        diags.append(
+            lax.dot_general(onehot, lo, NT, preferred_element_type=F32)
+            + lax.dot_general(onehot, hi, NT, preferred_element_type=F32)
         )
-    for m in range(8):
-        start, count = group_rows(m)
-        tile = diags[first[m]][start : start + count]
-        if m > 0:
-            tile = pltpu.roll(tile, (-bases[m]) & (W - 1), 1)
-        out_ref[start : start + count, :] = tile
+    row = lax.broadcasted_iota(jnp.int32, (LAGS, W), 0)
+    out_ref[...] = jnp.where(row < UPPER_ROWS, diags[0], diags[1])
 
 
 def gram_of(a, b):
@@ -112,14 +124,24 @@
     return c, s, c * c * upper_sq + cross + s * s * lower_sq, s * s * upper_sq - cross + c * c * lower_sq
 
 
-def angles(lags, o, coef_ref):
+def angles(lags, o, coef_ref, sum_ref, wide_ref):
+    sum_ref[...] = lags
+    for r, place in USES.items():
+        wide_ref[r : r + 1, :] = sum_ref[place : place + 1, :]
+    tiles, last = [], []
+    for m in range(8):
+        start, count = group_rows(m)
+        tile = wide_ref[start : start + count, :]
+        if m > 0:
+            tile = pltpu.roll(tile, (-shift_of(BASES[m], o)) & (W - 1), 1)
+        last.append(tile[0:8])
+        if m < 4:
+            tiles.append(tile[8:16])
     row = lax.broadcasted_iota(jnp.int32, (8, W), 0)
     a = jnp.ones((8, W), F32)
     b = jnp.ones((8, W), F32)
-    upper_sq = lags[15:16]
-    lower_sq = lags[30:31]
-    tiles = [lags[16 * m + 8 : 16 * m + 16] for m in range(4)]
-    last = [lags[group_rows(m)[0] : group_rows(m)[0] + 8] for m in range(8)]
+    upper_sq = tiles[0][7:8]
+    lower_sq = tiles[1][6:7]
     for step in range(4):
         count = 1 << step
         if step == 3:
@@ -176,7 +198,8 @@
 LAG_SHAPE = jax.ShapeDtypeStruct((LAGS, W), F32)
 COEF_SHAPE = jax.ShapeDtypeStruct((16, W), F32)
 ONEHOT_SHAPE = jax.ShapeDtypeStruct((LAGS, 2 * W), BF16)
-TABLE = pltpu.VMEM((LAGS, 128), jnp.int32)
+TABLE = pltpu.VMEM((LAGS, H), jnp.int32)
+LAG_SCRATCH = [pltpu.VMEM((LAGS, W), F32), pltpu.VMEM((WIDE, W), F32)]
 
 
 def tile_rows(rows, most=512):
@@ -266,7 +289,7 @@
         )
         upper_ref[part] = kernel[:, :W]
         lower_ref[part] = kernel[:, W:]
-    lag_products(gram_of(upper_ref[...], lower_ref[...]), o, onehot, lag_ref)
+    lag_products(gram_of(upper_ref[...], lower_ref[...]), onehot, lag_ref)
 
 
 def first(offsets, row_feats, col_feats):
@@ -311,10 +334,10 @@
             go(pl.ds(pl.multiple_of(k * part + i * r, r), r), k, pl.ds(start, r))
 
 
-def turn_first_kernel(o_ref, p_ref, mine_ref, other_ref, a_ref, b_ref, xa, xb, ya, yb, coef_ref):
+def turn_first_kernel(o_ref, p_ref, mine_ref, other_ref, a_ref, b_ref, xa, xb, ya, yb, coef_ref, *lag_refs):
     p = p_ref[0]
     o = offsets_of(o_ref, 0)
-    angles(mine_ref[...] + other_ref[...], o, coef_ref)
+    angles(mine_ref[...] + other_ref[...], o, coef_ref, *lag_refs)
     coef = coef_ref[...]
     keep = ((p & 1) == 1) | (p == 0)
 
@@ -336,6 +359,7 @@
         [SMEM, SMEM] + [VMEM] * 4,
         (VMEM,) * 5,
         (part, part, part, part, COEF_SHAPE),
+        LAG_SCRATCH,
         us=5,
     )(offsets, p, mine, other, a, b)
 
@@ -351,15 +375,15 @@
     )(p, a, b)
 
 
-def pairs_kernel(o_ref, p_ref, hot_ref, gram_ref, a_ref, b_ref, lag_ref):
+def pairs_kernel(p_ref, hot_ref, gram_ref, a_ref, b_ref, lag_ref):
     upper, lower = pick((p_ref[0] & 1) == 0, a_ref[...], b_ref[...])
-    lag_products(gram_ref[...] + gram_of(upper, lower), offsets_of(o_ref, 1), hot_ref[...], lag_ref)
-
-
-def pairs(offsets, p, hot, gram, a, b):
-    return call(
-        pairs_kernel, "pairs1", [SMEM, SMEM] + [VMEM] * 4, VMEM, LAG_SHAPE, us=4
-    )(offsets, p, hot, gram, a, b)
+    lag_products(gram_ref[...] + gram_of(upper, lower), hot_ref[...], lag_ref)
+
+
+def pairs(p, hot, gram, a, b):
+    return call(
+        pairs_kernel, "pairs1", [SMEM] + [VMEM] * 4, VMEM, LAG_SHAPE, us=4
+    )(p, hot, gram, a, b)
 
 
 def turn_second_kernel(o_ref, p_ref, coef_ref, rxa, rxb, sya, syb, za, zb, v_ref):
@@ -410,7 +434,7 @@
     by_parts(q_ref.shape[0], go)
     z = jnp.concatenate([za[...], zb[...]], axis=0)
     upper, lower = pick(core == 0, z, q_ref[...])
-    lag_products(gram_of(upper, lower), offsets_of(o_ref, 2), hot_ref[...], lag_ref)
+    lag_products(gram_of(upper, lower), hot_ref[...], lag_ref)
 
 
 def side(last, offsets, p, hot, coef, sxa, sxb, rya, ryb, za, zb):
@@ -424,8 +448,8 @@
     )(offsets, p, hot, coef, sxa, sxb, rya, ryb, za, zb)
 
 
-def solve_kernel(round_index, o_ref, mine_ref, other_ref, coef_ref):
-    angles(mine_ref[...] + other_ref[...], offsets_of(o_ref, round_index), coef_ref)
+def solve_kernel(round_index, o_ref, mine_ref, other_ref, coef_ref, *lag_refs):
+    angles(mine_ref[...] + other_ref[...], offsets_of(o_ref, round_index), coef_ref, *lag_refs)
 
 
 def solve(round_index, offsets, mine, other):
@@ -435,6 +459,7 @@
         [SMEM] + [VMEM] * 2,
         VMEM,
         COEF_SHAPE,
+        LAG_SCRATCH,
         us=2,
     )(offsets, mine, other)
 
@@ -531,7 +556,7 @@
     gram = pairs_start(p, rxa, sya)
     ya, gram = lax.optimization_barrier((ya, gram))
     rya = lax.ppermute(ya, "blk", lend)
-    lag = pairs(offsets, p, hot, gram, rxb, syb)
+    lag = pairs(p, hot, gram, rxb, syb)
     lag_other = lax.ppermute(lag, "row", across)
     hot = table(2, offsets, lag)
     yb, hot = lax.optimization_barrier((yb, hot))

time: 116 us -> 111 us (0.957)
  waiting for transfers between devices: 31.3 us -> 28.5 us
  starting transfers between devices: 39.9 us -> 38.5 us
    ppermute x3, waiting for transfers between devices: 14.6 us -> 10.5 us  [body(): lag_other = lax.ppermute(lag, 'row', across)]
    ppermute x1, starting transfers between devices: 3.31 us -> 0.82 us  [body(): coef_norm = lax.ppermute(coef_c, 'blk', sibling)]
    ppermute x1, starting transfers between devices: 6.85 us -> 8.6 us  [body(): coef_side = lax.ppermute(coef_b, 'blk', tell)]
  transfers between devices with their start and end apart: 16 -> 16, of which waited for: 6 -> 7; matrix products, arithmetic and copies ran while one was open for 0% -> 0% of each run, Pallas kernels for 20% -> 20%
where the time goes in v6:
time: 111 us
  Pallas kernels  42.2 us (38%)
  starting transfers between devices  38.5 us (35%)
  waiting for transfers between devices  28.5 us (26%)
    ppermute x3, starting transfers between devices, body(): lag_other = lax.ppermute(lag, 'row', across)  13.8 us
    pallas_call x1, Pallas kernels, first(): call(first_kernel, 'first', [ANY, ANY, ANY], (VMEM, VMEM, VMEM), (block(r...  10.6 us
    ppermute x3, waiting for transfers between devices, body(): lag_other = lax.ppermute(lag, 'row', across)  10.5 us
    ppermute x1, starting transfers between devices, body(): coef_side = lax.ppermute(coef_b, 'blk', tell)  8.6 us
    pallas_call x1, Pallas kernels, side(): call(functools.partial(side_kernel, last), 'side', [SMEM, SMEM] + [VMEM]...  7.56 us
    ppermute x1, waiting for transfers between devices, body(): rxa = lax.ppermute(xa, 'blk', meet)  7.03 us
    ppermute x1, starting transfers between devices, body(): rxa = lax.ppermute(xa, 'blk', meet)  5.98 us
    ppermute x1, waiting for transfers between devices, body(): coef_got = lax.ppermute(coef_c, 'blk', deal)  5.64 us
  transfers between devices with their start and end apart: 16, of which 7 were waited for; matrix products, arithmetic and copies ran while one was open for 0% of the time, Pallas kernels for 20%

profile of v6, /device:TPU:4, one launch (start us, length us, event | category | flops | bytes accessed | tf_op | source)
XLA Modules:
  0.0 110.9 jit_solution(15778353747032322319)
XLA Ops:
  1.3 10.6 %first.1 = (f32[1536,256]{1,0:T(8,128)S(1)}, f32[1536,256]{1,0:T(8,128)S(1)}, f32[56,256]{1,0:T(8,128)S(1)}) custom-call(s32[3,4]{1,0:T(4,128)S(1)} %copy-done, bf16[1536,2048]{1,0:T(8,128)(2,1)} %rows_hbm.1, bf16[512,2048]{1,0:T(8,128)(2,1)} %cols_hbm.1), custom_call_target="tpu_custom_call" | custom-call | flops 10000000000 | bytes 30000000 | tf_op jit(solution)/shard_map/first/pallas_call | solution.py:297
  11.9 7.3 %collective-permute-start = (f32[56,256]{1,0:T(8,128)S(1)}, f32[56,256]{1,0:T(8,128)S(1)}, u32[]{:S(2)}, u32[]{:S(2)}) collective-permute-start(f32[56,256]{1,0:T(8,128)S(1)} %get-tuple-element.29.mine_ref), channel_id=1, source_target_pairs={{0,1},{1,0},{2,3},{3,2},{4,5},{5,4},{6,7},{7,6},{8,9},{9,8},{10,11... | collective-permute-start | bytes 172040 | tf_op jit(solution)/shard_map/ppermute | solution.py:547
  19.2 2.2 %collective-permute-done.other_ref = f32[56,256]{1,0:T(8,128)S(1)} collective-permute-done((f32[56,256]{1,0:T(8,128)S(1)}, f32[56,256]{1,0:T(8,128)S(1)}, u32[]{:S(2)}, u32[]{:S(2)}) %collective-permute-start) | collective-permute-done | bytes 57376 | tf_op jit(solution)/shard_map/ppermute | solution.py:547
  21.4 4.2 %turn0.1 = (f32[768,256]{1,0:T(8,128)S(1)}, f32[768,256]{1,0:T(8,128)S(1)}, f32[768,256]{1,0:T(8,128)S(1)}, f32[768,256]{1,0:T(8,128)S(1)}, f32[16,256]{1,0:T(8,128)S(1)}) custom-call(s32[3,4]{1,0:T(4,128)S(1)} %copy-done.1, s32[1]{0:T(128)} %bitcast.p_ref, f32[56,256]{1,0:T(8,128)S(1)} %get-tuple-element.29.mine_ref, ...), custom_call_target="tpu_custom_call" | custom-call | flops 5000000000 | bytes 15000000 | tf_op jit(solution)/shard_map/turn0/pallas_call | solution.py:356
  25.5 6.0 %collective-permute-start.1 = (f32[768,256]{1,0:T(8,128)S(1)}, f32[768,256]{1,0:T(8,128)S(1)}, u32[]{:S(2)}, u32[]{:S(2)}) collective-permute-start(f32[768,256]{1,0:T(8,128)S(1)} %get-tuple-element.35), channel_id=1, source_target_pairs={{2,4},{6,8},{10,12},{14,16},{18,20},{22,24},{26,28},{30,32},{34,36... | collective-permute-start | bytes 2359304 | tf_op jit(solution)/shard_map/ppermute | solution.py:550
  31.6 4.4 %collective-permute-start.3 = (f32[768,256]{1,0:T(8,128)S(1)}, f32[768,256]{1,0:T(8,128)S(1)}, u32[]{:S(2)}, u32[]{:S(2)}) collective-permute-start(f32[768,256]{1,0:T(8,128)S(1)} %get-tuple-element.37), channel_id=1, source_target_pairs={{2,4},{6,8},{10,12},{14,16},{18,20},{22,24},{26,28},{30,32},{34,36... | collective-permute-start | bytes 2359304 | tf_op jit(solution)/shard_map/ppermute | solution.py:551
  36.6 7.0 %collective-permute-done.1.a_ref.rxa = f32[768,256]{1,0:T(8,128)S(1)} collective-permute-done((f32[768,256]{1,0:T(8,128)S(1)}, f32[768,256]{1,0:T(8,128)S(1)}, u32[]{:S(2)}, u32[]{:S(2)}) %collective-permute-start.1) | collective-permute-done | bytes 786464 | tf_op jit(solution)/shard_map/ppermute | solution.py:550
  43.7 1.5 %pairs0.1.gram_ref = f32[512,512]{1,0:T(8,128)S(1)} custom-call(s32[1]{0:T(128)} %bitcast.p_ref, f32[768,256]{1,0:T(8,128)S(1)} %collective-permute-done.1.a_ref.rxa, f32[768,256]{1,0:T(8,128)S(1)} %collective-permute-done.2.b_ref.sya), custom_call_target="tpu_custom_call" | custom-call | flops 3000000000 | bytes 9000000 | tf_op jit(solution)/shard_map/pairs0/pallas_call | solution.py:373
  45.1 1.9 %collective-permute-start.6 = (f32[768,256]{1,0:T(8,128)S(1)}, f32[768,256]{1,0:T(8,128)S(1)}, u32[]{:S(2)}, u32[]{:S(2)}) collective-permute-start(f32[768,256]{1,0:T(8,128)S(1)} %get-tuple-element.39), channel_id=1, source_target_pairs={{0,6},{4,10},{8,14},{12,18},{16,22},{20,26},{24,30},{28,34},{32,38... | collective-permute-start | bytes 2359304 | tf_op jit(solution)/shard_map/ppermute | solution.py:558
  47.7 4.4 %collective-permute-done.3.a_ref.rxb = f32[768,256]{1,0:T(8,128)S(1)} collective-permute-done((f32[768,256]{1,0:T(8,128)S(1)}, f32[768,256]{1,0:T(8,128)S(1)}, u32[]{:S(2)}, u32[]{:S(2)}) %collective-permute-start.3) | collective-permute-done | bytes 786464 | tf_op jit(solution)/shard_map/ppermute | solution.py:551
  52.1 2.8 %pairs1.1.after_ref.mine_ref = f32[56,256]{1,0:T(8,128)S(1)} custom-call(s32[1]{0:T(128)} %bitcast.p_ref, bf16[56,512]{1,0:T(8,128)(2,1)S(1)} %table1.1.hot_ref, f32[512,512]{1,0:T(8,128)S(1)} %pairs0.1.gram_ref, f32[768,256]{1,0:T(8,128)S(1)} %collective-permute-done.3.a_ref.rxb, f32[768,256]{1,0:T(8,128)S(1)} %collective-permute-done.4.b_ref.syb), custom_call_target="tpu_custom_call" | custom-call | flops 4000000000 | bytes 12000000 | tf_op jit(solution)/shard_map/pairs1/pallas_call | solution.py:384
  54.9 6.4 %collective-permute-start.5 = (f32[56,256]{1,0:T(8,128)S(1)}, f32[56,256]{1,0:T(8,128)S(1)}, u32[]{:S(2)}, u32[]{:S(2)}) collective-permute-start(f32[56,256]{1,0:T(8,128)S(1)} %pairs1.1.after_ref.mine_ref), channel_id=1, source_target_pairs={{0,1},{1,0},{2,3},{3,2},{4,5},{5,4},{6,7},{7,6},{8,9},{9,8},{10,11... | collective-permute-start | bytes 172040 | tf_op jit(solution)/shard_map/ppermute | solution.py:560
  61.9 1.9 %collective-permute-start.10 = (f32[768,256]{1,0:T(8,128)S(1)}, f32[768,256]{1,0:T(8,128)S(1)}, u32[]{:S(2)}, u32[]{:S(2)}) collective-permute-start(f32[768,256]{1,0:T(8,128)S(1)} %get-tuple-element.47), channel_id=1, source_target_pairs={{0,6},{4,10},{8,14},{12,18},{16,22},{20,26},{24,30},{28,34},{32,38... | collective-permute-start | bytes 2359304 | tf_op jit(solution)/shard_map/ppermute | solution.py:563
  64.1 1.2 %solve1.1.coef_ref.b_ref = f32[16,256]{1,0:T(8,128)S(1)} custom-call(s32[3,4]{1,0:T(4,128)S(1)} %copy-done.1, f32[56,256]{1,0:T(8,128)S(1)} %pairs1.1.after_ref.mine_ref, f32[56,256]{1,0:T(8,128)S(1)} %collective-permute-done.5.other_ref), custom_call_target="tpu_custom_call" | custom-call | flops 2000000000 | bytes 6000000 | tf_op jit(solution)/shard_map/solve1/pallas_call | solution.py:456
  65.3 8.6 %collective-permute-start.9 = (f32[16,256]{1,0:T(8,128)S(1)}, f32[16,256]{1,0:T(8,128)S(1)}, u32[]{:S(2)}, u32[]{:S(2)}) collective-permute-start(f32[16,256]{1,0:T(8,128)S(1)} %solve1.1.coef_ref.b_ref), channel_id=1, source_target_pairs={{4,0},{8,4},{12,8},{16,12},{20,16},{24,20},{28,24},{32,28},{36,32}... | collective-permute-start | bytes 49160 | tf_op jit(solution)/shard_map/ppermute | solution.py:565
  73.9 3.6 %turn1.1 = (f32[768,256]{1,0:T(8,128)S(1)}, f32[768,256]{1,0:T(8,128)S(1)}, f32[1536,256]{1,0:T(8,128)S(1)}) custom-call(s32[3,4]{1,0:T(4,128)S(1)} %copy-done.1, s32[1]{0:T(128)} %bitcast.p_ref, f32[16,256]{1,0:T(8,128)S(1)} %solve1.1.coef_ref.b_ref, f32[768,256]{1,0:T(8,128)S(1)} %collective-permute-done.1.a_ref.rxa, ...), custom_call_target="tpu_custom_call" | custom-call | flops 40000000000 | bytes 120000000 | tf_op jit(solution)/shard_map/turn1/pallas_call | solution.py:408
  77.8 7.6 %side.1 = (f32[1536,256]{1,0:T(8,128)S(1)}, f32[56,256]{1,0:T(8,128)S(1)}) custom-call(s32[3,4]{1,0:T(4,128)S(1)} %copy-done.1, s32[1]{0:T(128)} %bitcast.p_ref, bf16[56,512]{1,0:T(8,128)(2,1)S(1)} %table2.1.hot_ref, f32[16,256]{1,0:T(8,128)S(1)} %collective-permute-done.9.coef_ref, f32[768,256]{1,0:T(8,128)S(1)} %collective-permute-done.7.sxa, ...), custom_call_target="tpu_custom_call" | custom-call | flops 8000000000 | bytes 24000000 | tf_op jit(solution)/shard_map/side/pallas_call | solution.py:441
  85.6 8.0 %collective-permute-done.11.other_ref = f32[56,256]{1,0:T(8,128)S(1)} collective-permute-done((f32[56,256]{1,0:T(8,128)S(1)}, f32[56,256]{1,0:T(8,128)S(1)}, u32[]{:S(2)}, u32[]{:S(2)}) %collective-permute-start.11) | collective-permute-done | bytes 57376 | tf_op jit(solution)/shard_map/ppermute | solution.py:571
  93.6 1.2 %solve2.1.coef_ref = f32[16,256]{1,0:T(8,128)S(1)} custom-call(s32[3,4]{1,0:T(4,128)S(1)} %copy-done.1, f32[56,256]{1,0:T(8,128)S(1)} %get-tuple-element.50.mine_ref, f32[56,256]{1,0:T(8,128)S(1)} %collective-permute-done.11.other_ref), custom_call_target="tpu_custom_call" | custom-call | flops 2000000000 | bytes 6000000 | tf_op jit(solution)/shard_map/solve2/pallas_call | solution.py:456
  94.8 0.8 collective-permute-start.13
  95.6 0.9 collective-permute-done.14.ra
  96.5 3.6 %own.1.own_ref = f32[1536,256]{1,0:T(8,128)S(1)} custom-call(s32[3,4]{1,0:T(4,128)S(1)} %copy-done.1, s32[1]{0:T(128)} %bitcast.p_ref, f32[16,256]{1,0:T(8,128)S(1)} %solve2.1.coef_ref, f32[768,256]{1,0:T(8,128)S(1)} %get-tuple-element.48.za, f32[768,256]{1,0:T(8,128)S(1)} %get-tuple-element.54.zb, f32[1536,256]{1,0:T(8,128)S(1)} %get-tuple-element.52.q_ref), custom_call_target="tpu_custom_call" | custom-call | flops 40000000000 | bytes 120000000 | tf_op jit(solution)/shard_map/own/pallas_call | solution.py:483
  100.1 5.6 %collective-permute-done.12.coef_ref = f32[16,256]{1,0:T(8,128)S(1)} collective-permute-done((f32[16,256]{1,0:T(8,128)S(1)}, f32[16,256]{1,0:T(8,128)S(1)}, u32[]{:S(2)}, u32[]{:S(2)}) %collective-permute-start.12) | collective-permute-done | bytes 16416 | tf_op jit(solution)/shard_map/ppermute | solution.py:575
  105.7 5.0 %finish.1 = (f32[2,1536,256]{2,1,0:T(8,128)}, f32[3,2,256]{2,1,0:T(2,128)}) custom-call(s32[3,4]{1,0:T(4,128)S(1)} %copy-done.1, s32[1]{0:T(128)} %bitcast.p_ref, f32[16,256]{1,0:T(8,128)S(1)} %collective-permute-done.12.coef_ref, f32[16,256]{1,0:T(8,128)S(1)} %get-tuple-element.33.after_ref.a_ref, f32[16,256]{1,0:T(8,128)S(1)} %solve1.1.coef_ref.b_ref, ...), custom_call_target="tpu_custom_call" | custom-call | flops 5000000000 | bytes 15000000 | tf_op jit(solution)/shard_map/finish/pallas_call | solution.py:519
  (24 shorter events, 3.5 us)
Async XLA Ops:
  0.6 0.7 copy-start
  1.3 20.1 %copy-start.1 = (s32[3,4]{1,0:T(4,128)S(1)}, s32[3,4]{1,0:T(4,128)}, u32[]{:S(2)}) copy-start(s32[3,4]{1,0:T(4,128)} %o_ref.17) | copy-start | bytes 148
  11.9 9.4 %collective-permute-start = (f32[56,256]{1,0:T(8,128)S(1)}, f32[56,256]{1,0:T(8,128)S(1)}, u32[]{:S(2)}, u32[]{:S(2)}) collective-permute-start(f32[56,256]{1,0:T(8,128)S(1)} %get-tuple-element.29.mine_ref), channel_id=1, source_target_pairs={{0,1},{1,0},{2,3},{3,2},{4,5},{5,4},{6,7},{7,6},{8,9},{9,8},{10,11... | collective-permute-start | bytes 172040 | tf_op jit(solution)/shard_map/ppermute | solution.py:547
  25.5 18.1 %collective-permute-start.1 = (f32[768,256]{1,0:T(8,128)S(1)}, f32[768,256]{1,0:T(8,128)S(1)}, u32[]{:S(2)}, u32[]{:S(2)}) collective-permute-start(f32[768,256]{1,0:T(8,128)S(1)} %get-tuple-element.35), channel_id=1, source_target_pairs={{2,4},{6,8},{10,12},{14,16},{18,20},{22,24},{26,28},{30,32},{34,36... | collective-permute-start | bytes 2359304 | tf_op jit(solution)/shard_map/ppermute | solution.py:550
  31.5 12.1 %collective-permute-start.2 = (f32[768,256]{1,0:T(8,128)S(1)}, f32[768,256]{1,0:T(8,128)S(1)}, u32[]{:S(2)}, u32[]{:S(2)}) collective-permute-start(f32[768,256]{1,0:T(8,128)S(1)} %get-tuple-element.39), channel_id=1, source_target_pairs={{0,2},{2,0},{4,6},{6,4},{8,10},{10,8},{12,14},{14,12},{16,18},{18,... | collective-permute-start | bytes 2359304 | tf_op jit(solution)/shard_map/ppermute | solution.py:552
  31.6 20.5 %collective-permute-start.3 = (f32[768,256]{1,0:T(8,128)S(1)}, f32[768,256]{1,0:T(8,128)S(1)}, u32[]{:S(2)}, u32[]{:S(2)}) collective-permute-start(f32[768,256]{1,0:T(8,128)S(1)} %get-tuple-element.37), channel_id=1, source_target_pairs={{2,4},{6,8},{10,12},{14,16},{18,20},{22,24},{26,28},{30,32},{34,36... | collective-permute-start | bytes 2359304 | tf_op jit(solution)/shard_map/ppermute | solution.py:551
  36.0 16.1 %collective-permute-start.4 = (f32[768,256]{1,0:T(8,128)S(1)}, f32[768,256]{1,0:T(8,128)S(1)}, u32[]{:S(2)}, u32[]{:S(2)}) collective-permute-start(f32[768,256]{1,0:T(8,128)S(1)} %get-tuple-element.47), channel_id=1, source_target_pairs={{0,2},{2,0},{4,6},{6,4},{8,10},{10,8},{12,14},{14,12},{16,18},{18,... | collective-permute-start | bytes 2359304 | tf_op jit(solution)/shard_map/ppermute | solution.py:553
  36.1 37.8 %collective-permute-start.7 = (f32[768,256]{1,0:T(8,128)S(1)}, f32[768,256]{1,0:T(8,128)S(1)}, u32[]{:S(2)}, u32[]{:S(2)}) collective-permute-start(f32[768,256]{1,0:T(8,128)S(1)} %get-tuple-element.35), channel_id=1, source_target_pairs={{0,2},{2,0},{4,6},{6,4},{8,10},{10,8},{12,14},{14,12},{16,18},{18,... | collective-permute-start | bytes 2359304 | tf_op jit(solution)/shard_map/ppermute | solution.py:554
  43.7 30.3 %collective-permute-start.8 = (f32[768,256]{1,0:T(8,128)S(1)}, f32[768,256]{1,0:T(8,128)S(1)}, u32[]{:S(2)}, u32[]{:S(2)}) collective-permute-start(f32[768,256]{1,0:T(8,128)S(1)} %get-tuple-element.37), channel_id=1, source_target_pairs={{0,2},{2,0},{4,6},{6,4},{8,10},{10,8},{12,14},{14,12},{16,18},{18,... | collective-permute-start | bytes 2359304 | tf_op jit(solution)/shard_map/ppermute | solution.py:555
  45.1 28.8 %collective-permute-start.6 = (f32[768,256]{1,0:T(8,128)S(1)}, f32[768,256]{1,0:T(8,128)S(1)}, u32[]{:S(2)}, u32[]{:S(2)}) collective-permute-start(f32[768,256]{1,0:T(8,128)S(1)} %get-tuple-element.39), channel_id=1, source_target_pairs={{0,6},{4,10},{8,14},{12,18},{16,22},{20,26},{24,30},{28,34},{32,38... | collective-permute-start | bytes 2359304 | tf_op jit(solution)/shard_map/ppermute | solution.py:558
  54.9 9.3 %collective-permute-start.5 = (f32[56,256]{1,0:T(8,128)S(1)}, f32[56,256]{1,0:T(8,128)S(1)}, u32[]{:S(2)}, u32[]{:S(2)}) collective-permute-start(f32[56,256]{1,0:T(8,128)S(1)} %pairs1.1.after_ref.mine_ref), channel_id=1, source_target_pairs={{0,1},{1,0},{2,3},{3,2},{4,5},{5,4},{6,7},{7,6},{8,9},{9,8},{10,11... | collective-permute-start | bytes 172040 | tf_op jit(solution)/shard_map/ppermute | solution.py:560
  61.9 16.0 %collective-permute-start.10 = (f32[768,256]{1,0:T(8,128)S(1)}, f32[768,256]{1,0:T(8,128)S(1)}, u32[]{:S(2)}, u32[]{:S(2)}) collective-permute-start(f32[768,256]{1,0:T(8,128)S(1)} %get-tuple-element.47), channel_id=1, source_target_pairs={{0,6},{4,10},{8,14},{12,18},{16,22},{20,26},{24,30},{28,34},{32,38... | collective-permute-start | bytes 2359304 | tf_op jit(solution)/shard_map/ppermute | solution.py:563
  65.3 12.2 %collective-permute-start.9 = (f32[16,256]{1,0:T(8,128)S(1)}, f32[16,256]{1,0:T(8,128)S(1)}, u32[]{:S(2)}, u32[]{:S(2)}) collective-permute-start(f32[16,256]{1,0:T(8,128)S(1)} %solve1.1.coef_ref.b_ref), channel_id=1, source_target_pairs={{4,0},{8,4},{12,8},{16,12},{20,16},{24,20},{28,24},{32,28},{36,32}... | collective-permute-start | bytes 49160 | tf_op jit(solution)/shard_map/ppermute | solution.py:565
  77.5 19.0 %collective-permute-start.14 = (f32[768,256]{1,0:T(8,128)S(1)}, f32[768,256]{1,0:T(8,128)S(1)}, u32[]{:S(2)}, u32[]{:S(2)}) collective-permute-start(f32[768,256]{1,0:T(8,128)S(1)} %get-tuple-element.48.za), channel_id=1, source_target_pairs={{0,4},{4,8},{8,12},{12,16},{16,20},{20,24},{24,28},{28,32},{32,36}... | collective-permute-start | bytes 2359304 | tf_op jit(solution)/shard_map/ppermute | solution.py:569
  85.4 8.2 %collective-permute-start.11 = (f32[56,256]{1,0:T(8,128)S(1)}, f32[56,256]{1,0:T(8,128)S(1)}, u32[]{:S(2)}, u32[]{:S(2)}) collective-permute-start(f32[56,256]{1,0:T(8,128)S(1)} %get-tuple-element.50.mine_ref), channel_id=1, source_target_pairs={{0,1},{1,0},{2,3},{3,2},{4,5},{5,4},{6,7},{7,6},{8,9},{9,8},{10,11... | collective-permute-start | bytes 172040 | tf_op jit(solution)/shard_map/ppermute | solution.py:571
  85.5 20.2 %collective-permute-start.15 = (f32[768,256]{1,0:T(8,128)S(1)}, f32[768,256]{1,0:T(8,128)S(1)}, u32[]{:S(2)}, u32[]{:S(2)}) collective-permute-start(f32[768,256]{1,0:T(8,128)S(1)} %get-tuple-element.54.zb), channel_id=1, source_target_pairs={{0,4},{4,8},{8,12},{12,16},{16,20},{20,24},{24,28},{28,32},{32,36}... | collective-permute-start | bytes 2359304 | tf_op jit(solution)/shard_map/ppermute | solution.py:573
  94.8 11.0 %collective-permute-start.12 = (f32[16,256]{1,0:T(8,128)S(1)}, f32[16,256]{1,0:T(8,128)S(1)}, u32[]{:S(2)}, u32[]{:S(2)}) collective-permute-start(f32[16,256]{1,0:T(8,128)S(1)} %solve2.1.coef_ref), channel_id=1, source_target_pairs={{0,4},{4,8},{8,12},{12,16},{16,20},{20,24},{24,28},{28,32},{32,36}... | collective-permute-start | bytes 49160 | tf_op jit(solution)/shard_map/ppermute | solution.py:575
  94.8 10.9 %collective-permute-start.13 = (f32[16,256]{1,0:T(8,128)S(1)}, f32[16,256]{1,0:T(8,128)S(1)}, u32[]{:S(2)}, u32[]{:S(2)}) collective-permute-start(f32[16,256]{1,0:T(8,128)S(1)} %solve2.1.coef_ref), channel_id=1, source_target_pairs={{0,2},{2,0},{4,6},{6,4},{8,10},{10,8},{12,14},{14,12},{16,18},{18,... | collective-permute-start | bytes 49160 | tf_op jit(solution)/shard_map/ppermute | solution.py:576

commit v7 on v6

--- a/solution.py
+++ b/solution.py
@@ -103,6 +103,13 @@
         + lax.dot_general(lo, hi, TN, preferred_element_type=F32)
         + lax.dot_general(hi, hi, TN, preferred_element_type=F32)
     )
+
+
+def gram_whole(a, b):
+    hi, lo = split(jnp.concatenate([a, b], axis=1))
+    parts = lax.dot_general(hi, jnp.concatenate([hi, lo], axis=1), TN, preferred_element_type=F32)
+    mixed = parts[:, 2 * W :]
+    return parts[:, : 2 * W] + (mixed + jnp.transpose(mixed))
 
 
 def angle(g, upper_sq, lower_sq):
@@ -289,7 +296,7 @@
         )
         upper_ref[part] = kernel[:, :W]
         lower_ref[part] = kernel[:, W:]
-    lag_products(gram_of(upper_ref[...], lower_ref[...]), onehot, lag_ref)
+    lag_products(gram_whole(upper_ref[...], lower_ref[...]), onehot, lag_ref)
 
 
 def first(offsets, row_feats, col_feats):
@@ -422,19 +429,24 @@
     coef = coef_ref[...]
     near_end = (p == 1) | (p == last - 1)
     part = za.shape[0]
-
-    def go(rows, k, rows_part):
-        upper, lower = pick_halves(
-            (core == 0) != near_end, read((sxa, sxb)[k], rows_part), read((rya, ryb)[k], rows_part)
-        )
-        upper, lower = rotate(upper, lower, coef, o)
-        wanted, _ = pick_halves((core == 1) | (p == last - 1), upper, lower)
-        write(q_ref, rows, wanted)
-
-    by_parts(q_ref.shape[0], go)
-    z = jnp.concatenate([za[...], zb[...]], axis=0)
-    upper, lower = pick(core == 0, z, q_ref[...])
-    lag_products(gram_of(upper, lower), hot_ref[...], lag_ref)
+    r = tile_rows(part, 384)
+    parts, pending = None, None
+    for t in range(2 * part // r + 1):
+        ready, pending = pending, None
+        if t < 2 * part // r:
+            k = t * r // part
+            rows = slice(t * r - k * part, t * r - k * part + r)
+            upper, lower = pick_halves(
+                (core == 0) != near_end, read((sxa, sxb)[k], rows), read((rya, ryb)[k], rows)
+            )
+            upper, lower = rotate(upper, lower, coef, o)
+            wanted, _ = pick_halves((core == 1) | (p == last - 1), upper, lower)
+            write(q_ref, slice(t * r, (t + 1) * r), wanted)
+            pending = (za, zb)[k][rows], jnp.concatenate(wanted, axis=1)
+        if ready is not None:
+            added = gram_of(*pick(core == 0, *ready))
+            parts = added if parts is None else parts + added
+    lag_products(parts, hot_ref[...], lag_ref)
 
 
 def side(last, offsets, p, hot, coef, sxa, sxb, rya, ryb, za, zb):
@@ -573,9 +585,10 @@
     rb = lax.ppermute(later, "blk", deal)
     coef_c = solve(2, offsets, lag, lag_other)
     coef_got = lax.ppermute(coef_c, "blk", deal)
-    coef_norm = lax.ppermute(coef_c, "blk", sibling)
     coef_own, ra = lax.optimization_barrier((coef_c, ra))
     own_block = own(offsets, p, coef_own, za, zb, q)
+    coef_c, own_block = lax.optimization_barrier((coef_c, own_block))
+    coef_norm = lax.ppermute(coef_c, "blk", sibling)
     return finish(n - 1, row_total, offsets, p, coef_got, (coef_a, coef_b, coef_norm), own_block, ra, rb, v)
 
 

time: 111 us -> 111 us (level)
  waiting for transfers between devices: 28.5 us -> 29.7 us
    ppermute x1, waiting for transfers between devices: 0.88 us -> 2.52 us  [body(): ra = lax.ppermute(za, 'blk', deal)]
where the time goes in v7:
time: 111 us
  Pallas kernels  41.1 us (37%)
  starting transfers between devices  38 us (34%)
  waiting for transfers between devices  29.7 us (27%)
    ppermute x3, starting transfers between devices, body(): lag_other = lax.ppermute(lag, 'row', across)  13.8 us
    ppermute x3, waiting for transfers between devices, body(): lag_other = lax.ppermute(lag, 'row', across)  10.5 us
    pallas_call x1, Pallas kernels, first(): call(first_kernel, 'first', [ANY, ANY, ANY], (VMEM, VMEM, VMEM), (block(r...  10.3 us
    ppermute x1, starting transfers between devices, body(): coef_side = lax.ppermute(coef_b, 'blk', tell)  8.6 us
    ppermute x1, waiting for transfers between devices, body(): rxa = lax.ppermute(xa, 'blk', meet)  7.03 us
    pallas_call x1, Pallas kernels, side(): call(functools.partial(side_kernel, last), 'side', [SMEM, SMEM] + [VMEM]...  6.75 us
    ppermute x1, starting transfers between devices, body(): rxa = lax.ppermute(xa, 'blk', meet)  5.98 us
    ppermute x1, waiting for transfers between devices, body(): coef_got = lax.ppermute(coef_c, 'blk', deal)  5.27 us
  transfers between devices with their start and end apart: 16, of which 7 were waited for; matrix products, arithmetic and copies ran while one was open for 0% of the time, Pallas kernels for 20%

profile of v7, /device:TPU:4, one launch (start us, length us, event | category | flops | bytes accessed | tf_op | source)
XLA Modules:
  0.0 110.6 jit_solution(5959134682686920204)
XLA Ops:
  0.6 0.7 copy-done
  1.3 10.3 %first.1 = (f32[1536,256]{1,0:T(8,128)S(1)}, f32[1536,256]{1,0:T(8,128)S(1)}, f32[56,256]{1,0:T(8,128)S(1)}) custom-call(s32[3,4]{1,0:T(4,128)S(1)} %copy-done, bf16[1536,2048]{1,0:T(8,128)(2,1)} %rows_hbm.1, bf16[512,2048]{1,0:T(8,128)(2,1)} %cols_hbm.1), custom_call_target="tpu_custom_call" | custom-call | flops 10000000000 | bytes 30000000 | tf_op jit(solution)/shard_map/first/pallas_call | solution.py:304
  11.6 7.3 %collective-permute-start = (f32[56,256]{1,0:T(8,128)S(1)}, f32[56,256]{1,0:T(8,128)S(1)}, u32[]{:S(2)}, u32[]{:S(2)}) collective-permute-start(f32[56,256]{1,0:T(8,128)S(1)} %get-tuple-element.31.mine_ref), channel_id=1, source_target_pairs={{0,1},{1,0},{2,3},{3,2},{4,5},{5,4},{6,7},{7,6},{8,9},{9,8},{10,11... | collective-permute-start | bytes 172040 | tf_op jit(solution)/shard_map/ppermute | solution.py:559
  18.9 2.2 %collective-permute-done.other_ref = f32[56,256]{1,0:T(8,128)S(1)} collective-permute-done((f32[56,256]{1,0:T(8,128)S(1)}, f32[56,256]{1,0:T(8,128)S(1)}, u32[]{:S(2)}, u32[]{:S(2)}) %collective-permute-start) | collective-permute-done | bytes 57376 | tf_op jit(solution)/shard_map/ppermute | solution.py:559
  21.1 4.2 %turn0.1 = (f32[768,256]{1,0:T(8,128)S(1)}, f32[768,256]{1,0:T(8,128)S(1)}, f32[768,256]{1,0:T(8,128)S(1)}, f32[768,256]{1,0:T(8,128)S(1)}, f32[16,256]{1,0:T(8,128)S(1)}) custom-call(s32[3,4]{1,0:T(4,128)S(1)} %copy-done.1, s32[1]{0:T(128)} %bitcast.p_ref, f32[56,256]{1,0:T(8,128)S(1)} %get-tuple-element.31.mine_ref, ...), custom_call_target="tpu_custom_call" | custom-call | flops 5000000000 | bytes 15000000 | tf_op jit(solution)/shard_map/turn0/pallas_call | solution.py:363
  25.2 6.0 %collective-permute-start.1 = (f32[768,256]{1,0:T(8,128)S(1)}, f32[768,256]{1,0:T(8,128)S(1)}, u32[]{:S(2)}, u32[]{:S(2)}) collective-permute-start(f32[768,256]{1,0:T(8,128)S(1)} %get-tuple-element.37), channel_id=1, source_target_pairs={{2,4},{6,8},{10,12},{14,16},{18,20},{22,24},{26,28},{30,32},{34,36... | collective-permute-start | bytes 2359304 | tf_op jit(solution)/shard_map/ppermute | solution.py:562
  31.3 4.4 %collective-permute-start.3 = (f32[768,256]{1,0:T(8,128)S(1)}, f32[768,256]{1,0:T(8,128)S(1)}, u32[]{:S(2)}, u32[]{:S(2)}) collective-permute-start(f32[768,256]{1,0:T(8,128)S(1)} %get-tuple-element.39), channel_id=1, source_target_pairs={{2,4},{6,8},{10,12},{14,16},{18,20},{22,24},{26,28},{30,32},{34,36... | collective-permute-start | bytes 2359304 | tf_op jit(solution)/shard_map/ppermute | solution.py:563
  36.3 7.0 %collective-permute-done.1.a_ref.rxa = f32[768,256]{1,0:T(8,128)S(1)} collective-permute-done((f32[768,256]{1,0:T(8,128)S(1)}, f32[768,256]{1,0:T(8,128)S(1)}, u32[]{:S(2)}, u32[]{:S(2)}) %collective-permute-start.1) | collective-permute-done | bytes 786464 | tf_op jit(solution)/shard_map/ppermute | solution.py:562
  43.3 1.5 %pairs0.1.gram_ref = f32[512,512]{1,0:T(8,128)S(1)} custom-call(s32[1]{0:T(128)} %bitcast.p_ref, f32[768,256]{1,0:T(8,128)S(1)} %collective-permute-done.1.a_ref.rxa, f32[768,256]{1,0:T(8,128)S(1)} %collective-permute-done.2.b_ref.sya), custom_call_target="tpu_custom_call" | custom-call | flops 3000000000 | bytes 9000000 | tf_op jit(solution)/shard_map/pairs0/pallas_call | solution.py:380
  44.8 1.9 %collective-permute-start.6 = (f32[768,256]{1,0:T(8,128)S(1)}, f32[768,256]{1,0:T(8,128)S(1)}, u32[]{:S(2)}, u32[]{:S(2)}) collective-permute-start(f32[768,256]{1,0:T(8,128)S(1)} %get-tuple-element.41), channel_id=1, source_target_pairs={{0,6},{4,10},{8,14},{12,18},{16,22},{20,26},{24,30},{28,34},{32,38... | collective-permute-start | bytes 2359304 | tf_op jit(solution)/shard_map/ppermute | solution.py:570
  47.4 4.4 %collective-permute-done.3.a_ref.rxb = f32[768,256]{1,0:T(8,128)S(1)} collective-permute-done((f32[768,256]{1,0:T(8,128)S(1)}, f32[768,256]{1,0:T(8,128)S(1)}, u32[]{:S(2)}, u32[]{:S(2)}) %collective-permute-start.3) | collective-permute-done | bytes 786464 | tf_op jit(solution)/shard_map/ppermute | solution.py:563
  51.8 2.8 %pairs1.1.after_ref.mine_ref = f32[56,256]{1,0:T(8,128)S(1)} custom-call(s32[1]{0:T(128)} %bitcast.p_ref, bf16[56,512]{1,0:T(8,128)(2,1)S(1)} %table1.1.hot_ref, f32[512,512]{1,0:T(8,128)S(1)} %pairs0.1.gram_ref, f32[768,256]{1,0:T(8,128)S(1)} %collective-permute-done.3.a_ref.rxb, f32[768,256]{1,0:T(8,128)S(1)} %collective-permute-done.4.b_ref.syb), custom_call_target="tpu_custom_call" | custom-call | flops 4000000000 | bytes 12000000 | tf_op jit(solution)/shard_map/pairs1/pallas_call | solution.py:391
  54.5 6.4 %collective-permute-start.5 = (f32[56,256]{1,0:T(8,128)S(1)}, f32[56,256]{1,0:T(8,128)S(1)}, u32[]{:S(2)}, u32[]{:S(2)}) collective-permute-start(f32[56,256]{1,0:T(8,128)S(1)} %pairs1.1.after_ref.mine_ref), channel_id=1, source_target_pairs={{0,1},{1,0},{2,3},{3,2},{4,5},{5,4},{6,7},{7,6},{8,9},{9,8},{10,11... | collective-permute-start | bytes 172040 | tf_op jit(solution)/shard_map/ppermute | solution.py:572
  61.5 1.9 %collective-permute-start.10 = (f32[768,256]{1,0:T(8,128)S(1)}, f32[768,256]{1,0:T(8,128)S(1)}, u32[]{:S(2)}, u32[]{:S(2)}) collective-permute-start(f32[768,256]{1,0:T(8,128)S(1)} %get-tuple-element.49), channel_id=1, source_target_pairs={{0,6},{4,10},{8,14},{12,18},{16,22},{20,26},{24,30},{28,34},{32,38... | collective-permute-start | bytes 2359304 | tf_op jit(solution)/shard_map/ppermute | solution.py:575
  63.8 1.2 %solve1.1.coef_ref.b_ref = f32[16,256]{1,0:T(8,128)S(1)} custom-call(s32[3,4]{1,0:T(4,128)S(1)} %copy-done.1, f32[56,256]{1,0:T(8,128)S(1)} %pairs1.1.after_ref.mine_ref, f32[56,256]{1,0:T(8,128)S(1)} %collective-permute-done.5.other_ref), custom_call_target="tpu_custom_call" | custom-call | flops 2000000000 | bytes 6000000 | tf_op jit(solution)/shard_map/solve1/pallas_call | solution.py:468
  65.0 8.6 %collective-permute-start.9 = (f32[16,256]{1,0:T(8,128)S(1)}, f32[16,256]{1,0:T(8,128)S(1)}, u32[]{:S(2)}, u32[]{:S(2)}) collective-permute-start(f32[16,256]{1,0:T(8,128)S(1)} %solve1.1.coef_ref.b_ref), channel_id=1, source_target_pairs={{4,0},{8,4},{12,8},{16,12},{20,16},{24,20},{28,24},{32,28},{36,32}... | collective-permute-start | bytes 49160 | tf_op jit(solution)/shard_map/ppermute | solution.py:577
  73.6 3.6 %turn1.1 = (f32[768,256]{1,0:T(8,128)S(1)}, f32[768,256]{1,0:T(8,128)S(1)}, f32[1536,256]{1,0:T(8,128)S(1)}) custom-call(s32[3,4]{1,0:T(4,128)S(1)} %copy-done.1, s32[1]{0:T(128)} %bitcast.p_ref, f32[16,256]{1,0:T(8,128)S(1)} %solve1.1.coef_ref.b_ref, f32[768,256]{1,0:T(8,128)S(1)} %collective-permute-done.1.a_ref.rxa, ...), custom_call_target="tpu_custom_call" | custom-call | flops 40000000000 | bytes 120000000 | tf_op jit(solution)/shard_map/turn1/pallas_call | solution.py:415
  77.5 6.7 %side.1 = (f32[1536,256]{1,0:T(8,128)S(1)}, f32[56,256]{1,0:T(8,128)S(1)}) custom-call(s32[3,4]{1,0:T(4,128)S(1)} %copy-done.1, s32[1]{0:T(128)} %bitcast.p_ref, bf16[56,512]{1,0:T(8,128)(2,1)S(1)} %table2.1.hot_ref, f32[16,256]{1,0:T(8,128)S(1)} %collective-permute-done.9.coef_ref, f32[768,256]{1,0:T(8,128)S(1)} %collective-permute-done.7.sxa, ...), custom_call_target="tpu_custom_call" | custom-call | flops 8000000000 | bytes 24000000 | tf_op jit(solution)/shard_map/side/pallas_call | solution.py:453
  84.5 8.0 %collective-permute-done.11.other_ref = f32[56,256]{1,0:T(8,128)S(1)} collective-permute-done((f32[56,256]{1,0:T(8,128)S(1)}, f32[56,256]{1,0:T(8,128)S(1)}, u32[]{:S(2)}, u32[]{:S(2)}) %collective-permute-start.11) | collective-permute-done | bytes 57376 | tf_op jit(solution)/shard_map/ppermute | solution.py:583
  92.4 1.2 %solve2.1.coef_ref = f32[16,256]{1,0:T(8,128)S(1)} custom-call(s32[3,4]{1,0:T(4,128)S(1)} %copy-done.1, f32[56,256]{1,0:T(8,128)S(1)} %get-tuple-element.52.mine_ref, f32[56,256]{1,0:T(8,128)S(1)} %collective-permute-done.11.other_ref), custom_call_target="tpu_custom_call" | custom-call | flops 2000000000 | bytes 6000000 | tf_op jit(solution)/shard_map/solve2/pallas_call | solution.py:468
  93.7 2.5 %collective-permute-done.13.ra = f32[768,256]{1,0:T(8,128)S(1)} collective-permute-done((f32[768,256]{1,0:T(8,128)S(1)}, f32[768,256]{1,0:T(8,128)S(1)}, u32[]{:S(2)}, u32[]{:S(2)}) %collective-permute-start.13) | collective-permute-done | bytes 786464 | tf_op jit(solution)/shard_map/ppermute | solution.py:581
  96.2 3.6 %own.1.own_ref = f32[1536,256]{1,0:T(8,128)S(1)} custom-call(s32[3,4]{1,0:T(4,128)S(1)} %copy-done.1, s32[1]{0:T(128)} %bitcast.p_ref, f32[16,256]{1,0:T(8,128)S(1)} %solve2.1.coef_ref, f32[768,256]{1,0:T(8,128)S(1)} %get-tuple-element.50.za, f32[768,256]{1,0:T(8,128)S(1)} %get-tuple-element.58.zb, f32[1536,256]{1,0:T(8,128)S(1)} %get-tuple-element.54.q_ref), custom_call_target="tpu_custom_call" | custom-call | flops 40000000000 | bytes 120000000 | tf_op jit(solution)/shard_map/own/pallas_call | solution.py:495
  100.1 5.3 %collective-permute-done.12.coef_ref = f32[16,256]{1,0:T(8,128)S(1)} collective-permute-done((f32[16,256]{1,0:T(8,128)S(1)}, f32[16,256]{1,0:T(8,128)S(1)}, u32[]{:S(2)}, u32[]{:S(2)}) %collective-permute-start.12) | collective-permute-done | bytes 16416 | tf_op jit(solution)/shard_map/ppermute | solution.py:587
  105.4 5.0 %finish.1 = (f32[2,1536,256]{2,1,0:T(8,128)}, f32[3,2,256]{2,1,0:T(2,128)}) custom-call(s32[3,4]{1,0:T(4,128)S(1)} %copy-done.1, s32[1]{0:T(128)} %bitcast.p_ref, f32[16,256]{1,0:T(8,128)S(1)} %collective-permute-done.12.coef_ref, f32[16,256]{1,0:T(8,128)S(1)} %get-tuple-element.35.after_ref.a_ref, f32[16,256]{1,0:T(8,128)S(1)} %solve1.1.coef_ref.b_ref, ...), custom_call_target="tpu_custom_call" | custom-call | flops 5000000000 | bytes 15000000 | tf_op jit(solution)/shard_map/finish/pallas_call | solution.py:531
  (24 shorter events, 3.2 us)
Async XLA Ops:
  0.6 0.7 copy-start
  1.3 19.7 %copy-start.1 = (s32[3,4]{1,0:T(4,128)S(1)}, s32[3,4]{1,0:T(4,128)}, u32[]{:S(2)}) copy-start(s32[3,4]{1,0:T(4,128)} %o_ref.17) | copy-start | bytes 148
  11.6 9.4 %collective-permute-start = (f32[56,256]{1,0:T(8,128)S(1)}, f32[56,256]{1,0:T(8,128)S(1)}, u32[]{:S(2)}, u32[]{:S(2)}) collective-permute-start(f32[56,256]{1,0:T(8,128)S(1)} %get-tuple-element.31.mine_ref), channel_id=1, source_target_pairs={{0,1},{1,0},{2,3},{3,2},{4,5},{5,4},{6,7},{7,6},{8,9},{9,8},{10,11... | collective-permute-start | bytes 172040 | tf_op jit(solution)/shard_map/ppermute | solution.py:559
  25.2 18.1 %collective-permute-start.1 = (f32[768,256]{1,0:T(8,128)S(1)}, f32[768,256]{1,0:T(8,128)S(1)}, u32[]{:S(2)}, u32[]{:S(2)}) collective-permute-start(f32[768,256]{1,0:T(8,128)S(1)} %get-tuple-element.37), channel_id=1, source_target_pairs={{2,4},{6,8},{10,12},{14,16},{18,20},{22,24},{26,28},{30,32},{34,36... | collective-permute-start | bytes 2359304 | tf_op jit(solution)/shard_map/ppermute | solution.py:562
  31.2 12.1 %collective-permute-start.2 = (f32[768,256]{1,0:T(8,128)S(1)}, f32[768,256]{1,0:T(8,128)S(1)}, u32[]{:S(2)}, u32[]{:S(2)}) collective-permute-start(f32[768,256]{1,0:T(8,128)S(1)} %get-tuple-element.41), channel_id=1, source_target_pairs={{0,2},{2,0},{4,6},{6,4},{8,10},{10,8},{12,14},{14,12},{16,18},{18,... | collective-permute-start | bytes 2359304 | tf_op jit(solution)/shard_map/ppermute | solution.py:564
  31.3 20.5 %collective-permute-start.3 = (f32[768,256]{1,0:T(8,128)S(1)}, f32[768,256]{1,0:T(8,128)S(1)}, u32[]{:S(2)}, u32[]{:S(2)}) collective-permute-start(f32[768,256]{1,0:T(8,128)S(1)} %get-tuple-element.39), channel_id=1, source_target_pairs={{2,4},{6,8},{10,12},{14,16},{18,20},{22,24},{26,28},{30,32},{34,36... | collective-permute-start | bytes 2359304 | tf_op jit(solution)/shard_map/ppermute | solution.py:563
  35.7 16.1 %collective-permute-start.4 = (f32[768,256]{1,0:T(8,128)S(1)}, f32[768,256]{1,0:T(8,128)S(1)}, u32[]{:S(2)}, u32[]{:S(2)}) collective-permute-start(f32[768,256]{1,0:T(8,128)S(1)} %get-tuple-element.49), channel_id=1, source_target_pairs={{0,2},{2,0},{4,6},{6,4},{8,10},{10,8},{12,14},{14,12},{16,18},{18,... | collective-permute-start | bytes 2359304 | tf_op jit(solution)/shard_map/ppermute | solution.py:565
  35.8 37.8 %collective-permute-start.7 = (f32[768,256]{1,0:T(8,128)S(1)}, f32[768,256]{1,0:T(8,128)S(1)}, u32[]{:S(2)}, u32[]{:S(2)}) collective-permute-start(f32[768,256]{1,0:T(8,128)S(1)} %get-tuple-element.37), channel_id=1, source_target_pairs={{0,2},{2,0},{4,6},{6,4},{8,10},{10,8},{12,14},{14,12},{16,18},{18,... | collective-permute-start | bytes 2359304 | tf_op jit(solution)/shard_map/ppermute | solution.py:566
  43.3 30.3 %collective-permute-start.8 = (f32[768,256]{1,0:T(8,128)S(1)}, f32[768,256]{1,0:T(8,128)S(1)}, u32[]{:S(2)}, u32[]{:S(2)}) collective-permute-start(f32[768,256]{1,0:T(8,128)S(1)} %get-tuple-element.39), channel_id=1, source_target_pairs={{0,2},{2,0},{4,6},{6,4},{8,10},{10,8},{12,14},{14,12},{16,18},{18,... | collective-permute-start | bytes 2359304 | tf_op jit(solution)/shard_map/ppermute | solution.py:567
  44.8 28.8 %collective-permute-start.6 = (f32[768,256]{1,0:T(8,128)S(1)}, f32[768,256]{1,0:T(8,128)S(1)}, u32[]{:S(2)}, u32[]{:S(2)}) collective-permute-start(f32[768,256]{1,0:T(8,128)S(1)} %get-tuple-element.41), channel_id=1, source_target_pairs={{0,6},{4,10},{8,14},{12,18},{16,22},{20,26},{24,30},{28,34},{32,38... | collective-permute-start | bytes 2359304 | tf_op jit(solution)/shard_map/ppermute | solution.py:570
  54.5 9.3 %collective-permute-start.5 = (f32[56,256]{1,0:T(8,128)S(1)}, f32[56,256]{1,0:T(8,128)S(1)}, u32[]{:S(2)}, u32[]{:S(2)}) collective-permute-start(f32[56,256]{1,0:T(8,128)S(1)} %pairs1.1.after_ref.mine_ref), channel_id=1, source_target_pairs={{0,1},{1,0},{2,3},{3,2},{4,5},{5,4},{6,7},{7,6},{8,9},{9,8},{10,11... | collective-permute-start | bytes 172040 | tf_op jit(solution)/shard_map/ppermute | solution.py:572
  61.5 16.0 %collective-permute-start.10 = (f32[768,256]{1,0:T(8,128)S(1)}, f32[768,256]{1,0:T(8,128)S(1)}, u32[]{:S(2)}, u32[]{:S(2)}) collective-permute-start(f32[768,256]{1,0:T(8,128)S(1)} %get-tuple-element.49), channel_id=1, source_target_pairs={{0,6},{4,10},{8,14},{12,18},{16,22},{20,26},{24,30},{28,34},{32,38... | collective-permute-start | bytes 2359304 | tf_op jit(solution)/shard_map/ppermute | solution.py:575
  65.0 12.2 %collective-permute-start.9 = (f32[16,256]{1,0:T(8,128)S(1)}, f32[16,256]{1,0:T(8,128)S(1)}, u32[]{:S(2)}, u32[]{:S(2)}) collective-permute-start(f32[16,256]{1,0:T(8,128)S(1)} %solve1.1.coef_ref.b_ref), channel_id=1, source_target_pairs={{4,0},{8,4},{12,8},{16,12},{20,16},{24,20},{28,24},{32,28},{36,32}... | collective-permute-start | bytes 49160 | tf_op jit(solution)/shard_map/ppermute | solution.py:577
  77.2 19.0 %collective-permute-start.13 = (f32[768,256]{1,0:T(8,128)S(1)}, f32[768,256]{1,0:T(8,128)S(1)}, u32[]{:S(2)}, u32[]{:S(2)}) collective-permute-start(f32[768,256]{1,0:T(8,128)S(1)} %get-tuple-element.50.za), channel_id=1, source_target_pairs={{0,4},{4,8},{8,12},{12,16},{16,20},{20,24},{24,28},{28,32},{32,36}... | collective-permute-start | bytes 2359304 | tf_op jit(solution)/shard_map/ppermute | solution.py:581
  84.3 8.2 %collective-permute-start.11 = (f32[56,256]{1,0:T(8,128)S(1)}, f32[56,256]{1,0:T(8,128)S(1)}, u32[]{:S(2)}, u32[]{:S(2)}) collective-permute-start(f32[56,256]{1,0:T(8,128)S(1)} %get-tuple-element.52.mine_ref), channel_id=1, source_target_pairs={{0,1},{1,0},{2,3},{3,2},{4,5},{5,4},{6,7},{7,6},{8,9},{9,8},{10,11... | collective-permute-start | bytes 172040 | tf_op jit(solution)/shard_map/ppermute | solution.py:583
  84.4 21.0 %collective-permute-start.15 = (f32[768,256]{1,0:T(8,128)S(1)}, f32[768,256]{1,0:T(8,128)S(1)}, u32[]{:S(2)}, u32[]{:S(2)}) collective-permute-start(f32[768,256]{1,0:T(8,128)S(1)} %get-tuple-element.58.zb), channel_id=1, source_target_pairs={{0,4},{4,8},{8,12},{12,16},{16,20},{20,24},{24,28},{28,32},{32,36}... | collective-permute-start | bytes 2359304 | tf_op jit(solution)/shard_map/ppermute | solution.py:585
  93.6 11.8 %collective-permute-start.12 = (f32[16,256]{1,0:T(8,128)S(1)}, f32[16,256]{1,0:T(8,128)S(1)}, u32[]{:S(2)}, u32[]{:S(2)}) collective-permute-start(f32[16,256]{1,0:T(8,128)S(1)} %solve2.1.coef_ref), channel_id=1, source_target_pairs={{0,4},{4,8},{8,12},{12,16},{16,20},{20,24},{24,28},{28,32},{32,36}... | collective-permute-start | bytes 49160 | tf_op jit(solution)/shard_map/ppermute | solution.py:587
  99.8 5.6 %collective-permute-start.14 = (f32[16,256]{1,0:T(8,128)S(1)}, f32[16,256]{1,0:T(8,128)S(1)}, u32[]{:S(2)}, u32[]{:S(2)}) collective-permute-start(f32[16,256]{1,0:T(8,128)S(1)} %solve2.1.coef_ref), channel_id=1, source_target_pairs={{0,2},{2,0},{4,6},{6,4},{8,10},{10,8},{12,14},{14,12},{16,18},{18,... | collective-permute-start | bytes 49160 | tf_op jit(solution)/shard_map/ppermute | solution.py:591

commit v8 on v7

--- a/solution.py
+++ b/solution.py
@@ -574,11 +574,11 @@
     yb, hot = lax.optimization_barrier((yb, hot))
     ryb = lax.ppermute(yb, "blk", lend)
     coef_b = solve(1, offsets, lag, lag_other)
-    coef_side = lax.ppermute(coef_b, "blk", tell)
     rxa, rya, sxa, sxb = lax.optimization_barrier((rxa, rya, sxa, sxb))
     za, zb, v = turn_second(offsets, p, coef_b, rxa, rxb, sya, syb)
-    za, zb, coef_side = lax.optimization_barrier((za, zb, coef_side))
     ra = lax.ppermute(za, "blk", deal)
+    told, za = lax.optimization_barrier((coef_b, za))
+    coef_side = lax.ppermute(told, "blk", tell)
     q, lag = side(n - 1, offsets, p, hot, coef_side, sxa, sxb, rya, ryb, za, zb)
     lag_other = lax.ppermute(lag, "row", across)
     later, _ = lax.optimization_barrier((zb, lag))

time: 111 us -> 115 us (1.036)
  the two profiles are of different devices: /device:TPU:4 before, /device:TPU:49 now
where the time goes in v8:
time: 115 us
  starting transfers between devices  49.6 us (43%)
  Pallas kernels  41.1 us (36%)
  waiting for transfers between devices  22.9 us (20%)
    ppermute x1, starting transfers between devices, body(): coef_norm = lax.ppermute(coef_c, 'blk', sibling)  15.6 us
    ppermute x3, starting transfers between devices, body(): lag_other = lax.ppermute(lag, 'row', across)  12.8 us
    pallas_call x1, Pallas kernels, first(): call(first_kernel, 'first', [ANY, ANY, ANY], (VMEM, VMEM, VMEM), (block(r...  10.3 us
    ppermute x1, starting transfers between devices, body(): coef_side = lax.ppermute(told, 'blk', tell)  8.64 us
    ppermute x3, waiting for transfers between devices, body(): lag_other = lax.ppermute(lag, 'row', across)  8.53 us
    ppermute x1, waiting for transfers between devices, body(): rxa = lax.ppermute(xa, 'blk', meet)  7.32 us
    pallas_call x1, Pallas kernels, side(): call(functools.partial(side_kernel, last), 'side', [SMEM, SMEM] + [VMEM]...  6.75 us
    ppermute x1, waiting for transfers between devices, body(): rxb = lax.ppermute(xb, 'blk', meet)  5.34 us
  transfers between devices with their start and end apart: 16, of which 7 were waited for; matrix products, arithmetic and copies ran while one was open for 0% of the time, Pallas kernels for 19%

profile of v8, /device:TPU:49, one launch (start us, length us, event | category | flops | bytes accessed | tf_op | source)
XLA Modules:
  0.0 115.3 jit_solution(11345205798182711870)
XLA Ops:
  1.3 10.3 %first.1 = (f32[1536,256]{1,0:T(8,128)S(1)}, f32[1536,256]{1,0:T(8,128)S(1)}, f32[56,256]{1,0:T(8,128)S(1)}) custom-call(s32[3,4]{1,0:T(4,128)S(1)} %copy-done, bf16[1536,2048]{1,0:T(8,128)(2,1)} %rows_hbm.1, bf16[512,2048]{1,0:T(8,128)(2,1)} %cols_hbm.1), custom_call_target="tpu_custom_call" | custom-call | flops 10000000000 | bytes 30000000 | tf_op jit(solution)/shard_map/first/pallas_call | solution.py:304
  11.6 6.1 %collective-permute-start = (f32[56,256]{1,0:T(8,128)S(1)}, f32[56,256]{1,0:T(8,128)S(1)}, u32[]{:S(2)}, u32[]{:S(2)}) collective-permute-start(f32[56,256]{1,0:T(8,128)S(1)} %get-tuple-element.30.mine_ref), channel_id=1, source_target_pairs={{0,1},{1,0},{2,3},{3,2},{4,5},{5,4},{6,7},{7,6},{8,9},{9,8},{10,11... | collective-permute-start | bytes 172040 | tf_op jit(solution)/shard_map/ppermute | solution.py:559
  17.7 1.6 %collective-permute-done.other_ref = f32[56,256]{1,0:T(8,128)S(1)} collective-permute-done((f32[56,256]{1,0:T(8,128)S(1)}, f32[56,256]{1,0:T(8,128)S(1)}, u32[]{:S(2)}, u32[]{:S(2)}) %collective-permute-start) | collective-permute-done | bytes 57376 | tf_op jit(solution)/shard_map/ppermute | solution.py:559
  19.3 4.2 %turn0.1 = (f32[768,256]{1,0:T(8,128)S(1)}, f32[768,256]{1,0:T(8,128)S(1)}, f32[768,256]{1,0:T(8,128)S(1)}, f32[768,256]{1,0:T(8,128)S(1)}, f32[16,256]{1,0:T(8,128)S(1)}) custom-call(s32[3,4]{1,0:T(4,128)S(1)} %copy-done.1, s32[1]{0:T(128)} %bitcast.p_ref, f32[56,256]{1,0:T(8,128)S(1)} %get-tuple-element.30.mine_ref, ...), custom_call_target="tpu_custom_call" | custom-call | flops 5000000000 | bytes 15000000 | tf_op jit(solution)/shard_map/turn0/pallas_call | solution.py:363
  23.5 2.4 %collective-permute-start.2 = (f32[768,256]{1,0:T(8,128)S(1)}, f32[768,256]{1,0:T(8,128)S(1)}, u32[]{:S(2)}, u32[]{:S(2)}) collective-permute-start(f32[768,256]{1,0:T(8,128)S(1)} %get-tuple-element.40), channel_id=1, source_target_pairs={{0,2},{2,0},{4,6},{6,4},{8,10},{10,8},{12,14},{14,12},{16,18},{18,... | collective-permute-start | bytes 2359304 | tf_op jit(solution)/shard_map/ppermute | solution.py:564
  25.9 2.8 %collective-permute-start.1 = (f32[768,256]{1,0:T(8,128)S(1)}, f32[768,256]{1,0:T(8,128)S(1)}, u32[]{:S(2)}, u32[]{:S(2)}) collective-permute-start(f32[768,256]{1,0:T(8,128)S(1)} %get-tuple-element.36), channel_id=1, source_target_pairs={{2,4},{6,8},{10,12},{14,16},{18,20},{22,24},{26,28},{30,32},{34,36... | collective-permute-start | bytes 2359304 | tf_op jit(solution)/shard_map/ppermute | solution.py:562
  28.8 2.7 %collective-permute-start.3 = (f32[768,256]{1,0:T(8,128)S(1)}, f32[768,256]{1,0:T(8,128)S(1)}, u32[]{:S(2)}, u32[]{:S(2)}) collective-permute-start(f32[768,256]{1,0:T(8,128)S(1)} %get-tuple-element.38), channel_id=1, source_target_pairs={{2,4},{6,8},{10,12},{14,16},{18,20},{22,24},{26,28},{30,32},{34,36... | collective-permute-start | bytes 2359304 | tf_op jit(solution)/shard_map/ppermute | solution.py:563
  32.1 7.3 %collective-permute-done.1.a_ref.rxa = f32[768,256]{1,0:T(8,128)S(1)} collective-permute-done((f32[768,256]{1,0:T(8,128)S(1)}, f32[768,256]{1,0:T(8,128)S(1)}, u32[]{:S(2)}, u32[]{:S(2)}) %collective-permute-start.1) | collective-permute-done | bytes 786464 | tf_op jit(solution)/shard_map/ppermute | solution.py:562
  39.5 1.5 %pairs0.1.gram_ref = f32[512,512]{1,0:T(8,128)S(1)} custom-call(s32[1]{0:T(128)} %bitcast.p_ref, f32[768,256]{1,0:T(8,128)S(1)} %collective-permute-done.1.a_ref.rxa, f32[768,256]{1,0:T(8,128)S(1)} %collective-permute-done.2.b_ref.sya), custom_call_target="tpu_custom_call" | custom-call | flops 3000000000 | bytes 9000000 | tf_op jit(solution)/shard_map/pairs0/pallas_call | solution.py:380
  40.9 1.9 %collective-permute-start.6 = (f32[768,256]{1,0:T(8,128)S(1)}, f32[768,256]{1,0:T(8,128)S(1)}, u32[]{:S(2)}, u32[]{:S(2)}) collective-permute-start(f32[768,256]{1,0:T(8,128)S(1)} %get-tuple-element.40), channel_id=1, source_target_pairs={{0,6},{4,10},{8,14},{12,18},{16,22},{20,26},{24,30},{28,34},{32,38... | collective-permute-start | bytes 2359304 | tf_op jit(solution)/shard_map/ppermute | solution.py:570
  43.5 5.3 %collective-permute-done.3.a_ref.rxb = f32[768,256]{1,0:T(8,128)S(1)} collective-permute-done((f32[768,256]{1,0:T(8,128)S(1)}, f32[768,256]{1,0:T(8,128)S(1)}, u32[]{:S(2)}, u32[]{:S(2)}) %collective-permute-start.3) | collective-permute-done | bytes 786464 | tf_op jit(solution)/shard_map/ppermute | solution.py:563
  48.8 2.8 %pairs1.1.after_ref.mine_ref = f32[56,256]{1,0:T(8,128)S(1)} custom-call(s32[1]{0:T(128)} %bitcast.p_ref, bf16[56,512]{1,0:T(8,128)(2,1)S(1)} %table1.1.hot_ref, f32[512,512]{1,0:T(8,128)S(1)} %pairs0.1.gram_ref, f32[768,256]{1,0:T(8,128)S(1)} %collective-permute-done.3.a_ref.rxb, f32[768,256]{1,0:T(8,128)S(1)} %collective-permute-done.4.b_ref.syb), custom_call_target="tpu_custom_call" | custom-call | flops 4000000000 | bytes 12000000 | tf_op jit(solution)/shard_map/pairs1/pallas_call | solution.py:391
  51.6 6.2 %collective-permute-start.5 = (f32[56,256]{1,0:T(8,128)S(1)}, f32[56,256]{1,0:T(8,128)S(1)}, u32[]{:S(2)}, u32[]{:S(2)}) collective-permute-start(f32[56,256]{1,0:T(8,128)S(1)} %pairs1.1.after_ref.mine_ref), channel_id=1, source_target_pairs={{0,1},{1,0},{2,3},{3,2},{4,5},{5,4},{6,7},{7,6},{8,9},{9,8},{10,11... | collective-permute-start | bytes 172040 | tf_op jit(solution)/shard_map/ppermute | solution.py:572
  58.4 1.9 %collective-permute-start.10 = (f32[768,256]{1,0:T(8,128)S(1)}, f32[768,256]{1,0:T(8,128)S(1)}, u32[]{:S(2)}, u32[]{:S(2)}) collective-permute-start(f32[768,256]{1,0:T(8,128)S(1)} %get-tuple-element.47), channel_id=1, source_target_pairs={{0,6},{4,10},{8,14},{12,18},{16,22},{20,26},{24,30},{28,34},{32,38... | collective-permute-start | bytes 2359304 | tf_op jit(solution)/shard_map/ppermute | solution.py:575
  60.7 1.2 %solve1.1.coef_ref.b_ref = f32[16,256]{1,0:T(8,128)S(1)} custom-call(s32[3,4]{1,0:T(4,128)S(1)} %copy-done.1, f32[56,256]{1,0:T(8,128)S(1)} %pairs1.1.after_ref.mine_ref, f32[56,256]{1,0:T(8,128)S(1)} %collective-permute-done.5.other_ref), custom_call_target="tpu_custom_call" | custom-call | flops 2000000000 | bytes 6000000 | tf_op jit(solution)/shard_map/solve1/pallas_call | solution.py:468
  61.9 3.6 %turn1.1 = (f32[768,256]{1,0:T(8,128)S(1)}, f32[768,256]{1,0:T(8,128)S(1)}, f32[1536,256]{1,0:T(8,128)S(1)}) custom-call(s32[3,4]{1,0:T(4,128)S(1)} %copy-done.1, s32[1]{0:T(128)} %bitcast.p_ref, f32[16,256]{1,0:T(8,128)S(1)} %solve1.1.coef_ref.b_ref, f32[768,256]{1,0:T(8,128)S(1)} %collective-permute-done.1.a_ref.rxa, ...), custom_call_target="tpu_custom_call" | custom-call | flops 40000000000 | bytes 120000000 | tf_op jit(solution)/shard_map/turn1/pallas_call | solution.py:415
  65.5 8.6 %collective-permute-start.9 = (f32[16,256]{1,0:T(8,128)S(1)}, f32[16,256]{1,0:T(8,128)S(1)}, u32[]{:S(2)}, u32[]{:S(2)}) collective-permute-start(f32[16,256]{1,0:T(8,128)S(1)} %solve1.1.coef_ref.b_ref), channel_id=1, source_target_pairs={{4,0},{8,4},{12,8},{16,12},{20,16},{24,20},{28,24},{32,28},{36,32}... | collective-permute-start | bytes 49160 | tf_op jit(solution)/shard_map/ppermute | solution.py:581
  74.2 0.9 collective-permute-done.9.coef_ref
  75.0 6.8 %side.1 = (f32[1536,256]{1,0:T(8,128)S(1)}, f32[56,256]{1,0:T(8,128)S(1)}) custom-call(s32[3,4]{1,0:T(4,128)S(1)} %copy-done.1, s32[1]{0:T(128)} %bitcast.p_ref, bf16[56,512]{1,0:T(8,128)(2,1)S(1)} %table2.1.hot_ref, f32[16,256]{1,0:T(8,128)S(1)} %collective-permute-done.9.coef_ref, f32[768,256]{1,0:T(8,128)S(1)} %collective-permute-done.7.sxa, ...), custom_call_target="tpu_custom_call" | custom-call | flops 8000000000 | bytes 24000000 | tf_op jit(solution)/shard_map/side/pallas_call | solution.py:453
  82.3 6.5 %collective-permute-done.11.other_ref = f32[56,256]{1,0:T(8,128)S(1)} collective-permute-done((f32[56,256]{1,0:T(8,128)S(1)}, f32[56,256]{1,0:T(8,128)S(1)}, u32[]{:S(2)}, u32[]{:S(2)}) %collective-permute-start.11) | collective-permute-done | bytes 57376 | tf_op jit(solution)/shard_map/ppermute | solution.py:583
  88.9 1.2 %solve2.1.coef_ref = f32[16,256]{1,0:T(8,128)S(1)} custom-call(s32[3,4]{1,0:T(4,128)S(1)} %copy-done.1, f32[56,256]{1,0:T(8,128)S(1)} %get-tuple-element.50.mine_ref, f32[56,256]{1,0:T(8,128)S(1)} %collective-permute-done.11.other_ref), custom_call_target="tpu_custom_call" | custom-call | flops 2000000000 | bytes 6000000 | tf_op jit(solution)/shard_map/solve2/pallas_call | solution.py:468
  90.1 3.6 %own.1.own_ref = f32[1536,256]{1,0:T(8,128)S(1)} custom-call(s32[3,4]{1,0:T(4,128)S(1)} %copy-done.1, s32[1]{0:T(128)} %bitcast.p_ref, f32[16,256]{1,0:T(8,128)S(1)} %solve2.1.coef_ref, f32[768,256]{1,0:T(8,128)S(1)} %get-tuple-element.48.za, f32[768,256]{1,0:T(8,128)S(1)} %get-tuple-element.56.zb, f32[1536,256]{1,0:T(8,128)S(1)} %get-tuple-element.52.q_ref), custom_call_target="tpu_custom_call" | custom-call | flops 40000000000 | bytes 120000000 | tf_op jit(solution)/shard_map/own/pallas_call | solution.py:495
  93.7 15.6 %collective-permute-start.14 = (f32[16,256]{1,0:T(8,128)S(1)}, f32[16,256]{1,0:T(8,128)S(1)}, u32[]{:S(2)}, u32[]{:S(2)}) collective-permute-start(f32[16,256]{1,0:T(8,128)S(1)} %solve2.1.coef_ref), channel_id=1, source_target_pairs={{0,2},{2,0},{4,6},{6,4},{8,10},{10,8},{12,14},{14,12},{16,18},{18,... | collective-permute-start | bytes 49160 | tf_op jit(solution)/shard_map/ppermute | solution.py:591
  110.1 5.0 %finish.1 = (f32[2,1536,256]{2,1,0:T(8,128)}, f32[3,2,256]{2,1,0:T(2,128)}) custom-call(s32[3,4]{1,0:T(4,128)S(1)} %copy-done.1, s32[1]{0:T(128)} %bitcast.p_ref, f32[16,256]{1,0:T(8,128)S(1)} %collective-permute-done.12.coef_ref, f32[16,256]{1,0:T(8,128)S(1)} %get-tuple-element.34.after_ref.a_ref, f32[16,256]{1,0:T(8,128)S(1)} %solve1.1.coef_ref.b_ref, ...), custom_call_target="tpu_custom_call" | custom-call | flops 5000000000 | bytes 15000000 | tf_op jit(solution)/shard_map/finish/pallas_call | solution.py:531
  (24 shorter events, 4.5 us)
Async XLA Ops:
  0.6 0.7 copy-start
  1.3 18.0 %copy-start.1 = (s32[3,4]{1,0:T(4,128)S(1)}, s32[3,4]{1,0:T(4,128)}, u32[]{:S(2)}) copy-start(s32[3,4]{1,0:T(4,128)} %o_ref.17) | copy-start | bytes 148
  11.6 7.7 %collective-permute-start = (f32[56,256]{1,0:T(8,128)S(1)}, f32[56,256]{1,0:T(8,128)S(1)}, u32[]{:S(2)}, u32[]{:S(2)}) collective-permute-start(f32[56,256]{1,0:T(8,128)S(1)} %get-tuple-element.30.mine_ref), channel_id=1, source_target_pairs={{0,1},{1,0},{2,3},{3,2},{4,5},{5,4},{6,7},{7,6},{8,9},{9,8},{10,11... | collective-permute-start | bytes 172040 | tf_op jit(solution)/shard_map/ppermute | solution.py:559
  23.5 8.2 %collective-permute-start.2 = (f32[768,256]{1,0:T(8,128)S(1)}, f32[768,256]{1,0:T(8,128)S(1)}, u32[]{:S(2)}, u32[]{:S(2)}) collective-permute-start(f32[768,256]{1,0:T(8,128)S(1)} %get-tuple-element.40), channel_id=1, source_target_pairs={{0,2},{2,0},{4,6},{6,4},{8,10},{10,8},{12,14},{14,12},{16,18},{18,... | collective-permute-start | bytes 2359304 | tf_op jit(solution)/shard_map/ppermute | solution.py:564
  25.9 13.6 %collective-permute-start.1 = (f32[768,256]{1,0:T(8,128)S(1)}, f32[768,256]{1,0:T(8,128)S(1)}, u32[]{:S(2)}, u32[]{:S(2)}) collective-permute-start(f32[768,256]{1,0:T(8,128)S(1)} %get-tuple-element.36), channel_id=1, source_target_pairs={{2,4},{6,8},{10,12},{14,16},{18,20},{22,24},{26,28},{30,32},{34,36... | collective-permute-start | bytes 2359304 | tf_op jit(solution)/shard_map/ppermute | solution.py:562
  28.7 14.8 %collective-permute-start.4 = (f32[768,256]{1,0:T(8,128)S(1)}, f32[768,256]{1,0:T(8,128)S(1)}, u32[]{:S(2)}, u32[]{:S(2)}) collective-permute-start(f32[768,256]{1,0:T(8,128)S(1)} %get-tuple-element.47), channel_id=1, source_target_pairs={{0,2},{2,0},{4,6},{6,4},{8,10},{10,8},{12,14},{14,12},{16,18},{18,... | collective-permute-start | bytes 2359304 | tf_op jit(solution)/shard_map/ppermute | solution.py:565
  28.8 20.0 %collective-permute-start.3 = (f32[768,256]{1,0:T(8,128)S(1)}, f32[768,256]{1,0:T(8,128)S(1)}, u32[]{:S(2)}, u32[]{:S(2)}) collective-permute-start(f32[768,256]{1,0:T(8,128)S(1)} %get-tuple-element.38), channel_id=1, source_target_pairs={{2,4},{6,8},{10,12},{14,16},{18,20},{22,24},{26,28},{30,32},{34,36... | collective-permute-start | bytes 2359304 | tf_op jit(solution)/shard_map/ppermute | solution.py:563
  31.5 30.4 %collective-permute-start.7 = (f32[768,256]{1,0:T(8,128)S(1)}, f32[768,256]{1,0:T(8,128)S(1)}, u32[]{:S(2)}, u32[]{:S(2)}) collective-permute-start(f32[768,256]{1,0:T(8,128)S(1)} %get-tuple-element.36), channel_id=1, source_target_pairs={{0,2},{2,0},{4,6},{6,4},{8,10},{10,8},{12,14},{14,12},{16,18},{18,... | collective-permute-start | bytes 2359304 | tf_op jit(solution)/shard_map/ppermute | solution.py:566
  31.6 30.3 %collective-permute-start.8 = (f32[768,256]{1,0:T(8,128)S(1)}, f32[768,256]{1,0:T(8,128)S(1)}, u32[]{:S(2)}, u32[]{:S(2)}) collective-permute-start(f32[768,256]{1,0:T(8,128)S(1)} %get-tuple-element.38), channel_id=1, source_target_pairs={{0,2},{2,0},{4,6},{6,4},{8,10},{10,8},{12,14},{14,12},{16,18},{18,... | collective-permute-start | bytes 2359304 | tf_op jit(solution)/shard_map/ppermute | solution.py:567
  40.9 21.0 %collective-permute-start.6 = (f32[768,256]{1,0:T(8,128)S(1)}, f32[768,256]{1,0:T(8,128)S(1)}, u32[]{:S(2)}, u32[]{:S(2)}) collective-permute-start(f32[768,256]{1,0:T(8,128)S(1)} %get-tuple-element.40), channel_id=1, source_target_pairs={{0,6},{4,10},{8,14},{12,18},{16,22},{20,26},{24,30},{28,34},{32,38... | collective-permute-start | bytes 2359304 | tf_op jit(solution)/shard_map/ppermute | solution.py:570
  51.6 9.2 %collective-permute-start.5 = (f32[56,256]{1,0:T(8,128)S(1)}, f32[56,256]{1,0:T(8,128)S(1)}, u32[]{:S(2)}, u32[]{:S(2)}) collective-permute-start(f32[56,256]{1,0:T(8,128)S(1)} %pairs1.1.after_ref.mine_ref), channel_id=1, source_target_pairs={{0,1},{1,0},{2,3},{3,2},{4,5},{5,4},{6,7},{7,6},{8,9},{9,8},{10,11... | collective-permute-start | bytes 172040 | tf_op jit(solution)/shard_map/ppermute | solution.py:572
  58.4 15.8 %collective-permute-start.10 = (f32[768,256]{1,0:T(8,128)S(1)}, f32[768,256]{1,0:T(8,128)S(1)}, u32[]{:S(2)}, u32[]{:S(2)}) collective-permute-start(f32[768,256]{1,0:T(8,128)S(1)} %get-tuple-element.47), channel_id=1, source_target_pairs={{0,6},{4,10},{8,14},{12,18},{16,22},{20,26},{24,30},{28,34},{32,38... | collective-permute-start | bytes 2359304 | tf_op jit(solution)/shard_map/ppermute | solution.py:575
  65.5 9.5 %collective-permute-start.9 = (f32[16,256]{1,0:T(8,128)S(1)}, f32[16,256]{1,0:T(8,128)S(1)}, u32[]{:S(2)}, u32[]{:S(2)}) collective-permute-start(f32[16,256]{1,0:T(8,128)S(1)} %solve1.1.coef_ref.b_ref), channel_id=1, source_target_pairs={{4,0},{8,4},{12,8},{16,12},{20,16},{24,20},{28,24},{32,28},{36,32}... | collective-permute-start | bytes 49160 | tf_op jit(solution)/shard_map/ppermute | solution.py:581
  74.2 15.9 %collective-permute-start.13 = (f32[768,256]{1,0:T(8,128)S(1)}, f32[768,256]{1,0:T(8,128)S(1)}, u32[]{:S(2)}, u32[]{:S(2)}) collective-permute-start(f32[768,256]{1,0:T(8,128)S(1)} %get-tuple-element.48.za), channel_id=1, source_target_pairs={{0,4},{4,8},{8,12},{12,16},{16,20},{20,24},{24,28},{28,32},{32,36}... | collective-permute-start | bytes 2359304 | tf_op jit(solution)/shard_map/ppermute | solution.py:579
  81.8 7.1 %collective-permute-start.11 = (f32[56,256]{1,0:T(8,128)S(1)}, f32[56,256]{1,0:T(8,128)S(1)}, u32[]{:S(2)}, u32[]{:S(2)}) collective-permute-start(f32[56,256]{1,0:T(8,128)S(1)} %get-tuple-element.50.mine_ref), channel_id=1, source_target_pairs={{0,1},{1,0},{2,3},{3,2},{4,5},{5,4},{6,7},{7,6},{8,9},{9,8},{10,11... | collective-permute-start | bytes 172040 | tf_op jit(solution)/shard_map/ppermute | solution.py:583
  82.3 27.0 %collective-permute-start.15 = (f32[768,256]{1,0:T(8,128)S(1)}, f32[768,256]{1,0:T(8,128)S(1)}, u32[]{:S(2)}, u32[]{:S(2)}) collective-permute-start(f32[768,256]{1,0:T(8,128)S(1)} %get-tuple-element.56.zb), channel_id=1, source_target_pairs={{0,4},{4,8},{8,12},{12,16},{16,20},{20,24},{24,28},{28,32},{32,36}... | collective-permute-start | bytes 2359304 | tf_op jit(solution)/shard_map/ppermute | solution.py:585
  90.0 19.3 %collective-permute-start.12 = (f32[16,256]{1,0:T(8,128)S(1)}, f32[16,256]{1,0:T(8,128)S(1)}, u32[]{:S(2)}, u32[]{:S(2)}) collective-permute-start(f32[16,256]{1,0:T(8,128)S(1)} %solve2.1.coef_ref), channel_id=1, source_target_pairs={{0,4},{4,8},{8,12},{12,16},{16,20},{20,24},{24,28},{28,32},{32,36}... | collective-permute-start | bytes 49160 | tf_op jit(solution)/shard_map/ppermute | solution.py:587
  93.7 16.5 %collective-permute-start.14 = (f32[16,256]{1,0:T(8,128)S(1)}, f32[16,256]{1,0:T(8,128)S(1)}, u32[]{:S(2)}, u32[]{:S(2)}) collective-permute-start(f32[16,256]{1,0:T(8,128)S(1)} %solve2.1.coef_ref), channel_id=1, source_target_pairs={{0,2},{2,0},{4,6},{6,4},{8,10},{10,8},{12,14},{14,12},{16,18},{18,... | collective-permute-start | bytes 49160 | tf_op jit(solution)/shard_map/ppermute | solution.py:591

commit v9 on v7

--- a/solution.py
+++ b/solution.py
@@ -256,7 +256,7 @@
 
 
 def first_kernel(
-    o_hbm, rows_hbm, cols_hbm, upper_ref, lower_ref, lag_ref, rows_ref, cols_ref, table_ref, norm_ref, o_ref, sem
+    o_hbm, rows_hbm, cols_hbm, upper_ref, lower_ref, lag_ref, rows_ref, cols_ref, turned_ref, table_ref, norm_ref, o_ref, sem
 ):
     count, feat = cols_ref.shape
     total = rows_ref.shape[0]
@@ -279,6 +279,7 @@
     onehot = build_onehot(o, table_ref)
     for copy in fetch_cols:
         copy.wait()
+    turned_ref[...] = jnp.transpose(cols_ref[...])
     for t in range(tiles):
         fetch_rows[t].wait()
         if t == 0:
@@ -288,7 +289,7 @@
                 norm_ref[:, k : k + H] = jnp.transpose(jnp.broadcast_to(sums, (H, H)))[0:8]
         part = slice(t * r, (t + 1) * r)
         rows = rows_ref[part]
-        cross = lax.dot_general(rows, cols_ref[...], NT, preferred_element_type=F32)
+        cross = jnp.dot(rows, turned_ref[...], preferred_element_type=F32)
         wide = rows.astype(F32)
         row_norm = jnp.sum(wide * wide, axis=1, keepdims=True)
         kernel = jnp.exp(
@@ -310,6 +311,7 @@
         [
             pltpu.VMEM(row_feats.shape, BF16),
             pltpu.VMEM(col_feats.shape, BF16),
+            pltpu.VMEM(col_feats.shape[::-1], BF16),
             TABLE,
             pltpu.VMEM((8, 2 * W), F32),
             pltpu.SMEM((3, 4), jnp.int32),

time: 111 us -> 111 us (level)
  no operation moved by 1% of the time
where the time goes in v9:
time: 111 us
  Pallas kernels  41 us (37%)
  starting transfers between devices  38 us (34%)
  waiting for transfers between devices  29.7 us (27%)
    ppermute x3, starting transfers between devices, body(): lag_other = lax.ppermute(lag, 'row', across)  13.8 us
    ppermute x3, waiting for transfers between devices, body(): lag_other = lax.ppermute(lag, 'row', across)  10.5 us
    pallas_call x1, Pallas kernels, first(): call(first_kernel, 'first', [ANY, ANY, ANY], (VMEM, VMEM, VMEM), (block(r...  10.2 us
    ppermute x1, starting transfers between devices, body(): coef_side = lax.ppermute(coef_b, 'blk', tell)  8.6 us
    ppermute x1, waiting for transfers between devices, body(): rxa = lax.ppermute(xa, 'blk', meet)  7.03 us
    pallas_call x1, Pallas kernels, side(): call(functools.partial(side_kernel, last), 'side', [SMEM, SMEM] + [VMEM]...  6.75 us
    ppermute x1, starting transfers between devices, body(): rxa = lax.ppermute(xa, 'blk', meet)  5.99 us
    ppermute x1, waiting for transfers between devices, body(): coef_got = lax.ppermute(coef_c, 'blk', deal)  5.27 us
  transfers between devices with their start and end apart: 16, of which 7 were waited for; matrix products, arithmetic and copies ran while one was open for 0% of the time, Pallas kernels for 20%

profile of v9, /device:TPU:4, one launch (start us, length us, event | category | flops | bytes accessed | tf_op | source)
XLA Modules:
  0.0 110.5 jit_solution(10994390553454568599)
XLA Ops:
  0.6 0.7 copy-done
  1.3 10.2 %first.1 = (f32[1536,256]{1,0:T(8,128)S(1)}, f32[1536,256]{1,0:T(8,128)S(1)}, f32[56,256]{1,0:T(8,128)S(1)}) custom-call(s32[3,4]{1,0:T(4,128)S(1)} %copy-done, bf16[1536,2048]{1,0:T(8,128)(2,1)} %rows_hbm.1, bf16[512,2048]{1,0:T(8,128)(2,1)} %cols_hbm.1), custom_call_target="tpu_custom_call" | custom-call | flops 10000000000 | bytes 30000000 | tf_op jit(solution)/shard_map/first/pallas_call | solution.py:305
  11.6 7.3 %collective-permute-start = (f32[56,256]{1,0:T(8,128)S(1)}, f32[56,256]{1,0:T(8,128)S(1)}, u32[]{:S(2)}, u32[]{:S(2)}) collective-permute-start(f32[56,256]{1,0:T(8,128)S(1)} %get-tuple-element.31.mine_ref), channel_id=1, source_target_pairs={{0,1},{1,0},{2,3},{3,2},{4,5},{5,4},{6,7},{7,6},{8,9},{9,8},{10,11... | collective-permute-start | bytes 172040 | tf_op jit(solution)/shard_map/ppermute | solution.py:561
  18.8 2.2 %collective-permute-done.other_ref = f32[56,256]{1,0:T(8,128)S(1)} collective-permute-done((f32[56,256]{1,0:T(8,128)S(1)}, f32[56,256]{1,0:T(8,128)S(1)}, u32[]{:S(2)}, u32[]{:S(2)}) %collective-permute-start) | collective-permute-done | bytes 57376 | tf_op jit(solution)/shard_map/ppermute | solution.py:561
  21.0 4.2 %turn0.1 = (f32[768,256]{1,0:T(8,128)S(1)}, f32[768,256]{1,0:T(8,128)S(1)}, f32[768,256]{1,0:T(8,128)S(1)}, f32[768,256]{1,0:T(8,128)S(1)}, f32[16,256]{1,0:T(8,128)S(1)}) custom-call(s32[3,4]{1,0:T(4,128)S(1)} %copy-done.1, s32[1]{0:T(128)} %bitcast.p_ref, f32[56,256]{1,0:T(8,128)S(1)} %get-tuple-element.31.mine_ref, ...), custom_call_target="tpu_custom_call" | custom-call | flops 5000000000 | bytes 15000000 | tf_op jit(solution)/shard_map/turn0/pallas_call | solution.py:365
  25.2 6.0 %collective-permute-start.1 = (f32[768,256]{1,0:T(8,128)S(1)}, f32[768,256]{1,0:T(8,128)S(1)}, u32[]{:S(2)}, u32[]{:S(2)}) collective-permute-start(f32[768,256]{1,0:T(8,128)S(1)} %get-tuple-element.37), channel_id=1, source_target_pairs={{2,4},{6,8},{10,12},{14,16},{18,20},{22,24},{26,28},{30,32},{34,36... | collective-permute-start | bytes 2359304 | tf_op jit(solution)/shard_map/ppermute | solution.py:564
  31.3 4.4 %collective-permute-start.3 = (f32[768,256]{1,0:T(8,128)S(1)}, f32[768,256]{1,0:T(8,128)S(1)}, u32[]{:S(2)}, u32[]{:S(2)}) collective-permute-start(f32[768,256]{1,0:T(8,128)S(1)} %get-tuple-element.39), channel_id=1, source_target_pairs={{2,4},{6,8},{10,12},{14,16},{18,20},{22,24},{26,28},{30,32},{34,36... | collective-permute-start | bytes 2359304 | tf_op jit(solution)/shard_map/ppermute | solution.py:565
  36.2 7.0 %collective-permute-done.1.a_ref.rxa = f32[768,256]{1,0:T(8,128)S(1)} collective-permute-done((f32[768,256]{1,0:T(8,128)S(1)}, f32[768,256]{1,0:T(8,128)S(1)}, u32[]{:S(2)}, u32[]{:S(2)}) %collective-permute-start.1) | collective-permute-done | bytes 786464 | tf_op jit(solution)/shard_map/ppermute | solution.py:564
  43.3 1.5 %pairs0.1.gram_ref = f32[512,512]{1,0:T(8,128)S(1)} custom-call(s32[1]{0:T(128)} %bitcast.p_ref, f32[768,256]{1,0:T(8,128)S(1)} %collective-permute-done.1.a_ref.rxa, f32[768,256]{1,0:T(8,128)S(1)} %collective-permute-done.2.b_ref.sya), custom_call_target="tpu_custom_call" | custom-call | flops 3000000000 | bytes 9000000 | tf_op jit(solution)/shard_map/pairs0/pallas_call | solution.py:382
  44.7 1.9 %collective-permute-start.6 = (f32[768,256]{1,0:T(8,128)S(1)}, f32[768,256]{1,0:T(8,128)S(1)}, u32[]{:S(2)}, u32[]{:S(2)}) collective-permute-start(f32[768,256]{1,0:T(8,128)S(1)} %get-tuple-element.41), channel_id=1, source_target_pairs={{0,6},{4,10},{8,14},{12,18},{16,22},{20,26},{24,30},{28,34},{32,38... | collective-permute-start | bytes 2359304 | tf_op jit(solution)/shard_map/ppermute | solution.py:572
  47.3 4.4 %collective-permute-done.3.a_ref.rxb = f32[768,256]{1,0:T(8,128)S(1)} collective-permute-done((f32[768,256]{1,0:T(8,128)S(1)}, f32[768,256]{1,0:T(8,128)S(1)}, u32[]{:S(2)}, u32[]{:S(2)}) %collective-permute-start.3) | collective-permute-done | bytes 786464 | tf_op jit(solution)/shard_map/ppermute | solution.py:565
  51.7 2.8 %pairs1.1.after_ref.mine_ref = f32[56,256]{1,0:T(8,128)S(1)} custom-call(s32[1]{0:T(128)} %bitcast.p_ref, bf16[56,512]{1,0:T(8,128)(2,1)S(1)} %table1.1.hot_ref, f32[512,512]{1,0:T(8,128)S(1)} %pairs0.1.gram_ref, f32[768,256]{1,0:T(8,128)S(1)} %collective-permute-done.3.a_ref.rxb, f32[768,256]{1,0:T(8,128)S(1)} %collective-permute-done.4.b_ref.syb), custom_call_target="tpu_custom_call" | custom-call | flops 4000000000 | bytes 12000000 | tf_op jit(solution)/shard_map/pairs1/pallas_call | solution.py:393
  54.5 6.4 %collective-permute-start.5 = (f32[56,256]{1,0:T(8,128)S(1)}, f32[56,256]{1,0:T(8,128)S(1)}, u32[]{:S(2)}, u32[]{:S(2)}) collective-permute-start(f32[56,256]{1,0:T(8,128)S(1)} %pairs1.1.after_ref.mine_ref), channel_id=1, source_target_pairs={{0,1},{1,0},{2,3},{3,2},{4,5},{5,4},{6,7},{7,6},{8,9},{9,8},{10,11... | collective-permute-start | bytes 172040 | tf_op jit(solution)/shard_map/ppermute | solution.py:574
  61.5 1.9 %collective-permute-start.10 = (f32[768,256]{1,0:T(8,128)S(1)}, f32[768,256]{1,0:T(8,128)S(1)}, u32[]{:S(2)}, u32[]{:S(2)}) collective-permute-start(f32[768,256]{1,0:T(8,128)S(1)} %get-tuple-element.49), channel_id=1, source_target_pairs={{0,6},{4,10},{8,14},{12,18},{16,22},{20,26},{24,30},{28,34},{32,38... | collective-permute-start | bytes 2359304 | tf_op jit(solution)/shard_map/ppermute | solution.py:577
  63.8 1.2 %solve1.1.coef_ref.b_ref = f32[16,256]{1,0:T(8,128)S(1)} custom-call(s32[3,4]{1,0:T(4,128)S(1)} %copy-done.1, f32[56,256]{1,0:T(8,128)S(1)} %pairs1.1.after_ref.mine_ref, f32[56,256]{1,0:T(8,128)S(1)} %collective-permute-done.5.other_ref), custom_call_target="tpu_custom_call" | custom-call | flops 2000000000 | bytes 6000000 | tf_op jit(solution)/shard_map/solve1/pallas_call | solution.py:470
  64.9 8.6 %collective-permute-start.9 = (f32[16,256]{1,0:T(8,128)S(1)}, f32[16,256]{1,0:T(8,128)S(1)}, u32[]{:S(2)}, u32[]{:S(2)}) collective-permute-start(f32[16,256]{1,0:T(8,128)S(1)} %solve1.1.coef_ref.b_ref), channel_id=1, source_target_pairs={{4,0},{8,4},{12,8},{16,12},{20,16},{24,20},{28,24},{32,28},{36,32}... | collective-permute-start | bytes 49160 | tf_op jit(solution)/shard_map/ppermute | solution.py:579
  73.6 3.6 %turn1.1 = (f32[768,256]{1,0:T(8,128)S(1)}, f32[768,256]{1,0:T(8,128)S(1)}, f32[1536,256]{1,0:T(8,128)S(1)}) custom-call(s32[3,4]{1,0:T(4,128)S(1)} %copy-done.1, s32[1]{0:T(128)} %bitcast.p_ref, f32[16,256]{1,0:T(8,128)S(1)} %solve1.1.coef_ref.b_ref, f32[768,256]{1,0:T(8,128)S(1)} %collective-permute-done.1.a_ref.rxa, ...), custom_call_target="tpu_custom_call" | custom-call | flops 40000000000 | bytes 120000000 | tf_op jit(solution)/shard_map/turn1/pallas_call | solution.py:417
  77.5 6.7 %side.1 = (f32[1536,256]{1,0:T(8,128)S(1)}, f32[56,256]{1,0:T(8,128)S(1)}) custom-call(s32[3,4]{1,0:T(4,128)S(1)} %copy-done.1, s32[1]{0:T(128)} %bitcast.p_ref, bf16[56,512]{1,0:T(8,128)(2,1)S(1)} %table2.1.hot_ref, f32[16,256]{1,0:T(8,128)S(1)} %collective-permute-done.9.coef_ref, f32[768,256]{1,0:T(8,128)S(1)} %collective-permute-done.7.sxa, ...), custom_call_target="tpu_custom_call" | custom-call | flops 8000000000 | bytes 24000000 | tf_op jit(solution)/shard_map/side/pallas_call | solution.py:455
  84.4 8.0 %collective-permute-done.11.other_ref = f32[56,256]{1,0:T(8,128)S(1)} collective-permute-done((f32[56,256]{1,0:T(8,128)S(1)}, f32[56,256]{1,0:T(8,128)S(1)}, u32[]{:S(2)}, u32[]{:S(2)}) %collective-permute-start.11) | collective-permute-done | bytes 57376 | tf_op jit(solution)/shard_map/ppermute | solution.py:585
  92.4 1.2 %solve2.1.coef_ref = f32[16,256]{1,0:T(8,128)S(1)} custom-call(s32[3,4]{1,0:T(4,128)S(1)} %copy-done.1, f32[56,256]{1,0:T(8,128)S(1)} %get-tuple-element.52.mine_ref, f32[56,256]{1,0:T(8,128)S(1)} %collective-permute-done.11.other_ref), custom_call_target="tpu_custom_call" | custom-call | flops 2000000000 | bytes 6000000 | tf_op jit(solution)/shard_map/solve2/pallas_call | solution.py:470
  93.6 2.5 %collective-permute-done.13.ra = f32[768,256]{1,0:T(8,128)S(1)} collective-permute-done((f32[768,256]{1,0:T(8,128)S(1)}, f32[768,256]{1,0:T(8,128)S(1)}, u32[]{:S(2)}, u32[]{:S(2)}) %collective-permute-start.13) | collective-permute-done | bytes 786464 | tf_op jit(solution)/shard_map/ppermute | solution.py:583
  96.1 3.6 %own.1.own_ref = f32[1536,256]{1,0:T(8,128)S(1)} custom-call(s32[3,4]{1,0:T(4,128)S(1)} %copy-done.1, s32[1]{0:T(128)} %bitcast.p_ref, f32[16,256]{1,0:T(8,128)S(1)} %solve2.1.coef_ref, f32[768,256]{1,0:T(8,128)S(1)} %get-tuple-element.50.za, f32[768,256]{1,0:T(8,128)S(1)} %get-tuple-element.58.zb, f32[1536,256]{1,0:T(8,128)S(1)} %get-tuple-element.54.q_ref), custom_call_target="tpu_custom_call" | custom-call | flops 40000000000 | bytes 120000000 | tf_op jit(solution)/shard_map/own/pallas_call | solution.py:497
  100.1 5.3 %collective-permute-done.12.coef_ref = f32[16,256]{1,0:T(8,128)S(1)} collective-permute-done((f32[16,256]{1,0:T(8,128)S(1)}, f32[16,256]{1,0:T(8,128)S(1)}, u32[]{:S(2)}, u32[]{:S(2)}) %collective-permute-start.12) | collective-permute-done | bytes 16416 | tf_op jit(solution)/shard_map/ppermute | solution.py:589
  105.4 5.0 %finish.1 = (f32[2,1536,256]{2,1,0:T(8,128)}, f32[3,2,256]{2,1,0:T(2,128)}) custom-call(s32[3,4]{1,0:T(4,128)S(1)} %copy-done.1, s32[1]{0:T(128)} %bitcast.p_ref, f32[16,256]{1,0:T(8,128)S(1)} %collective-permute-done.12.coef_ref, f32[16,256]{1,0:T(8,128)S(1)} %get-tuple-element.35.after_ref.a_ref, f32[16,256]{1,0:T(8,128)S(1)} %solve1.1.coef_ref.b_ref, ...), custom_call_target="tpu_custom_call" | custom-call | flops 5000000000 | bytes 15000000 | tf_op jit(solution)/shard_map/finish/pallas_call | solution.py:533
  (24 shorter events, 3.2 us)
Async XLA Ops:
  0.6 0.7 copy-start
  1.3 19.7 %copy-start.1 = (s32[3,4]{1,0:T(4,128)S(1)}, s32[3,4]{1,0:T(4,128)}, u32[]{:S(2)}) copy-start(s32[3,4]{1,0:T(4,128)} %o_ref.17) | copy-start | bytes 148
  11.6 9.4 %collective-permute-start = (f32[56,256]{1,0:T(8,128)S(1)}, f32[56,256]{1,0:T(8,128)S(1)}, u32[]{:S(2)}, u32[]{:S(2)}) collective-permute-start(f32[56,256]{1,0:T(8,128)S(1)} %get-tuple-element.31.mine_ref), channel_id=1, source_target_pairs={{0,1},{1,0},{2,3},{3,2},{4,5},{5,4},{6,7},{7,6},{8,9},{9,8},{10,11... | collective-permute-start | bytes 172040 | tf_op jit(solution)/shard_map/ppermute | solution.py:561
  25.2 18.1 %collective-permute-start.1 = (f32[768,256]{1,0:T(8,128)S(1)}, f32[768,256]{1,0:T(8,128)S(1)}, u32[]{:S(2)}, u32[]{:S(2)}) collective-permute-start(f32[768,256]{1,0:T(8,128)S(1)} %get-tuple-element.37), channel_id=1, source_target_pairs={{2,4},{6,8},{10,12},{14,16},{18,20},{22,24},{26,28},{30,32},{34,36... | collective-permute-start | bytes 2359304 | tf_op jit(solution)/shard_map/ppermute | solution.py:564
  31.2 12.1 %collective-permute-start.2 = (f32[768,256]{1,0:T(8,128)S(1)}, f32[768,256]{1,0:T(8,128)S(1)}, u32[]{:S(2)}, u32[]{:S(2)}) collective-permute-start(f32[768,256]{1,0:T(8,128)S(1)} %get-tuple-element.41), channel_id=1, source_target_pairs={{0,2},{2,0},{4,6},{6,4},{8,10},{10,8},{12,14},{14,12},{16,18},{18,... | collective-permute-start | bytes 2359304 | tf_op jit(solution)/shard_map/ppermute | solution.py:566
  31.3 20.4 %collective-permute-start.3 = (f32[768,256]{1,0:T(8,128)S(1)}, f32[768,256]{1,0:T(8,128)S(1)}, u32[]{:S(2)}, u32[]{:S(2)}) collective-permute-start(f32[768,256]{1,0:T(8,128)S(1)} %get-tuple-element.39), channel_id=1, source_target_pairs={{2,4},{6,8},{10,12},{14,16},{18,20},{22,24},{26,28},{30,32},{34,36... | collective-permute-start | bytes 2359304 | tf_op jit(solution)/shard_map/ppermute | solution.py:565
  35.6 16.1 %collective-permute-start.4 = (f32[768,256]{1,0:T(8,128)S(1)}, f32[768,256]{1,0:T(8,128)S(1)}, u32[]{:S(2)}, u32[]{:S(2)}) collective-permute-start(f32[768,256]{1,0:T(8,128)S(1)} %get-tuple-element.49), channel_id=1, source_target_pairs={{0,2},{2,0},{4,6},{6,4},{8,10},{10,8},{12,14},{14,12},{16,18},{18,... | collective-permute-start | bytes 2359304 | tf_op jit(solution)/shard_map/ppermute | solution.py:567
  35.8 37.8 %collective-permute-start.7 = (f32[768,256]{1,0:T(8,128)S(1)}, f32[768,256]{1,0:T(8,128)S(1)}, u32[]{:S(2)}, u32[]{:S(2)}) collective-permute-start(f32[768,256]{1,0:T(8,128)S(1)} %get-tuple-element.37), channel_id=1, source_target_pairs={{0,2},{2,0},{4,6},{6,4},{8,10},{10,8},{12,14},{14,12},{16,18},{18,... | collective-permute-start | bytes 2359304 | tf_op jit(solution)/shard_map/ppermute | solution.py:568
  43.3 30.3 %collective-permute-start.8 = (f32[768,256]{1,0:T(8,128)S(1)}, f32[768,256]{1,0:T(8,128)S(1)}, u32[]{:S(2)}, u32[]{:S(2)}) collective-permute-start(f32[768,256]{1,0:T(8,128)S(1)} %get-tuple-element.39), channel_id=1, source_target_pairs={{0,2},{2,0},{4,6},{6,4},{8,10},{10,8},{12,14},{14,12},{16,18},{18,... | collective-permute-start | bytes 2359304 | tf_op jit(solution)/shard_map/ppermute | solution.py:569
  44.7 28.8 %collective-permute-start.6 = (f32[768,256]{1,0:T(8,128)S(1)}, f32[768,256]{1,0:T(8,128)S(1)}, u32[]{:S(2)}, u32[]{:S(2)}) collective-permute-start(f32[768,256]{1,0:T(8,128)S(1)} %get-tuple-element.41), channel_id=1, source_target_pairs={{0,6},{4,10},{8,14},{12,18},{16,22},{20,26},{24,30},{28,34},{32,38... | collective-permute-start | bytes 2359304 | tf_op jit(solution)/shard_map/ppermute | solution.py:572
  54.5 9.3 %collective-permute-start.5 = (f32[56,256]{1,0:T(8,128)S(1)}, f32[56,256]{1,0:T(8,128)S(1)}, u32[]{:S(2)}, u32[]{:S(2)}) collective-permute-start(f32[56,256]{1,0:T(8,128)S(1)} %pairs1.1.after_ref.mine_ref), channel_id=1, source_target_pairs={{0,1},{1,0},{2,3},{3,2},{4,5},{5,4},{6,7},{7,6},{8,9},{9,8},{10,11... | collective-permute-start | bytes 172040 | tf_op jit(solution)/shard_map/ppermute | solution.py:574
  61.5 16.0 %collective-permute-start.10 = (f32[768,256]{1,0:T(8,128)S(1)}, f32[768,256]{1,0:T(8,128)S(1)}, u32[]{:S(2)}, u32[]{:S(2)}) collective-permute-start(f32[768,256]{1,0:T(8,128)S(1)} %get-tuple-element.49), channel_id=1, source_target_pairs={{0,6},{4,10},{8,14},{12,18},{16,22},{20,26},{24,30},{28,34},{32,38... | collective-permute-start | bytes 2359304 | tf_op jit(solution)/shard_map/ppermute | solution.py:577
  64.9 12.2 %collective-permute-start.9 = (f32[16,256]{1,0:T(8,128)S(1)}, f32[16,256]{1,0:T(8,128)S(1)}, u32[]{:S(2)}, u32[]{:S(2)}) collective-permute-start(f32[16,256]{1,0:T(8,128)S(1)} %solve1.1.coef_ref.b_ref), channel_id=1, source_target_pairs={{4,0},{8,4},{12,8},{16,12},{20,16},{24,20},{28,24},{32,28},{36,32}... | collective-permute-start | bytes 49160 | tf_op jit(solution)/shard_map/ppermute | solution.py:579
  77.1 19.0 %collective-permute-start.13 = (f32[768,256]{1,0:T(8,128)S(1)}, f32[768,256]{1,0:T(8,128)S(1)}, u32[]{:S(2)}, u32[]{:S(2)}) collective-permute-start(f32[768,256]{1,0:T(8,128)S(1)} %get-tuple-element.50.za), channel_id=1, source_target_pairs={{0,4},{4,8},{8,12},{12,16},{16,20},{20,24},{24,28},{28,32},{32,36}... | collective-permute-start | bytes 2359304 | tf_op jit(solution)/shard_map/ppermute | solution.py:583
  84.2 8.2 %collective-permute-start.11 = (f32[56,256]{1,0:T(8,128)S(1)}, f32[56,256]{1,0:T(8,128)S(1)}, u32[]{:S(2)}, u32[]{:S(2)}) collective-permute-start(f32[56,256]{1,0:T(8,128)S(1)} %get-tuple-element.52.mine_ref), channel_id=1, source_target_pairs={{0,1},{1,0},{2,3},{3,2},{4,5},{5,4},{6,7},{7,6},{8,9},{9,8},{10,11... | collective-permute-start | bytes 172040 | tf_op jit(solution)/shard_map/ppermute | solution.py:585
  84.3 21.0 %collective-permute-start.15 = (f32[768,256]{1,0:T(8,128)S(1)}, f32[768,256]{1,0:T(8,128)S(1)}, u32[]{:S(2)}, u32[]{:S(2)}) collective-permute-start(f32[768,256]{1,0:T(8,128)S(1)} %get-tuple-element.58.zb), channel_id=1, source_target_pairs={{0,4},{4,8},{8,12},{12,16},{16,20},{20,24},{24,28},{28,32},{32,36}... | collective-permute-start | bytes 2359304 | tf_op jit(solution)/shard_map/ppermute | solution.py:587
  93.6 11.8 %collective-permute-start.12 = (f32[16,256]{1,0:T(8,128)S(1)}, f32[16,256]{1,0:T(8,128)S(1)}, u32[]{:S(2)}, u32[]{:S(2)}) collective-permute-start(f32[16,256]{1,0:T(8,128)S(1)} %solve2.1.coef_ref), channel_id=1, source_target_pairs={{0,4},{4,8},{8,12},{12,16},{16,20},{20,24},{24,28},{28,32},{32,36}... | collective-permute-start | bytes 49160 | tf_op jit(solution)/shard_map/ppermute | solution.py:589
  99.7 5.6 %collective-permute-start.14 = (f32[16,256]{1,0:T(8,128)S(1)}, f32[16,256]{1,0:T(8,128)S(1)}, u32[]{:S(2)}, u32[]{:S(2)}) collective-permute-start(f32[16,256]{1,0:T(8,128)S(1)} %solve2.1.coef_ref), channel_id=1, source_target_pairs={{0,2},{2,0},{4,6},{6,4},{8,10},{10,8},{12,14},{14,12},{16,18},{18,... | collective-permute-start | bytes 49160 | tf_op jit(solution)/shard_map/ppermute | solution.py:593
